TPU v7x, 32 devices: a whole 2x2x4 slice. The times are simulated.
32 devices in a mesh: cut: 4 (over z), cross: 8 (over y, x, core).
Axes of the slice: x: 2, y: 2, z: 4, core: 2. Of those that a mesh axis runs over, the one named last changes fastest.
Arguments:
- warming_above_ambient: float32 [512, 128, 128], P('cut', 'cross'), may hold values from 0 to 2
- fourier_stability_factor: float32 [512, 128, 128], P('cut', 'cross'), may hold values from 0.02 to 0.1
- patch_locator: int32 [65536], P(('cut', 'cross')), may hold values from 0 to 524287
- photon_gain_wattage: float32 [65536], P(('cut', 'cross')), may hold values from 0.5 to 4
- on_skin_marker: int32 [65536], P(('cut', 'cross')), may hold values 0 or 1
- grain_placements: float32 [3, 65536], P(None, ('cut', 'cross')), may hold values from -1 to 1
- grain_motion_parts: float32 [3, 65536], P(None, ('cut', 'cross')), may hold values from -3 to 3
- tether_acted_grain: int32 [262144], P(('cut', 'cross')), may hold values from 0 to 2047
- tether_other_grain: int32 [262144], P(('cut', 'cross')), may hold values from 0 to 2559
- tether_relaxed_gap: float32 [262144], P(('cut', 'cross')), may hold values from 0.5 to 1.5
- snapped_marker: int32 [262144], P(('cut', 'cross')), may hold values 0 or 1
- exported_copies: int32 [8192], P(('cut', 'cross')), may hold values from 0 to 2047
Outputs:
- temperature_new: float32 [512, 128, 128], P('cut', 'cross')
- positions_new: float32 [3, 65536], P(None, ('cut', 'cross'))
- velocities_new: float32 [3, 65536], P(None, ('cut', 'cross'))
Inputs may be any that keep to these rules, and one draw needn't show every extreme that they name: `patch_locator`: values below 262144 name cells of the particle's own grid block along the cutting direction, the others cells of the next block.
All inputs are finite; a program needn't handle non-finite values. No bound on the sum of `on_skin_marker` or of `snapped_marker` on one device may be relied on, other than what follows from the above.
Results may differ from a plain program's by a relative error of at most 0.000071.
Values sent between devices are 32-bit elements; how exact they have to be, the bound alone decides.
No kernel may reach another device: no remote copies, remote signals or barrier semaphores. Data moves between devices by JAX's collectives and lax.ppermute only.
A program may use at most 64 MiB of HBM per device.

v0:
```python
import jax
import jax.numpy as jnp
from jax import lax
from jax.sharding import PartitionSpec as P

STEPS = 3


def shifted(block, axis, distance):
    devices = range(lax.axis_size(axis))
    route = [((i - distance) % len(devices), i) for i in devices]
    return lax.ppermute(block, axis, route)


def with_halo(cells, sides, width):
    for axis, dim in sides:
        count = lax.axis_size(axis)
        head = lax.slice_in_dim(cells, 0, width, axis=dim)
        tail = lax.slice_in_dim(cells, cells.shape[dim] - width, cells.shape[dim], axis=dim)
        cells = jnp.concatenate(
            [
                lax.ppermute(tail, axis, [(i, (i + 1) % count) for i in range(count)]),
                cells,
                lax.ppermute(head, axis, [((i + 1) % count, i) for i in range(count)]),
            ],
            axis=dim,
        )
    return cells


def conduct(grain_warmth_reading):
    return 0.5 + 1.0 / (1.0 + grain_warmth_reading * grain_warmth_reading)


def advance(temp_pad, kappa_pad, thermal_input):
    temp_full = jnp.pad(temp_pad, ((0, 0), (0, 0), (1, 1)))
    kappa_full = jnp.pad(kappa_pad, ((0, 0), (0, 0), (1, 1)))
    conduct_full = kappa_full * conduct(temp_full)
    size_a = temp_full.shape[0] - 2
    size_b = temp_full.shape[1] - 2
    size_c = temp_full.shape[2] - 2
    center = temp_full[1 : 1 + size_a, 1 : 1 + size_b, 1 : 1 + size_c]
    middle = conduct_full[1 : 1 + size_a, 1 : 1 + size_b, 1 : 1 + size_c]
    change = jnp.zeros_like(center)
    for first, second, third in ((2, 1, 1), (0, 1, 1), (1, 2, 1), (1, 0, 1), (1, 1, 2), (1, 1, 0)):
        beside = temp_full[first : first + size_a, second : second + size_b, third : third + size_c]
        beside_c = conduct_full[
            first : first + size_a, second : second + size_b, third : third + size_c
        ]
        change = change + 0.5 * (middle + beside_c) * (beside - center)
    return center + (change + thermal_input)


def clear_rim(field, axis_dim, width):
    extent = field.shape[axis_dim]
    place = lax.broadcasted_iota(jnp.int32, field.shape, axis_dim)
    position = lax.axis_index("cross")
    final = lax.axis_size("cross") - 1
    drop = (place < width) & (position == 0) | (place >= extent - width) & (position == final)
    return jnp.where(drop, jnp.zeros_like(field), field)


def table_rows(table):
    channels = table.shape[0]
    columns = table.shape[1]
    padded_cols = -(-columns // 128) * 128
    high_count = padded_cols // 128
    return (
        table.reshape(channels, high_count, 128)
        .transpose(1, 0, 2)
        .reshape(high_count, channels * 128)
    )


def pick_columns(table, where_from):
    channels = table.shape[0]
    stacked_rows = table_rows(table)
    high_count = stacked_rows.shape[0]
    total_rows = where_from.shape[0]
    block_rows = min(1024, total_rows)

    def pick_block(idx_block):
        high_part = idx_block // 128
        low_part = idx_block % 128
        row_hot = (
            high_part[:, None] == lax.broadcasted_iota(jnp.int32, (1, high_count), 1)
        ).astype(jnp.float32)
        picked = jnp.dot(
            row_hot,
            stacked_rows,
            precision=lax.Precision.HIGHEST,
            preferred_element_type=jnp.float32,
        )
        picked = picked.reshape(idx_block.shape[0], channels, 128)
        lane_hot = (low_part[:, None] == lax.broadcasted_iota(jnp.int32, (1, 128), 1)).astype(
            jnp.float32
        )
        return jnp.sum(picked * lane_hot[:, None, :], axis=2)

    result = lax.map(pick_block, where_from.reshape(total_rows // block_rows, block_rows))
    return result.reshape(total_rows, channels).T


def add_columns(values, where_to, columns):
    channels = values.shape[0]
    total_rows = where_to.shape[0]
    block_rows = min(1024, total_rows)
    padded_cols = -(-columns // 128) * 128
    high_count = padded_cols // 128
    value_blocks = values.T.reshape(total_rows // block_rows, block_rows, channels)
    index_blocks = where_to.reshape(total_rows // block_rows, block_rows)

    def add_block(carried, pieces):
        value_block, idx_block = pieces
        high_part = idx_block // 128
        low_part = idx_block % 128
        row_hot = (
            high_part[:, None] == lax.broadcasted_iota(jnp.int32, (1, high_count), 1)
        ).astype(jnp.float32)
        lane_hot = (low_part[:, None] == lax.broadcasted_iota(jnp.int32, (1, 128), 1)).astype(
            jnp.float32
        )
        spread = (value_block[:, :, None] * lane_hot[:, None, :]).reshape(
            idx_block.shape[0], channels * 128
        )
        summed = lax.dot_general(
            row_hot,
            spread,
            (((0,), (0,)), ((), ())),
            precision=lax.Precision.HIGHEST,
            preferred_element_type=jnp.float32,
        )
        return (carried + summed, None)

    start_total = jnp.zeros((high_count, channels * 128), jnp.float32)
    totals, unused = lax.scan(add_block, start_total, (value_blocks, index_blocks))
    return (
        totals.reshape(high_count, channels, 128).transpose(1, 0, 2).reshape(channels, padded_cols)
    )


def per_device(
    warming_above_ambient,
    fourier_stability_factor,
    patch_locator,
    photon_gain_wattage,
    on_skin_marker,
    grain_placements,
    grain_motion_parts,
    tether_acted_grain,
    tether_other_grain,
    tether_relaxed_gap,
    snapped_marker,
    exported_copies,
):
    groups = lax.axis_size("cross")
    count = patch_locator.shape[0]
    capacity = count // groups
    structured_patch = (
        warming_above_ambient.shape[0]
        * warming_above_ambient.shape[1]
        * warming_above_ambient.shape[2]
    )
    energy_current = on_skin_marker.astype(jnp.float32) * photon_gain_wattage * 0.5
    got_cells, got_flux = (
        lax.all_to_all(
            patch_locator.reshape(groups, capacity),
            "cross",
            split_axis=0,
            concat_axis=0,
            tiled=True,
        ),
        lax.all_to_all(
            energy_current.reshape(groups, capacity),
            "cross",
            split_axis=0,
            concat_axis=0,
            tiled=True,
        ),
    )
    got_cells = got_cells.reshape(-1)
    got_flux = got_flux.reshape(-1)
    upper = got_cells >= structured_patch
    local_part = add_columns(
        got_flux[None, :], jnp.where(upper, structured_patch, got_cells), structured_patch
    )[0]
    moved_cells, moved_flux = shifted((got_cells, got_flux), "cut", 1)
    moved_upper = moved_cells >= structured_patch
    target = jnp.where(moved_upper, moved_cells - structured_patch, structured_patch)
    thermal_input = (
        local_part + add_columns(moved_flux[None, :], target, structured_patch)[0]
    ).reshape(warming_above_ambient.shape)
    grain_warmth_reading = warming_above_ambient
    kappa_pad = clear_rim(with_halo(fourier_stability_factor, (("cut", 0), ("cross", 1)), 1), 1, 1)
    for substep in range(STEPS):
        temp_pad = clear_rim(with_halo(grain_warmth_reading, (("cut", 0), ("cross", 1)), 1), 1, 1)
        grain_warmth_reading = advance(temp_pad, kappa_pad, thermal_input)
    temp_flat = grain_warmth_reading.reshape(1, -1)
    mine = pick_columns(temp_flat, jnp.where(upper, 0, got_cells))[0]
    theirs = pick_columns(temp_flat, jnp.where(moved_upper, moved_cells - structured_patch, 0))[0]
    returned = shifted(theirs, "cut", -1)
    looked = jnp.where(upper, returned, mine)
    particle_temp = lax.all_to_all(
        looked.reshape(groups, capacity), "cross", split_axis=0, concat_axis=0, tiled=True
    ).reshape(-1)
    state = jnp.concatenate([grain_placements, particle_temp[None, :]], axis=0)
    ghost_count = exported_copies.shape[0]
    ghost_data = pick_columns(state, exported_copies)
    ghost_wide = with_halo(ghost_data, (("cut", 1),), ghost_count)
    extended = jnp.concatenate(
        [state, ghost_wide[:, :ghost_count], ghost_wide[:, 2 * ghost_count :]], axis=1
    )
    first_state = pick_columns(state, tether_acted_grain)
    second_state = pick_columns(extended, tether_other_grain)
    delta = second_state[:3] - first_state[:3]
    dist = jnp.sqrt(jnp.sum(delta * delta, axis=0))
    hot = tether_relaxed_gap * (1.0 + 0.2 * (0.5 * (first_state[3] + second_state[3])))
    scale = (1.0 - snapped_marker.astype(jnp.float32)) * (dist - hot) / jnp.maximum(dist, 0.3)
    force = add_columns(scale * delta, tether_acted_grain, count)
    velocities_new = grain_motion_parts + 0.5 * force
    positions_new = grain_placements + 0.5 * velocities_new
    return (grain_warmth_reading, positions_new, velocities_new)


def solution(mesh):
    return jax.shard_map(
        per_device,
        mesh=mesh,
        in_specs=(
            P("cut", "cross", None),
            P("cut", "cross", None),
            P(("cut", "cross")),
            P(("cut", "cross")),
            P(("cut", "cross")),
            P(None, ("cut", "cross")),
            P(None, ("cut", "cross")),
            P(("cut", "cross")),
            P(("cut", "cross")),
            P(("cut", "cross")),
            P(("cut", "cross")),
            P(("cut", "cross")),
        ),
        out_specs=(P("cut", "cross", None), P(None, ("cut", "cross")), P(None, ("cut", "cross"))),
        check_vma=False,
    )
```

profile of v0, /device:TPU:0, one launch (start us, length us, event | category | flops | bytes accessed | tf_op | source)
XLA Modules:
  0.0 182.5 jit_solution(7815662485912924524)
XLA Ops:
  0.6 5.2 %all-to-all-start = ((s32[8,1,256]{2,1,0:T(1,128)}), s32[8,1,256]{2,1,0:T(1,128)S(1)}, u32[]{:S(2)}, u32[]{:S(2)}) async-start(s32[8,1,256]{2,1,0:T(1,128)} %bitcast.163), calls=%async_computation | async-start | bytes 16384 | tf_op jit(solution)/shard_map/all_to_all | solution.py:166
  6.5 1.6 collective-permute-start.4
  8.1 2.2 %collective-permute-start.5 = (f32[1,16,128]{2,1,0:T(8,128)S(1)}, f32[1,16,128]{2,1,0:T(8,128)S(1)}, u32[]{:S(2)}, u32[]{:S(2)}) collective-permute-start(f32[1,16,128]{2,1,0:T(8,128)S(1)} %get-tuple-element.566), channel_id=1, source_target_pairs={{8,0},{16,8},{24,16},{0,24},{9,1},{17,9},{25,17},{1,25},{10,2},{18... | collective-permute-start | bytes 24584 | tf_op jit(solution)/shard_map/ppermute | solution.py:24
  11.1 3.8 %collective-permute-start.1 = (f32[1,16,128]{2,1,0:T(8,128)S(1)}, f32[1,16,128]{2,1,0:T(8,128)S(1)}, u32[]{:S(2)}, u32[]{:S(2)}) collective-permute-start(f32[1,16,128]{2,1,0:T(8,128)S(1)} %get-tuple-element.568), channel_id=1, source_target_pairs={{8,0},{16,8},{24,16},{0,24},{9,1},{17,9},{25,17},{1,25},{10,2},{18... | collective-permute-start | bytes 24584 | tf_op jit(solution)/shard_map/ppermute | solution.py:24
  14.9 1.3 multiply_multiply_fusion
  16.2 4.2 %all-to-all-start.1 = ((f32[8,1,256]{2,1,0:T(1,128)}), f32[8,1,256]{2,1,0:T(1,128)S(1)}, u32[]{:S(2)}, u32[]{:S(2)}) async-start(f32[8,1,256]{2,1,0:T(1,128)} %bitcast.11), calls=%async_computation.1 | async-start | bytes 16384 | tf_op jit(solution)/shard_map/all_to_all | solution.py:173
  20.5 4.6 %all-to-all-done.1 = f32[8,1,256]{2,1,0:T(1,128)S(1)} async-done(((f32[8,1,256]{2,1,0:T(1,128)}), f32[8,1,256]{2,1,0:T(1,128)S(1)}, u32[]{:S(2)}, u32[]{:S(2)}) %all-to-all-start.1) | async-done | bytes 8224 | tf_op jit(solution)/shard_map/all_to_all | solution.py:173
  25.2 15.1 %while.95 = (s32[]{:T(128)}, f32[2048,128]{1,0:T(8,128)S(1)}, s32[2,1024]{1,0:T(2,128)S(1)}, f32[2,1024,1]{1,2,0:T(1,128)S(1)}, s32[]{:T(128)}, /*index=5*/s32[]{:T(128)}) while((s32[]{:T(128)}, f32[2048,128]{1,0:T(8,128)S(1)}, s32[2,1024]{1,0:T(2,128)S(1)}, f32[2,1024,1]{1,2,0:T(1,128)S(1)}, s32[]{:T(128)}, ...), condition=%wide.region_1.2_spmd.clone, body=%wide.region_0.1_spmd.clone.sunk | while | flops 3224128512 | bytes 2138207 | solution.py:136
  25.2 7.5 %fusion.165 = f32[2048,128]{1,0:T(8,128)S(1)} fusion(s32[1024]{0:T(1024)S(1)} %get-tuple-element.769, f32[2048,128]{1,0:T(8,128)S(1)} %get-tuple-element.790, pred[]{:T(512)S(6)} %compare.100, f32[1024]{0:T(1024)S(1)} %bitcast.151, s32[1024]{0:T(1024)S(1)} %get-tuple-element.770), kind=kOutput, calls=%fused_computation.67.clone.1 | convolution fusion | flops 3224109056 | bytes 2109441 | tf_op jit(solution)/shard_map/while/body/eval_jaxpr/dot_general | solution.py:126
  32.7 7.5 %fusion.165 = f32[2048,128]{1,0:T(8,128)S(1)} fusion(s32[1024]{0:T(1024)S(1)} %get-tuple-element.769, f32[2048,128]{1,0:T(8,128)S(1)} %get-tuple-element.790, pred[]{:T(512)S(6)} %compare.100, f32[1024]{0:T(1024)S(1)} %bitcast.151, s32[1024]{0:T(1024)S(1)} %get-tuple-element.770), kind=kOutput, calls=%fused_computation.67.clone.1 | convolution fusion | flops 3224109056 | bytes 2109441 | tf_op jit(solution)/shard_map/while/body/eval_jaxpr/dot_general | solution.py:126
  41.8 2.2 %collective-permute-start.3 = (f32[130,1,128]{2,0,1:T(8,128)S(1)}, f32[130,1,128]{2,0,1:T(8,128)}, u32[]{:S(2)}, u32[]{:S(2)}) collective-permute-start(f32[130,1,128]{2,0,1:T(8,128)S(1)} %copy.42), channel_id=1, source_target_pairs={{1,0},{2,1},{3,2},{4,3},{5,4},{6,5},{7,6},{0,7},{9,8},{10,9},{11,1... | collective-permute-start | bytes 199688 | tf_op jit(solution)/shard_map/ppermute | solution.py:24
  46.0 15.1 %while.96 = (s32[]{:T(128)}, f32[2048,128]{1,0:T(8,128)S(1)}, s32[2,1024]{1,0:T(2,128)S(1)}, f32[2,1024,1]{1,2,0:T(1,128)S(1)}, s32[]{:T(128)}, /*index=5*/s32[]{:T(128)}) while((s32[]{:T(128)}, f32[2048,128]{1,0:T(8,128)S(1)}, s32[2,1024]{1,0:T(2,128)S(1)}, f32[2,1024,1]{1,2,0:T(1,128)S(1)}, s32[]{:T(128)}, ...), condition=%wide.region_3.4_spmd.clone, body=%wide.region_2.3_spmd.clone.sunk | while | flops 3224128512 | bytes 2138207 | solution.py:136
  46.1 7.5 %fusion.167 = f32[2048,128]{1,0:T(8,128)S(1)} fusion(s32[1024]{0:T(1024)S(1)} %get-tuple-element.775, f32[2048,128]{1,0:T(8,128)S(1)} %get-tuple-element.808, pred[]{:T(512)S(6)} %compare.101, f32[1024]{0:T(1024)S(1)} %bitcast.152, s32[1024]{0:T(1024)S(1)} %get-tuple-element.776), kind=kOutput, calls=%fused_computation.87.clone.1 | convolution fusion | flops 3224109056 | bytes 2109441 | tf_op jit(solution)/shard_map/while/body/eval_jaxpr/dot_general | solution.py:126
  53.6 7.5 %fusion.167 = f32[2048,128]{1,0:T(8,128)S(1)} fusion(s32[1024]{0:T(1024)S(1)} %get-tuple-element.775, f32[2048,128]{1,0:T(8,128)S(1)} %get-tuple-element.808, pred[]{:T(512)S(6)} %compare.101, f32[1024]{0:T(1024)S(1)} %bitcast.152, s32[1024]{0:T(1024)S(1)} %get-tuple-element.776), kind=kOutput, calls=%fused_computation.87.clone.1 | convolution fusion | flops 3224109056 | bytes 2109441 | tf_op jit(solution)/shard_map/while/body/eval_jaxpr/dot_general | solution.py:126
  64.2 1.7 pad_multiply_fusion.5
  65.9 2.9 %fusion.63 = f32[128,16,128]{2,1,0:T(8,128)S(1)} fusion(f32[128,16,128]{2,1,0:T(8,128)S(1)} %bitcast.124, f32[130,18,128]{2,1,0:T(8,128)S(1)} %get-tuple-element.579, f32[130,18,130]{2,1,0:T(8,128)S(1)} %pad_multiply_fusion.5), kind=kLoop, calls=%fused_computation.153 | loop fusion | flops 8126464 | bytes 16277504 | tf_op jit(solution)/shard_map/add | solution.py:51
  68.8 14.0 %collective-permute-start.11 = (f32[1,16,128]{2,1,0:T(8,128)S(1)}, f32[1,16,128]{2,1,0:T(8,128)S(1)}, u32[]{:S(2)}, u32[]{:S(2)}) collective-permute-start(f32[1,16,128]{2,1,0:T(8,128)S(1)} %get-tuple-element.565), channel_id=1, source_target_pairs={{8,0},{16,8},{24,16},{0,24},{9,1},{17,9},{25,17},{1,25},{10,2},{18... | collective-permute-start | bytes 24584 | tf_op jit(solution)/shard_map/ppermute | solution.py:24
  82.8 1.4 collective-permute-done.11
  84.2 4.1 %collective-permute-done.10 = f32[1,16,128]{2,1,0:T(8,128)S(1)} collective-permute-done((f32[1,16,128]{2,1,0:T(8,128)S(1)}, f32[1,16,128]{2,1,0:T(8,128)S(1)}, u32[]{:S(2)}, u32[]{:S(2)}) %collective-permute-start.10) | collective-permute-done | bytes 8224 | tf_op jit(solution)/shard_map/ppermute | solution.py:22
  89.6 1.9 %collective-permute-done.13 = f32[130,1,128]{2,0,1:T(8,128)S(1)} collective-permute-done((f32[130,1,128]{2,0,1:T(8,128)S(1)}, f32[130,1,128]{2,0,1:T(8,128)S(1)}, u32[]{:S(2)}, u32[]{:S(2)}) %collective-permute-start.13) | collective-permute-done | bytes 66592 | tf_op jit(solution)/shard_map/ppermute | solution.py:24
  91.6 2.6 %collective-permute-done.12 = f32[130,1,128]{2,0,1:T(8,128)S(1)} collective-permute-done((f32[130,1,128]{2,0,1:T(8,128)S(1)}, f32[130,1,128]{2,0,1:T(8,128)S(1)}, u32[]{:S(2)}, u32[]{:S(2)}) %collective-permute-start.12) | collective-permute-done | bytes 66592 | tf_op jit(solution)/shard_map/ppermute | solution.py:22
  94.6 1.7 pad_multiply_fusion.4
  96.4 2.9 %fusion.71 = f32[128,16,128]{2,1,0:T(8,128)S(1)} fusion(f32[128,16,128]{2,1,0:T(8,128)S(1)} %bitcast.125, f32[130,18,128]{2,1,0:T(8,128)S(1)} %maximum_select_fusion.2, f32[130,18,130]{2,1,0:T(8,128)S(1)} %pad_multiply_fusion.4), kind=kLoop, calls=%fused_computation.161 | loop fusion | flops 8126464 | bytes 16277504 | tf_op jit(solution)/shard_map/add | solution.py:51
  99.6 1.7 collective-permute-start.14
  101.4 1.6 collective-permute-done.15
  103.0 2.1 %collective-permute-done.14 = f32[1,16,128]{2,1,0:T(8,128)S(1)} collective-permute-done((f32[1,16,128]{2,1,0:T(8,128)S(1)}, f32[1,16,128]{2,1,0:T(8,128)S(1)}, u32[]{:S(2)}, u32[]{:S(2)}) %collective-permute-start.14) | collective-permute-done | bytes 8224 | tf_op jit(solution)/shard_map/ppermute | solution.py:22
  105.8 1.9 %collective-permute-done.17 = f32[130,1,128]{2,0,1:T(8,128)S(1)} collective-permute-done((f32[130,1,128]{2,0,1:T(8,128)S(1)}, f32[130,1,128]{2,0,1:T(8,128)S(1)}, u32[]{:S(2)}, u32[]{:S(2)}) %collective-permute-start.17) | collective-permute-done | bytes 66592 | tf_op jit(solution)/shard_map/ppermute | solution.py:24
  107.7 2.2 %collective-permute-done.16 = f32[130,1,128]{2,0,1:T(8,128)S(1)} collective-permute-done((f32[130,1,128]{2,0,1:T(8,128)S(1)}, f32[130,1,128]{2,0,1:T(8,128)S(1)}, u32[]{:S(2)}, u32[]{:S(2)}) %collective-permute-start.16) | collective-permute-done | bytes 66592 | tf_op jit(solution)/shard_map/ppermute | solution.py:22
  110.0 1.5 maximum_select_fusion.3
  111.6 1.7 pad_multiply_fusion.3
  113.3 2.9 %fusion.79 = f32[128,16,128]{2,1,0:T(8,128)S(1)} fusion(f32[128,16,128]{2,1,0:T(8,128)S(1)} %bitcast.126, f32[130,18,128]{2,1,0:T(8,128)S(1)} %maximum_select_fusion.3, f32[130,18,130]{2,1,0:T(8,128)S(1)} %pad_multiply_fusion.3), kind=kLoop, calls=%fused_computation.169 | loop fusion | flops 8126464 | bytes 16277504 | tf_op jit(solution)/shard_map/add | solution.py:51
  116.2 10.0 %while.91 = (s32[]{:T(128)}, f32[2,1024,1]{1,2,0:T(1,128)S(1)}, s32[2,1024]{1,0:T(2,128)S(1)}, f32[2048,128]{1,0:T(8,128)S(1)}, s32[]{:T(128)}) while((s32[]{:T(128)}, f32[2,1024,1]{1,2,0:T(1,128)S(1)}, s32[2,1024]{1,0:T(2,128)S(1)}, f32[2048,128]{1,0:T(8,128)S(1)}, s32[]{:T(128)}) %tuple.235), condition=%wide.region_6.7_spmd, body=%wide.region_4.6_spmd.sunk | while | flops 3223734272 | bytes 1089613 | solution.py:100
  116.3 4.9 %fusion.157 = f32[1024]{0:T(1024)S(1)} fusion(f32[2048,128]{1,0:T(8,128)S(1)} %get-tuple-element.832, s32[1024]{0:T(1024)S(1)} %get-tuple-element.745, s32[1024]{0:T(1024)S(1)} %get-tuple-element.746), kind=kOutput, calls=%fused_computation.4.clone.1 | convolution fusion | flops 3223714816 | bytes 1060864 | tf_op jit(solution)/shard_map/while/body/eval_jaxpr/dot_general | solution.py:88
  121.3 4.9 %fusion.157 = f32[1024]{0:T(1024)S(1)} fusion(f32[2048,128]{1,0:T(8,128)S(1)} %get-tuple-element.832, s32[1024]{0:T(1024)S(1)} %get-tuple-element.745, s32[1024]{0:T(1024)S(1)} %get-tuple-element.746), kind=kOutput, calls=%fused_computation.4.clone.1 | convolution fusion | flops 3223714816 | bytes 1060864 | tf_op jit(solution)/shard_map/while/body/eval_jaxpr/dot_general | solution.py:88
  126.3 10.0 %while.92 = (s32[]{:T(128)}, f32[2,1024,1]{1,2,0:T(1,128)S(1)}, s32[2,1024]{1,0:T(2,128)S(1)}, f32[2048,128]{1,0:T(8,128)S(1)}, s32[]{:T(128)}) while((s32[]{:T(128)}, f32[2,1024,1]{1,2,0:T(1,128)S(1)}, s32[2,1024]{1,0:T(2,128)S(1)}, f32[2048,128]{1,0:T(8,128)S(1)}, s32[]{:T(128)}) %tuple.236), condition=%wide.region_9.10_spmd, body=%wide.region_7.9_spmd.sunk | while | flops 3223734272 | bytes 1089613 | solution.py:100
  126.4 4.9 %fusion.159 = f32[1024]{0:T(1024)S(1)} fusion(f32[2048,128]{1,0:T(8,128)S(1)} %get-tuple-element.847, s32[1024]{0:T(1024)S(1)} %get-tuple-element.751, s32[1024]{0:T(1024)S(1)} %get-tuple-element.752), kind=kOutput, calls=%fused_computation.20.clone.1 | convolution fusion | flops 3223714816 | bytes 1060864 | tf_op jit(solution)/shard_map/while/body/eval_jaxpr/dot_general | solution.py:88
  131.3 4.9 %fusion.159 = f32[1024]{0:T(1024)S(1)} fusion(f32[2048,128]{1,0:T(8,128)S(1)} %get-tuple-element.847, s32[1024]{0:T(1024)S(1)} %get-tuple-element.751, s32[1024]{0:T(1024)S(1)} %get-tuple-element.752), kind=kOutput, calls=%fused_computation.20.clone.1 | convolution fusion | flops 3223714816 | bytes 1060864 | tf_op jit(solution)/shard_map/while/body/eval_jaxpr/dot_general | solution.py:88
  137.0 3.5 %all-to-all-start.2 = ((f32[8,1,256]{2,1,0:T(1,128)}), f32[8,1,256]{2,1,0:T(1,128)S(1)}, u32[]{:S(2)}, u32[]{:S(2)}) async-start(f32[8,1,256]{2,1,0:T(1,128)} %bitcast.20), calls=%async_computation.2 | async-start | bytes 16384 | tf_op jit(solution)/shard_map/all_to_all | solution.py:203
  140.6 4.5 %all-to-all-done.2 = f32[8,1,256]{2,1,0:T(1,128)S(1)} async-done(((f32[8,1,256]{2,1,0:T(1,128)}), f32[8,1,256]{2,1,0:T(1,128)S(1)}, u32[]{:S(2)}, u32[]{:S(2)}) %all-to-all-start.2) | async-done | bytes 8224 | tf_op jit(solution)/shard_map/all_to_all | solution.py:203
  147.8 10.8 %while.94 = (s32[]{:T(128)}, f32[8,1024,4]{1,2,0:T(4,128)S(1)}, s32[8,1024]{1,0:T(8,128)S(1)}, f32[16,512]{1,0:T(8,128)S(1)}, s32[]{:T(128)}) while((s32[]{:T(128)}, f32[8,1024,4]{1,2,0:T(4,128)S(1)}, s32[8,1024]{1,0:T(8,128)S(1)}, f32[16,512]{1,0:T(8,128)S(1)}, s32[]{:T(128)}) %tuple.234), condition=%wide.region_16.17_spmd, body=%wide.region_14.16_spmd.sunk | while | flops 102005760 | bytes 1159245 | solution.py:100
  158.7 11.2 %while.93 = (s32[]{:T(128)}, f32[8,1024,4]{1,2,0:T(4,128)S(1)}, s32[8,1024]{1,0:T(8,128)S(1)}, f32[20,512]{1,0:T(8,128)S(1)}, s32[]{:T(128)}) while((s32[]{:T(128)}, f32[8,1024,4]{1,2,0:T(4,128)S(1)}, s32[8,1024]{1,0:T(8,128)S(1)}, f32[20,512]{1,0:T(8,128)S(1)}, s32[]{:T(128)}) %tuple.233), condition=%wide.region_13.14_spmd, body=%wide.region_11.13_spmd.sunk | while | flops 127175680 | bytes 1167437 | solution.py:100
  158.8 1.3 multiply_reduce_fusion.5
  161.6 1.3 multiply_reduce_fusion.5
  163.0 1.3 multiply_reduce_fusion.5
  164.4 1.3 multiply_reduce_fusion.5
  165.8 1.3 multiply_reduce_fusion.5
  167.2 1.3 multiply_reduce_fusion.5
  170.2 11.3 %while.97 = (s32[]{:T(128)}, f32[16,384]{1,0:T(8,128)S(1)}, s32[8,1024]{1,0:T(8,128)S(1)}, f32[8,1024,3]{1,2,0:T(4,128)S(1)}, s32[]{:T(128)}, /*index=5*/s32[]{:T(128)}) while((s32[]{:T(128)}, f32[16,384]{1,0:T(8,128)S(1)}, s32[8,1024]{1,0:T(8,128)S(1)}, f32[8,1024,3]{1,2,0:T(4,128)S(1)}, s32[]{:T(128)}, ...), condition=%wide.region_19.20_spmd.clone, body=%wide.region_18.19_spmd.clone.sunk | while | flops 76217344 | bytes 4309087 | solution.py:136
  (272 shorter events, 40.1 us)
Async XLA Ops:
  0.6 15.6 %all-to-all-start = ((s32[8,1,256]{2,1,0:T(1,128)}), s32[8,1,256]{2,1,0:T(1,128)S(1)}, u32[]{:S(2)}, u32[]{:S(2)}) async-start(s32[8,1,256]{2,1,0:T(1,128)} %bitcast.163), calls=%async_computation | async-start | bytes 16384 | tf_op jit(solution)/shard_map/all_to_all | solution.py:166
  6.5 33.8 %collective-permute-start.4 = (f32[1,16,128]{2,1,0:T(8,128)S(1)}, f32[1,16,128]{2,1,0:T(8,128)S(1)}, u32[]{:S(2)}, u32[]{:S(2)}) collective-permute-start(f32[1,16,128]{2,1,0:T(8,128)S(1)} %get-tuple-element.567), channel_id=1, source_target_pairs={{0,8},{8,16},{16,24},{24,0},{1,9},{9,17},{17,25},{25,1},{2,10},{10... | collective-permute-start | bytes 24584 | tf_op jit(solution)/shard_map/ppermute | solution.py:22
  8.1 32.4 %collective-permute-start.5 = (f32[1,16,128]{2,1,0:T(8,128)S(1)}, f32[1,16,128]{2,1,0:T(8,128)S(1)}, u32[]{:S(2)}, u32[]{:S(2)}) collective-permute-start(f32[1,16,128]{2,1,0:T(8,128)S(1)} %get-tuple-element.566), channel_id=1, source_target_pairs={{8,0},{16,8},{24,16},{0,24},{9,1},{17,9},{25,17},{1,25},{10,2},{18... | collective-permute-start | bytes 24584 | tf_op jit(solution)/shard_map/ppermute | solution.py:24
  11.1 29.9 %collective-permute-start = (f32[1,16,128]{2,1,0:T(8,128)S(1)}, f32[1,16,128]{2,1,0:T(8,128)S(1)}, u32[]{:S(2)}, u32[]{:S(2)}) collective-permute-start(f32[1,16,128]{2,1,0:T(8,128)S(1)} %get-tuple-element.569), channel_id=1, source_target_pairs={{0,8},{8,16},{16,24},{24,0},{1,9},{9,17},{17,25},{25,1},{2,10},{10... | collective-permute-start | bytes 24584 | tf_op jit(solution)/shard_map/ppermute | solution.py:22
  11.1 30.5 %collective-permute-start.1 = (f32[1,16,128]{2,1,0:T(8,128)S(1)}, f32[1,16,128]{2,1,0:T(8,128)S(1)}, u32[]{:S(2)}, u32[]{:S(2)}) collective-permute-start(f32[1,16,128]{2,1,0:T(8,128)S(1)} %get-tuple-element.568), channel_id=1, source_target_pairs={{8,0},{16,8},{24,16},{0,24},{9,1},{17,9},{25,17},{1,25},{10,2},{18... | collective-permute-start | bytes 24584 | tf_op jit(solution)/shard_map/ppermute | solution.py:24
  16.2 8.9 %all-to-all-start.1 = ((f32[8,1,256]{2,1,0:T(1,128)}), f32[8,1,256]{2,1,0:T(1,128)S(1)}, u32[]{:S(2)}, u32[]{:S(2)}) async-start(f32[8,1,256]{2,1,0:T(1,128)} %bitcast.11), calls=%async_computation.1 | async-start | bytes 16384 | tf_op jit(solution)/shard_map/all_to_all | solution.py:173
  25.1 15.2 %copy-start.5 = (f32[128,16,128]{2,1,0:T(8,128)S(1)}, f32[128,16,128]{2,1,0:T(8,128)}, u32[]{:S(2)}) copy-start(f32[128,16,128]{2,1,0:T(8,128)} %param.27) | copy-start | bytes 3145732
  40.2 1.3 copy-start.6
  40.2 5.5 %collective-permute-start.8 = (s32[2048]{0:T(1024)S(1)}, s32[2048]{0:T(1024)S(1)}, u32[]{:S(2)}, u32[]{:S(2)}) collective-permute-start(s32[2048]{0:T(1024)S(1)} %bitcast.157), channel_id=1, source_target_pairs={{24,0},{0,8},{8,16},{16,24},{25,1},{1,9},{9,17},{17,25},{26,2},{2,... | collective-permute-start | bytes 24584 | tf_op jit(solution)/shard_map/ppermute | solution.py:12
  40.3 5.7 %collective-permute-start.9 = (f32[2048]{0:T(1024)S(1)}, f32[2048]{0:T(1024)S(1)}, u32[]{:S(2)}, u32[]{:S(2)}) collective-permute-start(f32[2048]{0:T(1024)S(1)} %bitcast.156), channel_id=1, source_target_pairs={{24,0},{0,8},{8,16},{16,24},{25,1},{1,9},{9,17},{17,25},{26,2},{2,... | collective-permute-start | bytes 24584 | tf_op jit(solution)/shard_map/ppermute | solution.py:12
  40.5 4.1 %copy-start.1 = (f32[130,16,128]{2,1,0:T(8,128)}, f32[130,16,128]{2,1,0:T(8,128)S(1)}, u32[]{:S(2)}) copy-start(f32[130,16,128]{2,1,0:T(8,128)S(1)} %constant_dynamic-update-slice_fusion.5) | copy-start | bytes 3194884
  40.6 20.6 %collective-permute-start.7 = (f32[130,1,128]{2,0,1:T(8,128)S(1)}, f32[130,1,128]{2,0,1:T(8,128)S(1)}, u32[]{:S(2)}, u32[]{:S(2)}) collective-permute-start(f32[130,1,128]{2,0,1:T(8,128)S(1)} %copy.46), channel_id=1, source_target_pairs={{1,0},{2,1},{3,2},{4,3},{5,4},{6,5},{7,6},{0,7},{9,8},{10,9},{11,1... | collective-permute-start | bytes 199688 | tf_op jit(solution)/shard_map/ppermute | solution.py:24
  41.0 20.4 %collective-permute-start.6 = (f32[130,1,128]{2,0,1:T(8,128)S(1)}, f32[130,1,128]{2,0,1:T(8,128)S(1)}, u32[]{:S(2)}, u32[]{:S(2)}) collective-permute-start(f32[130,1,128]{2,0,1:T(8,128)S(1)} %copy.45), channel_id=1, source_target_pairs={{0,1},{1,2},{2,3},{3,4},{4,5},{5,6},{6,7},{7,0},{8,9},{9,10},{10,1... | collective-permute-start | bytes 199688 | tf_op jit(solution)/shard_map/ppermute | solution.py:22
  41.6 4.1 %copy-start.3 = (f32[130,16,128]{2,1,0:T(8,128)}, f32[130,16,128]{2,1,0:T(8,128)S(1)}, u32[]{:S(2)}) copy-start(f32[130,16,128]{2,1,0:T(8,128)S(1)} %constant_dynamic-update-slice_fusion.2) | copy-start | bytes 3194884
  41.8 19.7 %collective-permute-start.3 = (f32[130,1,128]{2,0,1:T(8,128)S(1)}, f32[130,1,128]{2,0,1:T(8,128)}, u32[]{:S(2)}, u32[]{:S(2)}) collective-permute-start(f32[130,1,128]{2,0,1:T(8,128)S(1)} %copy.42), channel_id=1, source_target_pairs={{1,0},{2,1},{3,2},{4,3},{5,4},{6,5},{7,6},{0,7},{9,8},{10,9},{11,1... | collective-permute-start | bytes 199688 | tf_op jit(solution)/shard_map/ppermute | solution.py:24
  45.7 16.8 %collective-permute-start.2 = (f32[130,1,128]{2,0,1:T(8,128)}, f32[130,1,128]{2,0,1:T(8,128)}, u32[]{:S(2)}, u32[]{:S(2)}) collective-permute-start(f32[130,1,128]{2,0,1:T(8,128)} %copy.41), channel_id=1, source_target_pairs={{0,1},{1,2},{2,3},{3,4},{4,5},{5,6},{6,7},{7,0},{8,9},{9,10},{10,1... | collective-permute-start | bytes 199688 | tf_op jit(solution)/shard_map/ppermute | solution.py:22
  61.1 2.4 %copy-start.2 = (f32[130,16,128]{2,1,0:T(8,128)S(1)}, f32[130,16,128]{2,1,0:T(8,128)}, u32[]{:S(2)}) copy-start(f32[130,16,128]{2,1,0:T(8,128)} %copy-done.1) | copy-start | bytes 3194884
  61.1 2.4 %copy-start.4 = (f32[130,16,128]{2,1,0:T(8,128)S(1)}, f32[130,16,128]{2,1,0:T(8,128)}, u32[]{:S(2)}) copy-start(f32[130,16,128]{2,1,0:T(8,128)} %copy-done.3) | copy-start | bytes 3194884
  68.8 15.4 %collective-permute-start.11 = (f32[1,16,128]{2,1,0:T(8,128)S(1)}, f32[1,16,128]{2,1,0:T(8,128)S(1)}, u32[]{:S(2)}, u32[]{:S(2)}) collective-permute-start(f32[1,16,128]{2,1,0:T(8,128)S(1)} %get-tuple-element.565), channel_id=1, source_target_pairs={{8,0},{16,8},{24,16},{0,24},{9,1},{17,9},{25,17},{1,25},{10,2},{18... | collective-permute-start | bytes 24584 | tf_op jit(solution)/shard_map/ppermute | solution.py:24
  82.8 5.4 %collective-permute-start.10 = (f32[1,16,128]{2,1,0:T(8,128)S(1)}, f32[1,16,128]{2,1,0:T(8,128)S(1)}, u32[]{:S(2)}, u32[]{:S(2)}) collective-permute-start(f32[1,16,128]{2,1,0:T(8,128)S(1)} %get-tuple-element.564), channel_id=1, source_target_pairs={{0,8},{8,16},{16,24},{24,0},{1,9},{9,17},{17,25},{25,1},{2,10},{10... | collective-permute-start | bytes 24584 | tf_op jit(solution)/shard_map/ppermute | solution.py:22
  88.4 3.2 %collective-permute-start.13 = (f32[130,1,128]{2,0,1:T(8,128)S(1)}, f32[130,1,128]{2,0,1:T(8,128)S(1)}, u32[]{:S(2)}, u32[]{:S(2)}) collective-permute-start(f32[130,1,128]{2,0,1:T(8,128)S(1)} %copy.51), channel_id=1, source_target_pairs={{1,0},{2,1},{3,2},{4,3},{5,4},{6,5},{7,6},{0,7},{9,8},{10,9},{11,1... | collective-permute-start | bytes 199688 | tf_op jit(solution)/shard_map/ppermute | solution.py:24
  89.6 4.6 %collective-permute-start.12 = (f32[130,1,128]{2,0,1:T(8,128)S(1)}, f32[130,1,128]{2,0,1:T(8,128)S(1)}, u32[]{:S(2)}, u32[]{:S(2)}) collective-permute-start(f32[130,1,128]{2,0,1:T(8,128)S(1)} %copy.50), channel_id=1, source_target_pairs={{0,1},{1,2},{2,3},{3,4},{4,5},{5,6},{6,7},{7,0},{8,9},{9,10},{10,1... | collective-permute-start | bytes 199688 | tf_op jit(solution)/shard_map/ppermute | solution.py:22
  96.3 9.4 %copy-start.14 = (s32[256]{0:T(256)S(1)}, s32[256]{0:T(256)}, u32[]{:S(2)}) copy-start(s32[256]{0:T(256)} %param.37) | copy-start | bytes 3076
  99.3 5.8 %copy-start = (f32[128,16,128]{2,1,0:T(8,128)}, f32[128,16,128]{2,1,0:T(8,128)S(1)}, u32[]{:S(2)}) copy-start(f32[128,16,128]{2,1,0:T(8,128)S(1)} %fusion.71) | copy-start | bytes 3145732
  99.3 3.7 %collective-permute-start.15 = (f32[1,16,128]{2,1,0:T(8,128)S(1)}, f32[1,16,128]{2,1,0:T(8,128)S(1)}, u32[]{:S(2)}, u32[]{:S(2)}) collective-permute-start(f32[1,16,128]{2,1,0:T(8,128)S(1)} %get-tuple-element.563), channel_id=1, source_target_pairs={{8,0},{16,8},{24,16},{0,24},{9,1},{17,9},{25,17},{1,25},{10,2},{18... | collective-permute-start | bytes 24584 | tf_op jit(solution)/shard_map/ppermute | solution.py:24
  99.6 5.4 %collective-permute-start.14 = (f32[1,16,128]{2,1,0:T(8,128)S(1)}, f32[1,16,128]{2,1,0:T(8,128)S(1)}, u32[]{:S(2)}, u32[]{:S(2)}) collective-permute-start(f32[1,16,128]{2,1,0:T(8,128)S(1)} %get-tuple-element.562), channel_id=1, source_target_pairs={{0,8},{8,16},{16,24},{24,0},{1,9},{9,17},{17,25},{25,1},{2,10},{10... | collective-permute-start | bytes 24584 | tf_op jit(solution)/shard_map/ppermute | solution.py:22
  105.2 2.5 %collective-permute-start.17 = (f32[130,1,128]{2,0,1:T(8,128)S(1)}, f32[130,1,128]{2,0,1:T(8,128)S(1)}, u32[]{:S(2)}, u32[]{:S(2)}) collective-permute-start(f32[130,1,128]{2,0,1:T(8,128)S(1)} %copy.55), channel_id=1, source_target_pairs={{1,0},{2,1},{3,2},{4,3},{5,4},{6,5},{7,6},{0,7},{9,8},{10,9},{11,1... | collective-permute-start | bytes 199688 | tf_op jit(solution)/shard_map/ppermute | solution.py:24
  105.3 4.7 %collective-permute-start.16 = (f32[130,1,128]{2,0,1:T(8,128)S(1)}, f32[130,1,128]{2,0,1:T(8,128)S(1)}, u32[]{:S(2)}, u32[]{:S(2)}) collective-permute-start(f32[130,1,128]{2,0,1:T(8,128)S(1)} %copy.54), channel_id=1, source_target_pairs={{0,1},{1,2},{2,3},{3,4},{4,5},{5,6},{6,7},{7,0},{8,9},{9,10},{10,1... | collective-permute-start | bytes 199688 | tf_op jit(solution)/shard_map/ppermute | solution.py:22
  126.2 10.1 %collective-permute-start.18 = (f32[2048]{0:T(1024)S(1)}, f32[2048]{0:T(1024)S(1)}, u32[]{:S(2)}, u32[]{:S(2)}) collective-permute-start(f32[2048]{0:T(1024)S(1)} %bitcast.164), channel_id=1, source_target_pairs={{8,0},{16,8},{24,16},{0,24},{9,1},{17,9},{25,17},{1,25},{10,2},{18... | collective-permute-start | bytes 24584 | tf_op jit(solution)/shard_map/ppermute | solution.py:12
  126.3 14.3 %copy-start.12 = (s32[8192]{0:T(1024)S(1)}, s32[8192]{0:T(1024)}, u32[]{:S(2)}) copy-start(s32[8192]{0:T(1024)} %param.33) | copy-start | bytes 98308
  126.3 14.3 %copy-start.13 = (s32[8192]{0:T(1024)S(1)}, s32[8192]{0:T(1024)}, u32[]{:S(2)}) copy-start(s32[8192]{0:T(1024)} %param.34) | copy-start | bytes 98308
  126.3 18.8 %copy-start.8 = (f32[3,2048]{1,0:T(4,128)S(1)}, f32[3,2048]{1,0:T(4,128)}, u32[]{:S(2)}) copy-start(f32[3,2048]{1,0:T(4,128)} %param.31) | copy-start | bytes 73732
  136.3 11.5 %copy-start.7 = (f32[2048,128]{1,0:T(8,128)}, f32[2048,128]{1,0:T(8,128)S(1)}, u32[]{:S(2)}) copy-start(f32[2048,128]{1,0:T(8,128)S(1)} %get-tuple-element.898) | copy-start | bytes 3145732
  137.0 8.2 %all-to-all-start.2 = ((f32[8,1,256]{2,1,0:T(1,128)}), f32[8,1,256]{2,1,0:T(1,128)S(1)}, u32[]{:S(2)}, u32[]{:S(2)}) async-start(f32[8,1,256]{2,1,0:T(1,128)} %bitcast.20), calls=%async_computation.2 | async-start | bytes 16384 | tf_op jit(solution)/shard_map/all_to_all | solution.py:203
  145.6 12.9 %collective-permute-start.20 = (f32[4,256]{1,0:T(4,128)S(1)}, f32[4,256]{1,0:T(4,128)S(1)}, u32[]{:S(2)}, u32[]{:S(2)}) collective-permute-start(f32[4,256]{1,0:T(4,128)S(1)} %bitcast.165), channel_id=1, source_target_pairs={{8,0},{16,8},{24,16},{0,24},{9,1},{17,9},{25,17},{1,25},{10,2},{18... | collective-permute-start | bytes 12296 | tf_op jit(solution)/shard_map/ppermute | solution.py:24
  146.5 12.1 %collective-permute-start.19 = (f32[4,256]{1,0:T(4,128)S(1)}, f32[4,256]{1,0:T(4,128)S(1)}, u32[]{:S(2)}, u32[]{:S(2)}) collective-permute-start(f32[4,256]{1,0:T(4,128)S(1)} %bitcast.166), channel_id=1, source_target_pairs={{0,8},{8,16},{16,24},{24,0},{1,9},{9,17},{17,25},{25,1},{2,10},{10... | collective-permute-start | bytes 12296 | tf_op jit(solution)/shard_map/ppermute | solution.py:22
  158.7 11.4 %copy-start.9 = (f32[8192]{0:T(1024)S(1)}, f32[8192]{0:T(1024)}, u32[]{:S(2)}) copy-start(f32[8192]{0:T(1024)} %param.35) | copy-start | bytes 98308
  158.7 11.4 %copy-start.10 = (s32[8192]{0:T(1024)S(1)}, s32[8192]{0:T(1024)}, u32[]{:S(2)}) copy-start(s32[8192]{0:T(1024)} %param.36) | copy-start | bytes 98308
  170.2 11.4 %copy-start.11 = (f32[3,2048]{1,0:T(4,128)S(1)}, f32[3,2048]{1,0:T(4,128)}, u32[]{:S(2)}) copy-start(f32[3,2048]{1,0:T(4,128)} %param.32) | copy-start | bytes 73732
where the time goes:
time: 184 us; the launch traced here: 182 us
  matrix products  78.6 us (43%)
  starting transfers between devices  43.8 us (24%)
  waiting for transfers between devices  28.2 us (15%)
  other arithmetic  22.6 us (12%)
  local copies, waits for them, and re-layouts  6.33 us (3%)
    dot_general x21, matrix products, pick_block(): jnp.dot(row_hot, stacked_rows, precision=lax.Precision.HIGHEST, preferred...  40 us
    dot_general x12, matrix products, add_block(): lax.dot_general(row_hot, spread, (((0,), (0,)), ((), ())), precision=lax....  38.6 us
    ppermute x9, starting transfers between devices, with_halo(): lax.ppermute(head, axis, [((i + 1) % count, i) for i in range(count)])  25.1 us
    ppermute x9, waiting for transfers between devices, with_halo(): lax.ppermute(tail, axis, [(i, (i + 1) % count) for i in range(count)])  11 us
    add x3, other arithmetic, advance(): return center + (change + thermal_input)  8.74 us
    ppermute x9, waiting for transfers between devices, with_halo(): lax.ppermute(head, axis, [((i + 1) % count, i) for i in range(count)])  6.79 us
    ppermute x9, starting transfers between devices, with_halo(): lax.ppermute(tail, axis, [(i, (i + 1) % count) for i in range(count)])  5.61 us
    all_to_all x1, starting transfers between devices, per_device(): lax.all_to_all(patch_locator.reshape(groups, capacity), 'cross', split_ax...  5.18 us
  transfers between devices with their start and end apart: 24, of which 11 were waited for; matrix products, arithmetic and copies ran while one was open for 31% of the time, Pallas kernels for 0%

commit v1 on v0

v1 whole, which is shorter than its diff:
```python
import functools

import jax
import jax.numpy as jnp
from jax import lax
from jax.experimental import pallas as pl
from jax.experimental.pallas import tpu as pltpu
from jax.sharding import PartitionSpec as P

F32 = jnp.float32
BF16 = jnp.bfloat16
I32 = jnp.int32
LANES = 128
BOTH = ("cut", "cross")
VMEM = pl.BlockSpec(memory_space=pltpu.VMEM)
SMEM = pl.BlockSpec(memory_space=pltpu.SMEM)
LIMIT = 48 * 1024 * 1024


def call(kernel, outs, operands, scratch=(), smem=1):
    return pl.pallas_call(
        kernel,
        out_shape=outs,
        in_specs=[SMEM] * smem + [VMEM] * (len(operands) - smem),
        out_specs=[VMEM] * len(outs),
        scratch_shapes=list(scratch),
        compiler_params=pltpu.CompilerParams(vmem_limit_bytes=LIMIT),
    )(*operands)


def split(value):
    high = value.astype(BF16)
    return high, (value - high.astype(F32)).astype(BF16)


def iota(shape, dim):
    return lax.broadcasted_iota(I32, shape, dim)


def with_rim(rows, below, above):
    rim = (8, rows.shape[1])
    place = iota(rim, 0)
    extra = jnp.where(
        place == 0,
        jnp.broadcast_to(above, rim),
        jnp.where(place == 7, jnp.broadcast_to(below, rim), jnp.zeros(rim, F32)),
    )
    return jnp.concatenate([rows, extra], axis=0)


def conduct(kappa, temp):
    return (0.5 * kappa) * (0.5 + 1.0 / (1.0 + temp * temp))


def heat_pass(temp, temp_x, temp_y, kappa, kappa_x, kappa_y, put):
    count, rows, lanes = temp.shape
    lane = iota((rows, lanes), 1)
    total = rows + 8

    def plane(i):
        t = with_rim(temp[i], temp_y[0][pl.ds(i, 1), :], temp_y[1][pl.ds(i, 1), :])
        k = with_rim(kappa[i], kappa_y[0][pl.ds(i, 1), :], kappa_y[1][pl.ds(i, 1), :])
        return t, conduct(k, t)

    def finish(i, t, c, flux_x, above):
        flux_y = (c + pltpu.roll(c, total - 1, 0)) * (pltpu.roll(t, total - 1, 0) - t)
        net = (flux_y - pltpu.roll(flux_y, 1, 0))[:rows]
        t = t[:rows]
        c = c[:rows]
        edge = c * t
        flux_z = (c + pltpu.roll(c, lanes - 1, 1)) * (pltpu.roll(t, lanes - 1, 1) - t)
        flux_z = jnp.where(lane == lanes - 1, -edge, flux_z)
        net = net + (flux_z - jnp.where(lane == 0, edge, pltpu.roll(flux_z, 1, 1)))
        put(i, t + (net + (above - flux_x)))

    def step(i, carried):
        t, c, flux_x = carried
        t_next, c_next = plane(i + 1)
        above = (c[:rows] + c_next[:rows]) * (t_next[:rows] - t[:rows])
        finish(i, t, c, flux_x, above)
        return t_next, c_next, above

    t, c = plane(0)
    t_low = temp_x[0][...]
    flux_x = (c[:rows] + conduct(kappa_x[0][...], t_low)) * (t[:rows] - t_low)
    t, c, flux_x = lax.fori_loop(0, count - 1, step, (t, c, flux_x), unroll=2)
    t_high = temp_x[1][...]
    above = (c[:rows] + conduct(kappa_x[1][...], t_high)) * (t_high - t[:rows])
    finish(count - 1, t, c, flux_x, above)


def parts_of(got, me):
    blocks = got.shape[0]
    return ((me, False), (lax.rem(me + blocks - 1, blocks), True))


def local_cell(cell, upper, patch):
    cell = cell.astype(I32)
    if upper:
        return jnp.where(cell >= patch, cell - patch, -1)
    return jnp.where(cell < patch, cell, -1)


def deposit(me, got, shape, put, spread, along, across):
    planes, rows, lanes = shape
    half = got.shape[2] // 2
    patch = planes * rows * lanes
    place = iota((lanes, LANES), 0)
    row_place = iota((rows, LANES), 0)
    at = 0
    for block, upper in parts_of(got, me):
        for s in range(got.shape[1]):
            for h in range(half):
                cell = local_cell(got[block, s, h : h + 1, :], upper, patch)
                high, low = split(got[block, s, half + h : half + h + 1, :])
                here = place == (cell & (lanes - 1))
                zero = jnp.zeros((lanes, LANES), F32)
                span = slice(at, at + LANES)
                spread[0:lanes, span] = jnp.where(here, high.astype(F32), zero).astype(BF16)
                spread[lanes : 2 * lanes, span] = jnp.where(here, low.astype(F32), zero).astype(BF16)
                row = lax.shift_right_arithmetic(cell, 7)
                across[:, span] = jnp.where((row & (rows - 1)) == row_place, 1.0, 0.0).astype(BF16)
                along[:, span] = jnp.broadcast_to(row // rows, (rows, LANES)).astype(jnp.int16)
                at += LANES
    tile = 32

    def body(m, unused):
        where_x = along[...] - (m * tile).astype(jnp.int16)
        where_y = across[...]
        zero = jnp.zeros_like(where_y)
        hot = jnp.concatenate(
            [jnp.where(where_x == jnp.int16(x), where_y, zero) for x in range(tile)], axis=0
        )
        both = lax.dot_general(
            hot, spread[...], (((1,), (1,)), ((), ())), preferred_element_type=F32
        )
        put(m * tile, (both[:, :lanes] + both[:, lanes:]).reshape(tile, rows, lanes))
        return unused

    lax.fori_loop(0, planes // tile, body, 0)


def first_kernel(
    me, got, temp, tx0, tx1, ty0, ty1, kappa, kx0, kx1, ky0, ky1,
    source, temp_out, x0, x1, y0, y1, spread, along, across,
):
    def put_source(first, planes):
        source[pl.ds(first, planes.shape[0])] = planes

    deposit(me[0], got, temp.shape, put_source, spread, along, across)
    substep(temp, (tx0, tx1), (ty0, ty1), kappa, (kx0, kx1), (ky0, ky1), source, temp_out, y0, y1)
    x0[...] = temp_out[0]
    x1[...] = temp_out[temp_out.shape[0] - 1]


def substep(temp, temp_x, temp_y, kappa, kappa_x, kappa_y, source, out, y0=None, y1=None):
    def put(i, plane):
        plane = plane + source[i]
        out[i] = plane
        if y0 is not None:
            y0[pl.ds(i, 1), :] = plane[:1]
            y1[pl.ds(i, 1), :] = plane[-1:]

    heat_pass(temp, temp_x, temp_y, kappa, kappa_x, kappa_y, put)


def middle_kernel(
    temp, tx0, tx1, ty0, ty1, kappa, kx0, kx1, ky0, ky1, source, temp_out, x0, x1, y0, y1
):
    substep(temp, (tx0, tx1), (ty0, ty1), kappa, (kx0, kx1), (ky0, ky1), source, temp_out, y0, y1)
    x0[...] = temp_out[0]
    x1[...] = temp_out[temp_out.shape[0] - 1]


def last_kernel(
    me, got, temp, tx0, tx1, ty0, ty1, kappa, kx0, kx1, ky0, ky1, source,
    temp_out, looked, pieces, turned, found,
):
    substep(temp, (tx0, tx1), (ty0, ty1), kappa, (kx0, kx1), (ky0, ky1), source, temp_out)
    planes, rows, lanes = temp.shape
    high, low = split(temp_out[...].reshape(planes * rows, lanes))
    pieces[:, :lanes] = high
    pieces[:, lanes:] = low
    half = got.shape[2] // 2
    patch = planes * rows * lanes
    groups = got.shape[1]
    chunks = []
    for block, upper in parts_of(got, me[0]):
        for s in range(groups):
            for h in range(half):
                chunks.append(local_cell(got[block, s, h : h + 1, :], upper, patch))
    count = len(chunks)
    chunks.append(jnp.zeros((LANES - count, LANES), I32))
    turned[...] = jnp.concatenate(chunks, axis=0).T
    lane = iota((LANES, LANES), 1)
    found[...] = jnp.zeros((LANES, LANES), F32)
    width = 4
    for first in range(0, count, width):
        hots = []
        cells = []
        for k in range(first, first + width):
            cell = jnp.broadcast_to(turned[:, k : k + 1], (LANES, LANES))
            cells.append(cell)
            row = lax.shift_right_arithmetic(cell, 7).astype(jnp.int16)
            one = jnp.ones((LANES, LANES), BF16)
            hots.append(
                jnp.concatenate(
                    [
                        jnp.where(
                            row == (lane + r * LANES).astype(jnp.int16), one, jnp.zeros_like(one)
                        )
                        for r in range(planes * rows // LANES)
                    ],
                    axis=1,
                )
            )
        both = jnp.dot(jnp.concatenate(hots, axis=0), pieces[...], preferred_element_type=F32)
        value = both[:, :lanes] + both[:, lanes:]
        for n in range(width):
            picked = jnp.take_along_axis(
                value[n * LANES : (n + 1) * LANES], cells[n] & (lanes - 1), axis=1
            )
            found[...] = jnp.where(lane == first + n, picked, found[...])
    back = found[...].T
    at = 0
    for part in range(2):
        for s in range(groups):
            for h in range(half):
                looked[s, part * half + h : part * half + h + 1, :] = back[at : at + 1, :]
                at += 1


def pick(tables, index):
    row = lax.shift_right_logical(index, 7)
    lane = index & (LANES - 1)
    results = [jnp.zeros(index.shape, F32) for _ in tables]
    for r in range(len(tables[0])):
        here = row == r
        for ch, rows in enumerate(tables):
            value = jnp.take_along_axis(jnp.broadcast_to(rows[r], index.shape), lane, axis=1)
            results[ch] = jnp.where(here, value, results[ch])
    return results


def bond_kernel(
    me, back, pos, vel, acted, other, gap, snapped, low_pos, high_pos, low_export, high_export,
    pos_out, vel_out, force, hot,
):
    blocks, groups, double, _ = back.shape
    half = double // 2
    here = me[0]

    def block(distance):
        return lax.rem(here + (blocks + distance), blocks)

    def temps(distance):
        return [
            back[block(distance), j, h : h + 1, :] + back[block(distance + 1), j, half + h : half + h + 1, :]
            for j in range(groups)
            for h in range(half)
        ]

    def rows_of(ref, ch):
        return [ref[ch : ch + 1, r * LANES : (r + 1) * LANES] for r in range(ref.shape[1] // LANES)]

    def ghosts(ref, distance, export):
        tables = [
            [ref[ch, r : r + 1, :] for r in range(ref.shape[1])] for ch in range(3)
        ] + [temps(distance)]
        found = pick(tables, export[...])
        return [[f[r : r + 1] for r in range(f.shape[0])] for f in found]

    own = [rows_of(pos, ch) for ch in range(3)] + [temps(0)]
    low = ghosts(low_pos, -1, low_export)
    high = ghosts(high_pos, 1, high_export)
    wide = [own[ch] + low[ch] + high[ch] for ch in range(4)]
    first = pick(own, acted[...])
    second = pick(wide, other[...])
    delta = [second[ch] - first[ch] for ch in range(3)]
    dist = jnp.sqrt(delta[0] * delta[0] + delta[1] * delta[1] + delta[2] * delta[2])
    relaxed = gap[...] * (1.0 + 0.2 * (0.5 * (first[3] + second[3])))
    scale = (1.0 - snapped[...].astype(F32)) * (dist - relaxed) / jnp.maximum(dist, 0.3)
    values = [split(scale * d) for d in delta]
    values = [piece.astype(F32) for pair in values for piece in pair]
    high_count = len(own[0])
    place = iota((LANES, LANES), 0)
    high_place = iota((high_count, LANES), 0)
    for r in range(acted.shape[0]):
        index = acted[r : r + 1, :]
        span = slice(r * LANES, (r + 1) * LANES)
        hot[:, span] = jnp.where(place == (index & (LANES - 1)), 1.0, 0.0).astype(BF16)
        at_row = lax.shift_right_logical(index, 7) == high_place
        for n, value in enumerate(values):
            force[n * high_count : (n + 1) * high_count, span] = jnp.where(
                at_row, jnp.broadcast_to(value[r : r + 1], (high_count, LANES)), 0.0
            ).astype(BF16)
    total = lax.dot_general(
        force[...], hot[...], (((1,), (1,)), ((), ())), preferred_element_type=F32
    )
    for ch in range(3):
        base = 2 * ch * high_count
        summed = total[base : base + high_count] + total[base + high_count : base + 2 * high_count]
        for r in range(high_count):
            span = slice(r * LANES, (r + 1) * LANES)
            velocity = vel[ch : ch + 1, span] + 0.5 * summed[r : r + 1]
            vel_out[ch : ch + 1, span] = velocity
            pos_out[ch : ch + 1, span] = pos[ch : ch + 1, span] + 0.5 * velocity


def ring(block, distance):
    count = lax.axis_size("cut")
    return lax.ppermute(block, "cut", [(i, (i + distance) % count) for i in range(count)])


def line(block, distance):
    count = lax.axis_size("cross")
    pairs = [(i, i + distance) for i in range(count) if 0 <= i + distance < count]
    return lax.ppermute(block, "cross", pairs)


def per_device(
    warming_above_ambient,
    fourier_stability_factor,
    patch_locator,
    photon_gain_wattage,
    on_skin_marker,
    grain_placements,
    grain_motion_parts,
    tether_acted_grain,
    tether_other_grain,
    tether_relaxed_gap,
    snapped_marker,
    exported_copies,
):
    temp = warming_above_ambient
    kappa = fourier_stability_factor
    blocks = lax.axis_size("cut")
    groups = lax.axis_size("cross")
    planes, rows, lanes = temp.shape
    count = patch_locator.shape[0]
    half = count // groups // LANES
    me = lax.axis_index("cut").reshape(1).astype(I32)

    power = on_skin_marker.astype(F32) * photon_gain_wattage * 0.5
    parcel = jnp.concatenate(
        [
            patch_locator.astype(F32).reshape(groups, half, LANES),
            power.reshape(groups, half, LANES),
        ],
        axis=1,
    )

    def exchange(parcel):
        sent = jnp.broadcast_to(parcel[None], (blocks,) + parcel.shape)
        sent = sent.reshape((blocks * groups,) + parcel.shape[1:])
        got = lax.all_to_all(sent, BOTH, split_axis=0, concat_axis=0, tiled=True)
        return got.reshape((blocks, groups) + parcel.shape[1:])

    got = exchange(parcel)

    ghost = jnp.concatenate(
        [
            grain_placements.reshape(-1, LANES),
            exported_copies.astype(F32).reshape(-1, LANES),
        ],
        axis=0,
    )
    place_rows = grain_placements.size // LANES

    def side(plane):
        return jnp.concatenate([temp[plane], kappa[plane], ghost], axis=0)

    low = ring(side(planes - 1), 1)
    high = ring(side(0), -1)
    tx = (low[:rows], high[:rows])
    kx = (low[rows : 2 * rows], high[rows : 2 * rows])

    def neighbour(block):
        ghost = block[2 * rows :]
        return (
            ghost[:place_rows].reshape(3, -1, LANES),
            ghost[place_rows:].astype(I32),
        )

    low_pos, low_export = neighbour(low)
    high_pos, high_export = neighbour(high)
    y_low = line(jnp.stack([temp[:, rows - 1], kappa[:, rows - 1]]), 1)
    y_high = line(jnp.stack([temp[:, 0], kappa[:, 0]]), -1)
    ty = (y_low[0], y_high[0])
    ky = (y_low[1], y_high[1])

    grid = jax.ShapeDtypeStruct(temp.shape, F32)
    x_side = jax.ShapeDtypeStruct((rows, lanes), F32)
    y_side = jax.ShapeDtypeStruct((planes, lanes), F32)
    entries = 2 * count
    source, temp, x0, x1, y0, y1 = call(
        first_kernel,
        [grid, grid, x_side, x_side, y_side, y_side],
        [me, got, temp, *tx, *ty, kappa, *kx, *ky],
        [
            pltpu.VMEM((2 * lanes, entries), BF16),
            pltpu.VMEM((rows, entries), jnp.int16),
            pltpu.VMEM((rows, entries), BF16),
        ],
    )

    def halo():
        return (ring(x1, 1), ring(x0, -1)), (line(y1, 1), line(y0, -1))

    tx, ty = halo()
    temp, x0, x1, y0, y1 = call(
        middle_kernel,
        [grid, x_side, x_side, y_side, y_side],
        [temp, *tx, *ty, kappa, *kx, *ky, source],
        smem=0,
    )
    tx, ty = halo()
    temp, looked = call(
        last_kernel,
        [grid, jax.ShapeDtypeStruct((groups, 2 * half, LANES), F32)],
        [me, got, temp, *tx, *ty, kappa, *kx, *ky, source],
        [
            pltpu.VMEM((planes * rows, 2 * lanes), BF16),
            pltpu.VMEM((LANES, LANES), I32),
            pltpu.VMEM((LANES, LANES), F32),
        ],
    )
    back = exchange(looked)
    bonds = tether_acted_grain.shape[0]
    out = jax.ShapeDtypeStruct(grain_placements.shape, F32)
    positions_new, velocities_new = call(
        bond_kernel,
        [out, out],
        [
            me,
            back,
            grain_placements,
            grain_motion_parts,
            tether_acted_grain.reshape(-1, LANES),
            tether_other_grain.reshape(-1, LANES),
            tether_relaxed_gap.reshape(-1, LANES),
            snapped_marker.reshape(-1, LANES),
            low_pos,
            high_pos,
            low_export,
            high_export,
        ],
        [
            pltpu.VMEM((6 * (count // LANES), bonds), BF16),
            pltpu.VMEM((LANES, bonds), BF16),
        ],
    )
    return (temp, positions_new, velocities_new)


def solution(mesh):
    return jax.shard_map(
        per_device,
        mesh=mesh,
        in_specs=(
            P("cut", "cross", None),
            P("cut", "cross", None),
            P(("cut", "cross")),
            P(("cut", "cross")),
            P(("cut", "cross")),
            P(None, ("cut", "cross")),
            P(None, ("cut", "cross")),
            P(("cut", "cross")),
            P(("cut", "cross")),
            P(("cut", "cross")),
            P(("cut", "cross")),
            P(("cut", "cross")),
        ),
        out_specs=(P("cut", "cross", None), P(None, ("cut", "cross")), P(None, ("cut", "cross"))),
        check_vma=False,
    )
```

time: 184 us -> 110 us (0.60)
  matrix products: 78.6 us -> 0 us
  Pallas kernels: 0 us -> 46.4 us
  other arithmetic: 22.6 us -> 0.77 us
  waiting for transfers between devices: 28.2 us -> 16.7 us
  starting transfers between devices: 43.8 us -> 39.5 us
    dot_general x33 -> x0, matrix products: 78.6 us -> none  [the longest x21 40 us: pick_block(): jnp.dot(row_hot, stacked_rows, precision=lax.Precision.HIGHEST, preferred...]
    pallas_call x0 -> x4, Pallas kernels: none -> 46.4 us  [call(): pl.pallas_call(kernel, out_shape=outs, in_specs=[SMEM] * smem + [VMEM] *...]
    ppermute x21 -> x12, waiting for transfers between devices: 19 us -> 9.28 us  [the longest x6 7.61 us: line(): return lax.ppermute(block, 'cross', pairs)]
    add x6 -> x0, other arithmetic: 9.58 us -> none  [the longest x3 8.74 us: advance(): return center + (change + thermal_input)]
    mul x14 -> x1, other arithmetic: 7.93 us -> 0.01 us  [per_device(): power = on_skin_marker.astype(F32) * photon_gain_wattage * 0.5]
    ppermute x21 -> x12, starting transfers between devices: 30.8 us -> 24.4 us  [the longest x6 12.8 us: line(): return lax.ppermute(block, 'cross', pairs)]
    select_n x39 -> x0, other arithmetic: 3.47 us -> none  [the longest x3 2.44 us: clear_rim(): return jnp.where(drop, jnp.zeros_like(field), field)]
    ppermute x8 -> x0, local copies, waits for them, and re-layouts: 2.48 us -> none  [the longest x4 1.32 us: with_halo(): lax.ppermute(head, axis, [((i + 1) % count, i) for i in range(count)])]
  transfers between devices with their start and end apart: 24 -> 14, of which waited for: 11 -> 5; matrix products, arithmetic and copies ran while one was open for 31% -> 3% of each run, Pallas kernels for 0% -> 0%
where the time goes in v1:
time: 110 us; the launch traced here: 109 us
  Pallas kernels  46.4 us (42%)
  starting transfers between devices  39.5 us (36%)
  waiting for transfers between devices  16.7 us (15%)
  local copies, waits for them, and re-layouts  4.72 us (4%)
    pallas_call x4, Pallas kernels, call(): pl.pallas_call(kernel, out_shape=outs, in_specs=[SMEM] * smem + [VMEM] *...  46.4 us
    all_to_all x2, starting transfers between devices, exchange(): got = lax.all_to_all(sent, BOTH, split_axis=0, concat_axis=0, tiled=True)  15 us
    ppermute x6, starting transfers between devices, line(): return lax.ppermute(block, 'cross', pairs)  12.8 us
    ppermute x6, starting transfers between devices, ring(): lax.ppermute(block, 'cut', [(i, (i + distance) % count) for i in range(co...  11.6 us
    ppermute x6, waiting for transfers between devices, line(): return lax.ppermute(block, 'cross', pairs)  7.61 us
    all_to_all x2, waiting for transfers between devices, exchange(): got = lax.all_to_all(sent, BOTH, split_axis=0, concat_axis=0, tiled=True)  7.4 us
    slice x2, local copies, waits for them, and re-layouts, per_device(): y_high = line(jnp.stack([temp[:, 0], kappa[:, 0]]), -1)  2.58 us
  transfers between devices with their start and end apart: 14, of which 5 were waited for; matrix products, arithmetic and copies ran while one was open for 3% of the time, Pallas kernels for 0%

profile of v1, /device:TPU:0, one launch (start us, length us, event | category | flops | bytes accessed | tf_op | source)
XLA Modules:
  0.0 109.0 jit_solution(8404748493106274515)
XLA Ops:
  0.6 0.0 copy-start.9
  0.6 0.0 copy-start.8
  0.7 0.7 convert_element_type.15
  1.4 0.0 copy-done.9
  1.4 0.0 copy-done.8
  1.4 0.0 copy-start.10
  1.4 0.0 copy-start.2
  1.4 0.6 broadcast_in_dim.4
  2.1 7.3 %all-to-all-start = ((f32[32,4,128]{2,1,0:T(4,128)}), f32[32,4,128]{2,1,0:T(4,128)S(1)}, u32[]{:S(2)}, u32[]{:S(2)}) async-start(f32[32,4,128]{2,1,0:T(4,128)} %bitcast.3), calls=%async_computation | async-start | bytes 131072 | tf_op jit(solution)/shard_map/all_to_all | solution.py:356
  9.4 0.0 copy-done.10
  9.4 0.0 copy-done.2
  9.4 0.8 slice_bitcast_fusion.4
  10.2 3.7 %collective-permute-start.1 = (f32[82,128]{1,0:T(8,128)S(1)}, f32[82,128]{1,0:T(8,128)S(1)}, u32[]{:S(2)}, u32[]{:S(2)}) collective-permute-start(f32[82,128]{1,0:T(8,128)S(1)} %get-tuple-element.49), channel_id=1, source_target_pairs={{0,24},{8,0},{16,8},{24,16},{1,25},{9,1},{17,9},{25,17},{2,26},{10... | collective-permute-start | bytes 125960 | tf_op jit(solution)/shard_map/ppermute | solution.py:312
  13.9 0.0 collective-permute-start
  13.9 1.3 %fusion = (f32[128,1,128]{2,1,0:T(1,128)S(1)}, f32[128,1,128]{2,1,0:T(1,128)S(1)}) fusion(f32[128,16,128]{2,1,0:T(8,128)} %temp.1), kind=kLoop, calls=%fused_computation.19 | loop fusion | bytes 262144 | tf_op jit(solution)/shard_map/slice | solution.py:388
  15.2 1.3 %fusion.1 = (f32[128,1,128]{2,1,0:T(1,128)S(1)}, f32[128,1,128]{2,1,0:T(1,128)S(1)}) fusion(f32[128,16,128]{2,1,0:T(8,128)} %kappa.5), kind=kLoop, calls=%fused_computation.20 | loop fusion | bytes 262144 | tf_op jit(solution)/shard_map/slice | solution.py:388
  16.5 1.8 %collective-permute-start.2 = (f32[2,128,128]{2,1,0:T(8,128)S(1)}, f32[2,128,128]{2,1,0:T(8,128)S(1)}, u32[]{:S(2)}, u32[]{:S(2)}) collective-permute-start(f32[2,128,128]{2,1,0:T(8,128)S(1)} %pad_maximum_fusion), channel_id=1, source_target_pairs={{0,1},{1,2},{2,3},{3,4},{4,5},{5,6},{6,7},{8,9},{9,10},{10,11},{11... | collective-permute-start | bytes 393224 | tf_op jit(solution)/shard_map/ppermute | solution.py:318
  18.3 1.3 %collective-permute-start.3 = (f32[2,128,128]{2,1,0:T(8,128)S(1)}, f32[2,128,128]{2,1,0:T(8,128)S(1)}, u32[]{:S(2)}, u32[]{:S(2)}) collective-permute-start(f32[2,128,128]{2,1,0:T(8,128)S(1)} %pad_maximum_fusion.1), channel_id=1, source_target_pairs={{1,0},{2,1},{3,2},{4,3},{5,4},{6,5},{7,6},{9,8},{10,9},{11,10},{12... | collective-permute-start | bytes 393224 | tf_op jit(solution)/shard_map/ppermute | solution.py:318
  19.6 0.0 collective-permute-done.1
  19.6 0.1 collective-permute-done
  19.7 0.0 collective-permute-done.2
  19.7 3.0 %collective-permute-done.3 = f32[2,128,128]{2,1,0:T(8,128)S(1)} collective-permute-done((f32[2,128,128]{2,1,0:T(8,128)S(1)}, f32[2,128,128]{2,1,0:T(8,128)S(1)}, u32[]{:S(2)}, u32[]{:S(2)}) %collective-permute-start.3) | collective-permute-done | bytes 131104 | tf_op jit(solution)/shard_map/ppermute | solution.py:318
  22.8 0.0 all-to-all-done
  22.8 16.0 %shard_map.139 = (f32[128,16,128]{2,1,0:T(8,128)S(1)}, f32[128,16,128]{2,1,0:T(8,128)S(1)}, f32[16,128]{1,0:T(8,128)S(1)}, f32[16,128]{1,0:T(8,128)S(1)}, f32[12...) custom-call(s32[1]{0:T(128)} %bitcast.me, f32[4,8,4,128]{3,2,1,0:T(4,128)S(1)} %bitcast.43, f32[128,16,128]{2,1,0:T(8,128)S(1)} %copy-done.1, ...), custom_call_target="tpu_custom_call" | custom-call | tf_op jit(solution)/shard_map/pallas_call | solution.py:21
  38.8 5.4 %collective-permute-start.6 = (f32[128,128]{1,0:T(8,128)S(1)}, f32[128,128]{1,0:T(8,128)S(1)}, u32[]{:S(2)}, u32[]{:S(2)}) collective-permute-start(f32[128,128]{1,0:T(8,128)S(1)} %get-tuple-element.21), channel_id=1, source_target_pairs={{0,1},{1,2},{2,3},{3,4},{4,5},{5,6},{6,7},{8,9},{9,10},{10,11},{11... | collective-permute-start | bytes 196616 | tf_op jit(solution)/shard_map/ppermute | solution.py:318
  44.3 1.3 %collective-permute-start.7 = (f32[128,128]{1,0:T(8,128)S(1)}, f32[128,128]{1,0:T(8,128)S(1)}, u32[]{:S(2)}, u32[]{:S(2)}) collective-permute-start(f32[128,128]{1,0:T(8,128)S(1)} %get-tuple-element.22), channel_id=1, source_target_pairs={{1,0},{2,1},{3,2},{4,3},{5,4},{6,5},{7,6},{9,8},{10,9},{11,10},{12... | collective-permute-start | bytes 196616 | tf_op jit(solution)/shard_map/ppermute | solution.py:318
  45.6 0.2 collective-permute-start.4
  45.8 3.7 %collective-permute-start.5 = (f32[16,128]{1,0:T(8,128)S(1)}, f32[16,128]{1,0:T(8,128)S(1)}, u32[]{:S(2)}, u32[]{:S(2)}) collective-permute-start(f32[16,128]{1,0:T(8,128)S(1)} %get-tuple-element.20), channel_id=1, source_target_pairs={{0,24},{8,0},{16,8},{24,16},{1,25},{9,1},{17,9},{25,17},{2,26},{10... | collective-permute-start | bytes 24584 | tf_op jit(solution)/shard_map/ppermute | solution.py:312
  49.5 1.6 %collective-permute-done.4.tx0 = f32[16,128]{1,0:T(8,128)S(1)} collective-permute-done((f32[16,128]{1,0:T(8,128)S(1)}, f32[16,128]{1,0:T(8,128)S(1)}, u32[]{:S(2)}, u32[]{:S(2)}) %collective-permute-start.4) | collective-permute-done | bytes 8224 | tf_op jit(solution)/shard_map/ppermute | solution.py:312
  51.1 0.0 collective-permute-done.5.tx1
  51.1 0.0 collective-permute-done.6.ty0
  51.1 0.0 collective-permute-done.7.ty1
  51.1 10.1 %shard_map.140 = (f32[128,16,128]{2,1,0:T(8,128)S(1)}, f32[16,128]{1,0:T(8,128)S(1)}, f32[16,128]{1,0:T(8,128)S(1)}, f32[128,128]{1,0:T(8,128)S(1)}, f32[128,128]{1,0:T(8,128)S(1)}) custom-call(f32[128,16,128]{2,1,0:T(8,128)S(1)} %get-tuple-element.18.temp, f32[16,128]{1,0:T(8,128)S(1)} %collective-permute-done.4.tx0, ...), custom_call_target="tpu_custom_call" | custom-call | tf_op jit(solution)/shard_map/pallas_call | solution.py:21
  61.2 1.2 %collective-permute-start.8 = (f32[16,128]{1,0:T(8,128)S(1)}, f32[16,128]{1,0:T(8,128)S(1)}, u32[]{:S(2)}, u32[]{:S(2)}) collective-permute-start(f32[16,128]{1,0:T(8,128)S(1)} %get-tuple-element.25), channel_id=1, source_target_pairs={{0,8},{8,16},{16,24},{24,0},{1,9},{9,17},{17,25},{25,1},{2,10},{10... | collective-permute-start | bytes 24584 | tf_op jit(solution)/shard_map/ppermute | solution.py:312
  62.4 2.8 %collective-permute-start.9 = (f32[16,128]{1,0:T(8,128)S(1)}, f32[16,128]{1,0:T(8,128)S(1)}, u32[]{:S(2)}, u32[]{:S(2)}) collective-permute-start(f32[16,128]{1,0:T(8,128)S(1)} %get-tuple-element.26), channel_id=1, source_target_pairs={{0,24},{8,0},{16,8},{24,16},{1,25},{9,1},{17,9},{25,17},{2,26},{10... | collective-permute-start | bytes 24584 | tf_op jit(solution)/shard_map/ppermute | solution.py:312
  65.2 1.7 %collective-permute-start.10 = (f32[128,128]{1,0:T(8,128)S(1)}, f32[128,128]{1,0:T(8,128)S(1)}, u32[]{:S(2)}, u32[]{:S(2)}) collective-permute-start(f32[128,128]{1,0:T(8,128)S(1)} %get-tuple-element.27), channel_id=1, source_target_pairs={{0,1},{1,2},{2,3},{3,4},{4,5},{5,6},{6,7},{8,9},{9,10},{10,11},{11... | collective-permute-start | bytes 196616 | tf_op jit(solution)/shard_map/ppermute | solution.py:318
  66.9 1.3 %collective-permute-start.11 = (f32[128,128]{1,0:T(8,128)S(1)}, f32[128,128]{1,0:T(8,128)S(1)}, u32[]{:S(2)}, u32[]{:S(2)}) collective-permute-start(f32[128,128]{1,0:T(8,128)S(1)} %get-tuple-element.28), channel_id=1, source_target_pairs={{1,0},{2,1},{3,2},{4,3},{5,4},{6,5},{7,6},{9,8},{10,9},{11,10},{12... | collective-permute-start | bytes 196616 | tf_op jit(solution)/shard_map/ppermute | solution.py:318
  68.3 0.0 collective-permute-done.8.tx0
  68.3 0.0 collective-permute-done.9.tx1
  68.3 0.0 collective-permute-done.10.ty0
  68.3 4.6 %collective-permute-done.11.ty1 = f32[128,128]{1,0:T(8,128)S(1)} collective-permute-done((f32[128,128]{1,0:T(8,128)S(1)}, f32[128,128]{1,0:T(8,128)S(1)}, u32[]{:S(2)}, u32[]{:S(2)}) %collective-permute-start.11) | collective-permute-done | bytes 65568 | tf_op jit(solution)/shard_map/ppermute | solution.py:318
  72.9 15.1 %shard_map.141 = (f32[128,16,128]{2,1,0:T(8,128)}, f32[8,4,128]{2,1,0:T(4,128)S(1)}) custom-call(s32[1]{0:T(128)} %bitcast.me, f32[4,8,4,128]{3,2,1,0:T(4,128)S(1)} %bitcast.44, f32[128,16,128]{2,1,0:T(8,128)S(1)} %get-tuple-element.24.temp, f32[16,128]{1,0:T(8,128)S(1)} %collective-permute-done.8.tx0, f32[16,128]{1,0:T(8,128)S(1)} %collective-permute-done.9.tx1, ...), custom_call_target="tpu_custom_call" | custom-call | tf_op jit(solution)/shard_map/pallas_call | solution.py:21
  88.0 0.0 copy-start.7
  88.0 0.6 broadcast_in_dim.5
  88.7 7.7 %all-to-all-start.1 = ((f32[32,4,128]{2,1,0:T(4,128)}), f32[32,4,128]{2,1,0:T(4,128)S(1)}, u32[]{:S(2)}, u32[]{:S(2)}) async-start(f32[32,4,128]{2,1,0:T(4,128)} %bitcast.18), calls=%async_computation.1 | async-start | bytes 131072 | tf_op jit(solution)/shard_map/all_to_all | solution.py:356
  96.4 7.4 %all-to-all-done.1 = f32[32,4,128]{2,1,0:T(4,128)S(1)} async-done(((f32[32,4,128]{2,1,0:T(4,128)}), f32[32,4,128]{2,1,0:T(4,128)S(1)}, u32[]{:S(2)}, u32[]{:S(2)}) %all-to-all-start.1) | async-done | bytes 65568 | tf_op jit(solution)/shard_map/all_to_all | solution.py:356
  103.8 0.0 copy-done.7
  103.8 5.2 %shard_map.142 = (f32[3,2048]{1,0:T(4,128)}, f32[3,2048]{1,0:T(4,128)}) custom-call(s32[1]{0:T(128)} %bitcast.me, f32[4,8,4,128]{3,2,1,0:T(4,128)S(1)} %bitcast.45, f32[3,2048]{1,0:T(4,128)S(1)} %copy-done.2, f32[3,2048]{1,0:T(4,128)S(1)} %copy-done.3, s32[64,128]{1,0:T(8,128)S(1)} %bitcast.48, s32[64,128]{1,0:T(8,128)S(1)} %bitcast.49, ...), custom_call_target="tpu_custom_call" | custom-call | tf_op jit(solution)/shard_map/pallas_call | solution.py:21
  (27 shorter events, 0.1 us)
Async XLA Ops:
  0.6 0.7 copy-start.9
  0.6 0.7 copy-start.8
  1.4 8.0 %copy-start.10 = (s32[256]{0:T(256)S(1)}, s32[256]{0:T(256)}, u32[]{:S(2)}) copy-start(s32[256]{0:T(256)} %param.23) | copy-start | bytes 3076
  1.4 8.0 %copy-start.2 = (f32[3,2048]{1,0:T(4,128)S(1)}, f32[3,2048]{1,0:T(4,128)}, u32[]{:S(2)}) copy-start(f32[3,2048]{1,0:T(4,128)} %pos.1) | copy-start | bytes 73732
  2.1 20.7 %copy-start.1 = (f32[128,16,128]{2,1,0:T(8,128)S(1)}, f32[128,16,128]{2,1,0:T(8,128)}, u32[]{:S(2)}) copy-start(f32[128,16,128]{2,1,0:T(8,128)} %temp.1) | copy-start | bytes 3145732
  2.1 20.7 %copy-start = (f32[128,16,128]{2,1,0:T(8,128)S(1)}, f32[128,16,128]{2,1,0:T(8,128)}, u32[]{:S(2)}) copy-start(f32[128,16,128]{2,1,0:T(8,128)} %kappa.5) | copy-start | bytes 3145732
  2.1 20.7 %all-to-all-start = ((f32[32,4,128]{2,1,0:T(4,128)}), f32[32,4,128]{2,1,0:T(4,128)S(1)}, u32[]{:S(2)}, u32[]{:S(2)}) async-start(f32[32,4,128]{2,1,0:T(4,128)} %bitcast.3), calls=%async_computation | async-start | bytes 131072 | tf_op jit(solution)/shard_map/all_to_all | solution.py:356
  10.2 9.4 %collective-permute-start.1 = (f32[82,128]{1,0:T(8,128)S(1)}, f32[82,128]{1,0:T(8,128)S(1)}, u32[]{:S(2)}, u32[]{:S(2)}) collective-permute-start(f32[82,128]{1,0:T(8,128)S(1)} %get-tuple-element.49), channel_id=1, source_target_pairs={{0,24},{8,0},{16,8},{24,16},{1,25},{9,1},{17,9},{25,17},{2,26},{10... | collective-permute-start | bytes 125960 | tf_op jit(solution)/shard_map/ppermute | solution.py:312
  13.9 5.8 %collective-permute-start = (f32[82,128]{1,0:T(8,128)S(1)}, f32[82,128]{1,0:T(8,128)S(1)}, u32[]{:S(2)}, u32[]{:S(2)}) collective-permute-start(f32[82,128]{1,0:T(8,128)S(1)} %get-tuple-element.50), channel_id=1, source_target_pairs={{0,8},{8,16},{16,24},{24,0},{1,9},{9,17},{17,25},{25,1},{2,10},{10... | collective-permute-start | bytes 125960 | tf_op jit(solution)/shard_map/ppermute | solution.py:312
  16.5 3.2 %collective-permute-start.2 = (f32[2,128,128]{2,1,0:T(8,128)S(1)}, f32[2,128,128]{2,1,0:T(8,128)S(1)}, u32[]{:S(2)}, u32[]{:S(2)}) collective-permute-start(f32[2,128,128]{2,1,0:T(8,128)S(1)} %pad_maximum_fusion), channel_id=1, source_target_pairs={{0,1},{1,2},{2,3},{3,4},{4,5},{5,6},{6,7},{8,9},{9,10},{10,11},{11... | collective-permute-start | bytes 393224 | tf_op jit(solution)/shard_map/ppermute | solution.py:318
  18.3 4.5 %collective-permute-start.3 = (f32[2,128,128]{2,1,0:T(8,128)S(1)}, f32[2,128,128]{2,1,0:T(8,128)S(1)}, u32[]{:S(2)}, u32[]{:S(2)}) collective-permute-start(f32[2,128,128]{2,1,0:T(8,128)S(1)} %pad_maximum_fusion.1), channel_id=1, source_target_pairs={{1,0},{2,1},{3,2},{4,3},{5,4},{6,5},{7,6},{9,8},{10,9},{11,10},{12... | collective-permute-start | bytes 393224 | tf_op jit(solution)/shard_map/ppermute | solution.py:318
  38.8 12.3 %collective-permute-start.6 = (f32[128,128]{1,0:T(8,128)S(1)}, f32[128,128]{1,0:T(8,128)S(1)}, u32[]{:S(2)}, u32[]{:S(2)}) collective-permute-start(f32[128,128]{1,0:T(8,128)S(1)} %get-tuple-element.21), channel_id=1, source_target_pairs={{0,1},{1,2},{2,3},{3,4},{4,5},{5,6},{6,7},{8,9},{9,10},{10,11},{11... | collective-permute-start | bytes 196616 | tf_op jit(solution)/shard_map/ppermute | solution.py:318
  44.3 6.8 %collective-permute-start.7 = (f32[128,128]{1,0:T(8,128)S(1)}, f32[128,128]{1,0:T(8,128)S(1)}, u32[]{:S(2)}, u32[]{:S(2)}) collective-permute-start(f32[128,128]{1,0:T(8,128)S(1)} %get-tuple-element.22), channel_id=1, source_target_pairs={{1,0},{2,1},{3,2},{4,3},{5,4},{6,5},{7,6},{9,8},{10,9},{11,10},{12... | collective-permute-start | bytes 196616 | tf_op jit(solution)/shard_map/ppermute | solution.py:318
  45.6 5.5 %collective-permute-start.4 = (f32[16,128]{1,0:T(8,128)S(1)}, f32[16,128]{1,0:T(8,128)S(1)}, u32[]{:S(2)}, u32[]{:S(2)}) collective-permute-start(f32[16,128]{1,0:T(8,128)S(1)} %get-tuple-element.19), channel_id=1, source_target_pairs={{0,8},{8,16},{16,24},{24,0},{1,9},{9,17},{17,25},{25,1},{2,10},{10... | collective-permute-start | bytes 24584 | tf_op jit(solution)/shard_map/ppermute | solution.py:312
  45.8 5.3 %collective-permute-start.5 = (f32[16,128]{1,0:T(8,128)S(1)}, f32[16,128]{1,0:T(8,128)S(1)}, u32[]{:S(2)}, u32[]{:S(2)}) collective-permute-start(f32[16,128]{1,0:T(8,128)S(1)} %get-tuple-element.20), channel_id=1, source_target_pairs={{0,24},{8,0},{16,8},{24,16},{1,25},{9,1},{17,9},{25,17},{2,26},{10... | collective-permute-start | bytes 24584 | tf_op jit(solution)/shard_map/ppermute | solution.py:312
  61.2 7.1 %collective-permute-start.8 = (f32[16,128]{1,0:T(8,128)S(1)}, f32[16,128]{1,0:T(8,128)S(1)}, u32[]{:S(2)}, u32[]{:S(2)}) collective-permute-start(f32[16,128]{1,0:T(8,128)S(1)} %get-tuple-element.25), channel_id=1, source_target_pairs={{0,8},{8,16},{16,24},{24,0},{1,9},{9,17},{17,25},{25,1},{2,10},{10... | collective-permute-start | bytes 24584 | tf_op jit(solution)/shard_map/ppermute | solution.py:312
  62.4 5.9 %collective-permute-start.9 = (f32[16,128]{1,0:T(8,128)S(1)}, f32[16,128]{1,0:T(8,128)S(1)}, u32[]{:S(2)}, u32[]{:S(2)}) collective-permute-start(f32[16,128]{1,0:T(8,128)S(1)} %get-tuple-element.26), channel_id=1, source_target_pairs={{0,24},{8,0},{16,8},{24,16},{1,25},{9,1},{17,9},{25,17},{2,26},{10... | collective-permute-start | bytes 24584 | tf_op jit(solution)/shard_map/ppermute | solution.py:312
  65.2 3.1 %collective-permute-start.10 = (f32[128,128]{1,0:T(8,128)S(1)}, f32[128,128]{1,0:T(8,128)S(1)}, u32[]{:S(2)}, u32[]{:S(2)}) collective-permute-start(f32[128,128]{1,0:T(8,128)S(1)} %get-tuple-element.27), channel_id=1, source_target_pairs={{0,1},{1,2},{2,3},{3,4},{4,5},{5,6},{6,7},{8,9},{9,10},{10,11},{11... | collective-permute-start | bytes 196616 | tf_op jit(solution)/shard_map/ppermute | solution.py:318
  66.9 5.9 %collective-permute-start.11 = (f32[128,128]{1,0:T(8,128)S(1)}, f32[128,128]{1,0:T(8,128)S(1)}, u32[]{:S(2)}, u32[]{:S(2)}) collective-permute-start(f32[128,128]{1,0:T(8,128)S(1)} %get-tuple-element.28), channel_id=1, source_target_pairs={{1,0},{2,1},{3,2},{4,3},{5,4},{6,5},{7,6},{9,8},{10,9},{11,10},{12... | collective-permute-start | bytes 196616 | tf_op jit(solution)/shard_map/ppermute | solution.py:318
  88.0 15.8 %copy-start.7 = (s32[8192]{0:T(1024)S(1)}, s32[8192]{0:T(1024)}, u32[]{:S(2)}) copy-start(s32[8192]{0:T(1024)} %param.22) | copy-start | bytes 98308
  88.6 15.2 %copy-start.3 = (f32[3,2048]{1,0:T(4,128)S(1)}, f32[3,2048]{1,0:T(4,128)}, u32[]{:S(2)}) copy-start(f32[3,2048]{1,0:T(4,128)} %vel.1) | copy-start | bytes 73732
  88.7 15.2 %copy-start.4 = (s32[8192]{0:T(1024)S(1)}, s32[8192]{0:T(1024)}, u32[]{:S(2)}) copy-start(s32[8192]{0:T(1024)} %param.19) | copy-start | bytes 98308
  88.7 15.2 %copy-start.5 = (s32[8192]{0:T(1024)S(1)}, s32[8192]{0:T(1024)}, u32[]{:S(2)}) copy-start(s32[8192]{0:T(1024)} %param.20) | copy-start | bytes 98308
  88.7 15.2 %copy-start.6 = (f32[8192]{0:T(1024)S(1)}, f32[8192]{0:T(1024)}, u32[]{:S(2)}) copy-start(f32[8192]{0:T(1024)} %param.21) | copy-start | bytes 98308
  88.7 15.2 %all-to-all-start.1 = ((f32[32,4,128]{2,1,0:T(4,128)}), f32[32,4,128]{2,1,0:T(4,128)S(1)}, u32[]{:S(2)}, u32[]{:S(2)}) async-start(f32[32,4,128]{2,1,0:T(4,128)} %bitcast.18), calls=%async_computation.1 | async-start | bytes 131072 | tf_op jit(solution)/shard_map/all_to_all | solution.py:356

commit v2 on v1

v2 whole, which is shorter than its diff:
```python
import functools

import jax
import jax.numpy as jnp
from jax import lax
from jax.experimental import pallas as pl
from jax.experimental.pallas import tpu as pltpu
from jax.sharding import PartitionSpec as P

F32 = jnp.float32
BF16 = jnp.bfloat16
I32 = jnp.int32
LANES = 128
BOTH = ("cut", "cross")
VMEM = pl.BlockSpec(memory_space=pltpu.VMEM)
SMEM = pl.BlockSpec(memory_space=pltpu.SMEM)
LIMIT = 48 * 1024 * 1024


def call(kernel, outs, operands, scratch=(), smem=1):
    return pl.pallas_call(
        kernel,
        out_shape=outs,
        in_specs=[SMEM] * smem + [VMEM] * (len(operands) - smem),
        out_specs=[VMEM] * len(outs),
        scratch_shapes=list(scratch),
        compiler_params=pltpu.CompilerParams(vmem_limit_bytes=LIMIT),
    )(*operands)


def split(value):
    high = value.astype(BF16)
    return high, (value - high.astype(F32)).astype(BF16)


def iota(shape, dim):
    return lax.broadcasted_iota(I32, shape, dim)


RIM = 3
PAD = 8


def groups_of(count, most):
    return max(n for n in range(1, most + 1) if count % n == 0)


def difference_matrices(lanes):
    shape = (2 * lanes, 2 * lanes)
    given = iota(shape, 0) & (lanes - 1)
    wanted = iota(shape, 1)
    lower = wanted >= lanes
    wanted = wanted & (lanes - 1)
    beside = jnp.where(lower, wanted - 1, wanted + 1)
    neighbour = jnp.where(given == beside, 1.0, 0.0)
    same = jnp.where(given == wanted, 1.0, 0.0)
    return (neighbour - same).astype(BF16), (neighbour + same).astype(BF16)


def pieces_of(value):
    high, low = split(value)
    return jnp.concatenate([high, low], axis=1)


def conduct_pass(temp, kappa, cond, along_z, minus, plus, first, blocks, pitch):
    lanes = temp.shape[1]
    size = groups_of(blocks, 9)

    def body(n, unused):
        at = pl.ds(pl.multiple_of((first + n * size) * pitch, 8), size * pitch)
        t = temp[at, :]
        c = kappa[at, :] * (0.5 + 1.0 / (1.0 + t * t))
        cond[at, :] = c
        change = jnp.dot(pieces_of(t), minus[...], preferred_element_type=F32)
        both = jnp.dot(pieces_of(c), plus[...], preferred_element_type=F32)
        along_z[at, :] = change[:, :lanes] * both[:, :lanes] + change[:, lanes:] * both[:, lanes:]
        return unused

    lax.fori_loop(0, blocks // size, body, 0)


def flow_pass(temp, cond, along_z, first, blocks, pitch, most, put):
    size = groups_of(blocks, most)

    def body(n, unused):
        block = first + n * size
        base = pl.multiple_of(block * pitch, 8)
        at = pl.ds(base, size * pitch)
        t = temp[at, :]
        c = cond[at, :]
        net = along_z[at, :]
        for shift in (pitch, -pitch, 1, -1):
            beside = pl.ds(base + shift, size * pitch)
            net = net + (c + cond[beside, :]) * (temp[beside, :] - t)
        put(block, size, t + net)
        return unused

    lax.fori_loop(0, blocks // size, body, 0)


def rim_mask(ends, pitch, lanes):
    place = iota((pitch, lanes), 0)
    below = jnp.where(ends[0] > 0, 1.0, 0.0)
    above = jnp.where(ends[1] > 0, 1.0, 0.0)
    return jnp.where(place < PAD - RIM, above, jnp.where(place < PAD, below, 1.0))


def fill(flat, own, x_low, x_high, y_low, y_high, rows, pitch, scale):
    planes = own.shape[0] // rows
    total = planes + 2 * RIM
    flat[...] = jnp.zeros(flat.shape, F32)

    def place(p, part):
        flat[pl.ds(pl.multiple_of(p * pitch + PAD, 8), rows), :] = part * scale

    for n in range(RIM):
        place(n, x_low[n * rows : (n + 1) * rows, :])
        place(RIM + planes + n, x_high[n * rows : (n + 1) * rows, :])

    def body(p, unused):
        place(p + RIM, own[pl.ds(pl.multiple_of(p * rows, 8), rows), :])
        return unused

    lax.fori_loop(0, planes, body, 0, unroll=8)
    for r in range(RIM):
        flat[pl.ds(PAD - RIM + r, total, stride=pitch), :] = y_low[r, :total, :] * scale
        flat[pl.ds(PAD + rows + r, total, stride=pitch), :] = y_high[r, :total, :] * scale


def rows_kernel(temp, kappa, low, high, down, up):
    side = low.shape[0] // 2
    rows = side // RIM
    planes = temp.shape[0] // rows
    for n, own in enumerate((temp, kappa)):
        for r in range(RIM):
            for out, row in ((down, r), (up, rows - RIM + r)):
                target = n * RIM + r
                for p in range(RIM):
                    at = n * side + p * rows + row
                    out[target, p : p + 1, :] = low[at : at + 1, :]
                    out[target, RIM + planes + p : RIM + planes + p + 1, :] = high[at : at + 1, :]
                out[target, RIM : RIM + planes, :] = own[pl.ds(row, planes, stride=rows), :]


def open_kernel(
    ends, temp, kappa, x_low, x_high, y_low, y_high,
    spread_temp, spread_kappa, start, cond, along_z, minus, plus,
):
    lanes = temp.shape[1]
    side = x_low.shape[0] // 2
    rows = side // RIM
    pitch = rows + PAD
    planes = temp.shape[0] // rows
    minus[...], plus[...] = difference_matrices(lanes)
    fill(start, temp, x_low.at[:side], x_high.at[:side], y_low.at[:RIM], y_high.at[:RIM], rows, pitch, 1.0)
    fill(
        spread_kappa, kappa, x_low.at[side : 2 * side], x_high.at[side : 2 * side],
        y_low.at[RIM : 2 * RIM], y_high.at[RIM : 2 * RIM], rows, pitch, 0.5,
    )
    blocks = planes + 2 * RIM + 1
    conduct_pass(start, spread_kappa, cond, along_z, minus, plus, 0, blocks, pitch)
    mask = rim_mask(ends, pitch, lanes)
    for at in (0, blocks - 1):
        spread_temp[at * pitch : (at + 1) * pitch, :] = jnp.zeros((pitch, lanes), F32)
    spread_temp[blocks * pitch :, :] = jnp.zeros((spread_temp.shape[0] - blocks * pitch, lanes), F32)

    def put(block, size, value):
        value = value.reshape(size, pitch, lanes) * mask[None]
        at = pl.ds(pl.multiple_of(block * pitch, 8), size * pitch)
        spread_temp[at, :] = value.reshape(size * pitch, lanes)

    flow_pass(start, cond, along_z, 1, blocks - 2, pitch, 7, put)


def close_kernel(
    me, ends, got, opened, kappa, source_own, source_low, source_high,
    temp_out, looked, source, now, then, cond, along_z, minus, plus, pieces, turned, found,
):
    lanes = kappa.shape[1]
    planes, rows, _ = temp_out.shape
    pitch = rows + PAD
    total = planes + 2 * RIM
    blocks = total + 1
    minus[...], plus[...] = difference_matrices(lanes)
    wide = RIM - 1
    source[...] = source_own[...]
    for r in range(wide):
        source[pl.ds(PAD - wide + r, total, stride=pitch), :] = source_low[r, :total, :]
        source[pl.ds(PAD + rows + r, total, stride=pitch), :] = source_high[r, :total, :]
    now[...] = opened[...] + source[...]
    mask = rim_mask(ends, pitch, lanes)
    conduct_pass(now, kappa, cond, along_z, minus, plus, 0, blocks, pitch)
    then[0:pitch, :] = jnp.zeros((pitch, lanes), F32)
    then[(blocks - 1) * pitch :, :] = jnp.zeros((then.shape[0] - (blocks - 1) * pitch, lanes), F32)

    def middle(block, size, value):
        at = pl.ds(pl.multiple_of(block * pitch, 8), size * pitch)
        value = (value + source[at, :]).reshape(size, pitch, lanes) * mask[None]
        then[at, :] = value.reshape(size * pitch, lanes)

    flow_pass(now, cond, along_z, 1, blocks - 2, pitch, 7, middle)
    conduct_pass(then, kappa, cond, along_z, minus, plus, 0, blocks, pitch)

    def last(block, size, value):
        at = pl.ds(pl.multiple_of(block * pitch, 8), size * pitch)
        value = (value + source[at, :]).reshape(size, pitch, lanes)[:, PAD:]
        temp_out[pl.ds(block - RIM, size)] = value
        high, low = split(value.reshape(size * rows, lanes))
        at = pl.ds(pl.multiple_of((block - RIM) * rows, rows), size * rows)
        pieces[at, :lanes] = high
        pieces[at, lanes:] = low

    flow_pass(then, cond, along_z, RIM, planes, pitch, 8, last)
    lookup(me[0], got, planes * rows, lanes, looked, pieces, turned, found)


def deposit_kernel(planes, me, got, source, down, up, spread, across, inside, beside):
    blocks, groups, double, _ = got.shape
    half = double // 2
    lanes = source.shape[1]
    rows = across.shape[0]
    pitch = rows + PAD
    patch = planes * rows * lanes
    count = groups * half * LANES
    here = me[0]
    place = iota((rows, LANES), 0)
    place16 = place.astype(jnp.int16)
    zero = jnp.zeros((rows, LANES), BF16)
    order = (1, 0, blocks - 1, blocks - 2)

    for part, distance in enumerate(order):
        block = lax.rem(here + distance, blocks)

        def body(s, unused, part=part, block=block):
            for h in range(half):
                at = pl.multiple_of((s * half + h) * LANES, LANES)
                span = pl.ds(part * count + at, LANES)
                cell = jnp.broadcast_to(got[block, s, h : h + 1, :], (rows, LANES)).astype(I32)
                power = jnp.broadcast_to(got[block, s, half + h : half + h + 1, :], (rows, LANES))
                high, low = split(power)
                lane = (cell & (lanes - 1)).astype(jnp.int16)
                for t in range(lanes // rows):
                    hit = lane == place16 + jnp.int16(t * rows)
                    spread[t * rows : (t + 1) * rows, span] = jnp.where(hit, high, zero)
                    spread[lanes + t * rows : lanes + (t + 1) * rows, span] = jnp.where(hit, low, zero)
                upper = cell >= patch
                row = lax.shift_right_logical(jnp.where(upper, cell - patch, cell), 7)
                across[:, span] = jnp.where((row & (rows - 1)) == place, 1.0, 0.0).astype(BF16)
                plane = row // rows
                own = jnp.where(upper, -1, plane).astype(jnp.int16)
                on = jnp.where(upper, plane, -1).astype(jnp.int16)
                if part == 0:
                    beside[:, span] = own
                elif part == 1:
                    inside[:, pl.ds(at, LANES)] = own
                    beside[:, span] = on
                elif part == 2:
                    inside[:, pl.ds(count + at, LANES)] = on
                    beside[:, span] = own
                else:
                    beside[:, span] = on
            return unused

        lax.fori_loop(0, groups, body, 0)

    source[...] = jnp.zeros(source.shape, F32)

    def product(first, tile, where_x, columns):
        where_y = across[:, columns]
        nothing = jnp.zeros_like(where_y)
        hot = jnp.concatenate(
            [jnp.where(where_x == jnp.int16(x), where_y, nothing) for x in range(tile)], axis=0
        )
        both = lax.dot_general(
            hot, spread[:, columns], (((1,), (1,)), ((), ())), preferred_element_type=F32
        )
        value = both[:, :lanes] + both[:, lanes:]
        for n in range(tile):
            at = pl.ds(pl.multiple_of((first + n + RIM) * pitch + PAD, 8), rows)
            source[at, :] = value[n * rows : (n + 1) * rows]

    tile = 32

    def body(m, unused):
        product(m * tile, tile, inside[...] - (m * tile).astype(jnp.int16), slice(count, 3 * count))
        return unused

    lax.fori_loop(0, planes // tile, body, 0)
    wide = RIM - 1
    product(planes, wide, beside[:, : 2 * count], slice(0, 2 * count))
    low = beside[:, 2 * count :] - jnp.int16(planes - wide)
    product(-wide, wide, low, slice(2 * count, 4 * count))
    planes_all = planes + 2 * RIM
    for r in range(wide):
        down[r, :planes_all, :] = source[pl.ds(PAD + r, planes_all, stride=pitch), :]
        up[r, :planes_all, :] = source[pl.ds(PAD + rows - wide + r, planes_all, stride=pitch), :]


def lookup(me, got, height, lanes, looked, pieces, turned, found):
    blocks, groups, double, _ = got.shape
    half = double // 2
    patch = height * lanes
    chunks = []
    for block, upper in ((me, False), (lax.rem(me + blocks - 1, blocks), True)):
        for s in range(groups):
            for h in range(half):
                cell = got[block, s, h : h + 1, :].astype(I32)
                if upper:
                    cell = jnp.where(cell >= patch, cell - patch, -1)
                else:
                    cell = jnp.where(cell < patch, cell, -1)
                chunks.append(cell)
    count = len(chunks)
    chunks.append(jnp.zeros((LANES - count, LANES), I32))
    turned[...] = jnp.concatenate(chunks, axis=0).T
    lane = iota((LANES, LANES), 1)
    found[...] = jnp.zeros((LANES, LANES), F32)
    width = 4
    for first in range(0, count, width):
        hots = []
        cells = []
        for k in range(first, first + width):
            cell = jnp.broadcast_to(turned[:, k : k + 1], (LANES, LANES))
            cells.append(cell)
            row = lax.shift_right_arithmetic(cell, 7).astype(jnp.int16)
            one = jnp.ones((LANES, LANES), BF16)
            hots.append(
                jnp.concatenate(
                    [
                        jnp.where(
                            row == (lane + r * LANES).astype(jnp.int16), one, jnp.zeros_like(one)
                        )
                        for r in range(height // LANES)
                    ],
                    axis=1,
                )
            )
        both = jnp.dot(jnp.concatenate(hots, axis=0), pieces[...], preferred_element_type=F32)
        value = both[:, :lanes] + both[:, lanes:]
        for n in range(width):
            picked = jnp.take_along_axis(
                value[n * LANES : (n + 1) * LANES], cells[n] & (lanes - 1), axis=1
            )
            found[...] = jnp.where(lane == first + n, picked, found[...])
    back = found[...].T
    at = 0
    for part in range(2):
        for s in range(groups):
            for h in range(half):
                looked[s, part * half + h : part * half + h + 1, :] = back[at : at + 1, :]
                at += 1


def pick(tables, index):
    row = lax.shift_right_logical(index, 7)
    lane = index & (LANES - 1)
    results = [jnp.zeros(index.shape, F32) for _ in tables]
    for r in range(len(tables[0])):
        here = row == r
        for ch, rows in enumerate(tables):
            value = jnp.take_along_axis(jnp.broadcast_to(rows[r], index.shape), lane, axis=1)
            results[ch] = jnp.where(here, value, results[ch])
    return results


def bond_kernel(
    me, back, pos, vel, acted, other, gap, snapped, low_pos, high_pos, low_export, high_export,
    pos_out, vel_out, force, hot,
):
    blocks, groups, double, _ = back.shape
    half = double // 2
    here = me[0]

    def block(distance):
        return lax.rem(here + (blocks + distance), blocks)

    def temps(distance):
        return [
            back[block(distance), j, h : h + 1, :] + back[block(distance + 1), j, half + h : half + h + 1, :]
            for j in range(groups)
            for h in range(half)
        ]

    def rows_of(ref, ch):
        return [ref[ch : ch + 1, r * LANES : (r + 1) * LANES] for r in range(ref.shape[1] // LANES)]

    def ghosts(ref, distance, export):
        tables = [
            [ref[ch, r : r + 1, :] for r in range(ref.shape[1])] for ch in range(3)
        ] + [temps(distance)]
        found = pick(tables, export[...])
        return [[f[r : r + 1] for r in range(f.shape[0])] for f in found]

    own = [rows_of(pos, ch) for ch in range(3)] + [temps(0)]
    low = ghosts(low_pos, -1, low_export)
    high = ghosts(high_pos, 1, high_export)
    wide = [own[ch] + low[ch] + high[ch] for ch in range(4)]
    first = pick(own, acted[...])
    second = pick(wide, other[...])
    delta = [second[ch] - first[ch] for ch in range(3)]
    dist = jnp.sqrt(delta[0] * delta[0] + delta[1] * delta[1] + delta[2] * delta[2])
    relaxed = gap[...] * (1.0 + 0.2 * (0.5 * (first[3] + second[3])))
    scale = (1.0 - snapped[...].astype(F32)) * (dist - relaxed) / jnp.maximum(dist, 0.3)
    values = [split(scale * d) for d in delta]
    values = [piece.astype(F32) for pair in values for piece in pair]
    high_count = len(own[0])
    place = iota((LANES, LANES), 0)
    high_place = iota((high_count, LANES), 0)
    for r in range(acted.shape[0]):
        index = acted[r : r + 1, :]
        span = slice(r * LANES, (r + 1) * LANES)
        hot[:, span] = jnp.where(place == (index & (LANES - 1)), 1.0, 0.0).astype(BF16)
        at_row = lax.shift_right_logical(index, 7) == high_place
        for n, value in enumerate(values):
            force[n * high_count : (n + 1) * high_count, span] = jnp.where(
                at_row, jnp.broadcast_to(value[r : r + 1], (high_count, LANES)), 0.0
            ).astype(BF16)
    total = lax.dot_general(
        force[...], hot[...], (((1,), (1,)), ((), ())), preferred_element_type=F32
    )
    for ch in range(3):
        base = 2 * ch * high_count
        summed = total[base : base + high_count] + total[base + high_count : base + 2 * high_count]
        for r in range(high_count):
            span = slice(r * LANES, (r + 1) * LANES)
            velocity = vel[ch : ch + 1, span] + 0.5 * summed[r : r + 1]
            vel_out[ch : ch + 1, span] = velocity
            pos_out[ch : ch + 1, span] = pos[ch : ch + 1, span] + 0.5 * velocity


def ring(block, distance):
    count = lax.axis_size("cut")
    return lax.ppermute(block, "cut", [(i, (i + distance) % count) for i in range(count)])


def line(block, distance):
    count = lax.axis_size("cross")
    pairs = [(i, i + distance) for i in range(count) if 0 <= i + distance < count]
    return lax.ppermute(block, "cross", pairs)


def per_device(
    warming_above_ambient,
    fourier_stability_factor,
    patch_locator,
    photon_gain_wattage,
    on_skin_marker,
    grain_placements,
    grain_motion_parts,
    tether_acted_grain,
    tether_other_grain,
    tether_relaxed_gap,
    snapped_marker,
    exported_copies,
):
    planes, rows, lanes = warming_above_ambient.shape
    temp = warming_above_ambient.reshape(planes * rows, lanes)
    kappa = fourier_stability_factor.reshape(planes * rows, lanes)
    blocks = lax.axis_size("cut")
    groups = lax.axis_size("cross")
    count = patch_locator.shape[0]
    half = count // groups // LANES
    me = lax.axis_index("cut").reshape(1).astype(I32)
    side = lax.axis_index("cross")
    ends = jnp.stack([side > 0, side < groups - 1]).astype(I32)
    pitch = rows + PAD
    total = planes + 2 * RIM
    flat = jax.ShapeDtypeStruct(((total + 2) * pitch, lanes), F32)
    wide = RIM * rows

    ghost = jnp.concatenate(
        [
            grain_placements.reshape(-1, LANES),
            exported_copies.astype(F32).reshape(-1, LANES),
        ],
        axis=0,
    )
    place_rows = grain_placements.size // LANES
    height = planes * rows
    low = ring(jnp.concatenate([temp[height - wide :], kappa[height - wide :], ghost], axis=0), 1)
    high = ring(jnp.concatenate([temp[:wide], kappa[:wide], ghost], axis=0), -1)

    def neighbour(block):
        ghost = block[2 * wide :]
        return (
            block[: 2 * wide],
            ghost[:place_rows].reshape(3, -1, LANES),
            ghost[place_rows:].astype(I32),
        )

    x_low, low_pos, low_export = neighbour(low)
    x_high, high_pos, high_export = neighbour(high)

    power = on_skin_marker.astype(F32) * photon_gain_wattage * 0.5
    parcel = jnp.concatenate(
        [
            patch_locator.astype(F32).reshape(groups, half, LANES),
            power.reshape(groups, half, LANES),
        ],
        axis=1,
    )

    def exchange(parcel):
        sent = jnp.broadcast_to(parcel[None], (blocks,) + parcel.shape)
        sent = sent.reshape((blocks * groups,) + parcel.shape[1:])
        got = lax.all_to_all(sent, BOTH, split_axis=0, concat_axis=0, tiled=True)
        return got.reshape((blocks, groups) + parcel.shape[1:])

    got = exchange(parcel)

    across = jax.ShapeDtypeStruct((2 * RIM, -(-total // 8) * 8, lanes), F32)
    down, up = call(rows_kernel, [across, across], [temp, kappa, x_low, x_high], smem=0)
    y_low, y_high = line(up, 1), line(down, -1)

    strips = jax.ShapeDtypeStruct((RIM - 1,) + across.shape[1:], F32)
    entries = count
    source, down, up = call(
        functools.partial(deposit_kernel, planes),
        [flat, strips, strips],
        [me, got],
        [
            pltpu.VMEM((2 * lanes, 4 * entries), BF16),
            pltpu.VMEM((rows, 4 * entries), BF16),
            pltpu.VMEM((rows, 2 * entries), jnp.int16),
            pltpu.VMEM((rows, 4 * entries), jnp.int16),
        ],
    )
    source_low, source_high = line(up, 1), line(down, -1)

    grid = pltpu.VMEM(flat.shape, F32)
    matrix = pltpu.VMEM((2 * lanes, 2 * lanes), BF16)
    opened, kappa = call(
        open_kernel,
        [flat, flat],
        [ends, temp, kappa, x_low, x_high, y_low, y_high],
        [grid, grid, grid, matrix, matrix],
    )
    temp, looked = call(
        close_kernel,
        [
            jax.ShapeDtypeStruct((planes, rows, lanes), F32),
            jax.ShapeDtypeStruct((groups, 2 * half, LANES), F32),
        ],
        [me, ends, got, opened, kappa, source, source_low, source_high],
        [
            grid, grid, grid, grid, grid, matrix, matrix,
            pltpu.VMEM((planes * rows, 2 * lanes), BF16),
            pltpu.VMEM((LANES, LANES), I32),
            pltpu.VMEM((LANES, LANES), F32),
        ],
        smem=2,
    )
    back = exchange(looked)
    bonds = tether_acted_grain.shape[0]
    out = jax.ShapeDtypeStruct(grain_placements.shape, F32)
    positions_new, velocities_new = call(
        bond_kernel,
        [out, out],
        [
            me,
            back,
            grain_placements,
            grain_motion_parts,
            tether_acted_grain.reshape(-1, LANES),
            tether_other_grain.reshape(-1, LANES),
            tether_relaxed_gap.reshape(-1, LANES),
            snapped_marker.reshape(-1, LANES),
            low_pos,
            high_pos,
            low_export,
            high_export,
        ],
        [
            pltpu.VMEM((6 * (count // LANES), bonds), BF16),
            pltpu.VMEM((LANES, bonds), BF16),
        ],
    )
    return (temp, positions_new, velocities_new)


def solution(mesh):
    return jax.shard_map(
        per_device,
        mesh=mesh,
        in_specs=(
            P("cut", "cross", None),
            P("cut", "cross", None),
            P(("cut", "cross")),
            P(("cut", "cross")),
            P(("cut", "cross")),
            P(None, ("cut", "cross")),
            P(None, ("cut", "cross")),
            P(("cut", "cross")),
            P(("cut", "cross")),
            P(("cut", "cross")),
            P(("cut", "cross")),
            P(("cut", "cross")),
        ),
        out_specs=(P("cut", "cross", None), P(None, ("cut", "cross")), P(None, ("cut", "cross"))),
        check_vma=False,
    )
```

time: 110 us -> 88.7 us (0.81)
  starting transfers between devices: 39.5 us -> 21.4 us
  Pallas kernels: 46.4 us -> 36.8 us
  local copies, waits for them, and re-layouts: 4.72 us -> 7.5 us
  waiting for transfers between devices: 16.7 us -> 19.3 us
  other arithmetic: 0.77 us -> 2.21 us
    pallas_call x4 -> x5, Pallas kernels: 46.4 us -> 36.8 us  [call(): pl.pallas_call(kernel, out_shape=outs, in_specs=[SMEM] * smem + [VMEM] *...]
    ppermute x6 -> x4, waiting for transfers between devices: 7.61 us -> 0.01 us  [line(): return lax.ppermute(block, 'cross', pairs)]
    all_to_all x2, waiting for transfers between devices: 7.4 us -> 14.5 us  [exchange(): got = lax.all_to_all(sent, BOTH, split_axis=0, concat_axis=0, tiled=True)]
    ppermute x6 -> x4, starting transfers between devices: 12.8 us -> 5.91 us  [line(): return lax.ppermute(block, 'cross', pairs)]
    ppermute x6 -> x2, starting transfers between devices: 11.6 us -> 5.1 us  [ring(): lax.ppermute(block, 'cut', [(i, (i + distance) % count) for i in range(co...]
    all_to_all x2, starting transfers between devices: 15 us -> 10.4 us  [exchange(): got = lax.all_to_all(sent, BOTH, split_axis=0, concat_axis=0, tiled=True)]
    unnamed x22, local copies, waits for them, and re-layouts: 0.05 us -> 3.92 us
    ppermute x6 -> x2, waiting for transfers between devices: 1.67 us -> 4.77 us  [ring(): lax.ppermute(block, 'cut', [(i, (i + distance) % count) for i in range(co...]
  transfers between devices with their start and end apart: 14 -> 8, of which waited for: 5 -> 4; matrix products, arithmetic and copies ran while one was open for 3% -> 2% of each run, Pallas kernels for 0% -> 17%
where the time goes in v2:
time: 88.7 us; the launch traced here: 88.1 us
  Pallas kernels  36.8 us (41%)
  starting transfers between devices  21.4 us (24%)
  waiting for transfers between devices  19.3 us (22%)
  local copies, waits for them, and re-layouts  7.5 us (8%)
  other arithmetic  2.21 us (2%)
    pallas_call x5, Pallas kernels, call(): pl.pallas_call(kernel, out_shape=outs, in_specs=[SMEM] * smem + [VMEM] *...  36.8 us
    all_to_all x2, waiting for transfers between devices, exchange(): got = lax.all_to_all(sent, BOTH, split_axis=0, concat_axis=0, tiled=True)  14.5 us
    all_to_all x2, starting transfers between devices, exchange(): got = lax.all_to_all(sent, BOTH, split_axis=0, concat_axis=0, tiled=True)  10.4 us
    ppermute x4, starting transfers between devices, line(): return lax.ppermute(block, 'cross', pairs)  5.91 us
    ppermute x2, starting transfers between devices, ring(): lax.ppermute(block, 'cut', [(i, (i + distance) % count) for i in range(co...  5.1 us
    ppermute x2, waiting for transfers between devices, ring(): lax.ppermute(block, 'cut', [(i, (i + distance) % count) for i in range(co...  4.77 us
    unnamed x22, local copies, waits for them, and re-layouts  3.92 us
  transfers between devices with their start and end apart: 8, of which 4 were waited for; matrix products, arithmetic and copies ran while one was open for 2% of the time, Pallas kernels for 17%

profile of v2, /device:TPU:0, one launch (start us, length us, event | category | flops | bytes accessed | tf_op | source)
XLA Modules:
  0.0 88.1 jit_solution(13899211373418444522)
XLA Ops:
  0.6 0.7 convert_bitcast_fusion
  1.3 0.8 reshape.70
  2.1 0.8 fusion
  2.9 0.8 fusion.1
  3.6 5.1 %collective-permute-start.1 = (f32[146,128]{1,0:T(8,128)S(1)}, f32[146,128]{1,0:T(8,128)S(1)}, u32[]{:S(2)}, u32[]{:S(2)}) collective-permute-start(f32[146,128]{1,0:T(8,128)S(1)} %get-tuple-element.29), channel_id=1, source_target_pairs={{0,24},{8,0},{16,8},{24,16},{1,25},{9,1},{17,9},{25,17},{2,26},{10... | collective-permute-start | bytes 224264 | tf_op jit(solution)/shard_map/ppermute | solution.py:433
  8.7 0.0 collective-permute-start
  8.7 0.7 multiply_multiply_fusion
  9.5 0.7 convert_element_type.19
  10.2 1.0 %collective-permute-done.1 = f32[146,128]{1,0:T(8,128)S(1)} collective-permute-done((f32[146,128]{1,0:T(8,128)S(1)}, f32[146,128]{1,0:T(8,128)S(1)}, u32[]{:S(2)}, u32[]{:S(2)}) %collective-permute-start.1) | collective-permute-done | bytes 74784 | tf_op jit(solution)/shard_map/ppermute | solution.py:433
  11.2 3.7 %collective-permute-done = f32[146,128]{1,0:T(8,128)S(1)} collective-permute-done((f32[146,128]{1,0:T(8,128)S(1)}, f32[146,128]{1,0:T(8,128)S(1)}, u32[]{:S(2)}, u32[]{:S(2)}) %collective-permute-start) | collective-permute-done | bytes 74784 | tf_op jit(solution)/shard_map/ppermute | solution.py:433
  14.9 0.0 copy-start
  14.9 1.2 %copy-done = f32[128,16,128]{2,1,0:T(8,128)S(1)} copy-done((f32[128,16,128]{2,1,0:T(8,128)S(1)}, f32[128,16,128]{2,1,0:T(8,128)}, u32[]{:S(2)}) %copy-start) | copy-done | bytes 1048600
  16.2 0.0 copy-start.2
  16.2 1.2 %copy-done.2 = f32[128,16,128]{2,1,0:T(8,128)S(1)} copy-done((f32[128,16,128]{2,1,0:T(8,128)S(1)}, f32[128,16,128]{2,1,0:T(8,128)}, u32[]{:S(2)}) %copy-start.2) | copy-done | bytes 1048600
  17.4 0.0 copy-start.1
  17.4 0.0 copy-start.3
  17.4 1.2 %shard_map.139 = (f32[6,136,128]{2,1,0:T(8,128)}, f32[6,136,128]{2,1,0:T(8,128)}) custom-call(f32[2048,128]{1,0:T(8,128)S(1)} %bitcast.23, f32[2048,128]{1,0:T(8,128)S(1)} %bitcast.25, f32[96,128]{1,0:T(8,128)S(1)} %slice.62.low.x_low, f32[96,128]{1,0:T(8,128)S(1)} %slice.63.high.x_high), custom_call_target="tpu_custom_call" | custom-call | tf_op jit(solution)/shard_map/pallas_call | solution.py:21
  18.6 1.3 %collective-permute-start.2 = (f32[6,136,128]{2,1,0:T(8,128)}, f32[6,136,128]{2,1,0:T(8,128)S(1)}, u32[]{:S(2)}, u32[]{:S(2)}) collective-permute-start(f32[6,136,128]{2,1,0:T(8,128)} %get-tuple-element.14), channel_id=1, source_target_pairs={{0,1},{1,2},{2,3},{3,4},{4,5},{5,6},{6,7},{8,9},{9,10},{10,11},{11... | collective-permute-start | bytes 1253384 | tf_op jit(solution)/shard_map/ppermute | solution.py:439
  19.9 1.3 %collective-permute-start.3 = (f32[6,136,128]{2,1,0:T(8,128)}, f32[6,136,128]{2,1,0:T(8,128)S(1)}, u32[]{:S(2)}, u32[]{:S(2)}) collective-permute-start(f32[6,136,128]{2,1,0:T(8,128)} %get-tuple-element.15), channel_id=1, source_target_pairs={{1,0},{2,1},{3,2},{4,3},{5,4},{6,5},{7,6},{9,8},{10,9},{11,10},{12... | collective-permute-start | bytes 1253384 | tf_op jit(solution)/shard_map/ppermute | solution.py:439
  21.2 0.6 broadcast_in_dim.4
  21.9 5.8 %all-to-all-start = ((f32[32,4,128]{2,1,0:T(4,128)}), f32[32,4,128]{2,1,0:T(4,128)S(1)}, u32[]{:S(2)}, u32[]{:S(2)}) async-start(f32[32,4,128]{2,1,0:T(4,128)} %bitcast.5), calls=%async_computation | async-start | bytes 131072 | tf_op jit(solution)/shard_map/all_to_all | solution.py:506
  27.7 0.1 add_convert_fusion.ends
  27.7 7.3 %all-to-all-done = f32[32,4,128]{2,1,0:T(4,128)S(1)} async-done(((f32[32,4,128]{2,1,0:T(4,128)}), f32[32,4,128]{2,1,0:T(4,128)S(1)}, u32[]{:S(2)}, u32[]{:S(2)}) %all-to-all-start) | async-done | bytes 65568 | tf_op jit(solution)/shard_map/all_to_all | solution.py:506
  35.1 8.1 %shard_map.141 = (f32[3264,128]{1,0:T(8,128)S(1)}, f32[2,136,128]{2,1,0:T(8,128)S(1)}, f32[2,136,128]{2,1,0:T(8,128)S(1)}) custom-call(s32[1]{0:T(128)} %bitcast.me, f32[4,8,4,128]{3,2,1,0:T(4,128)S(1)} %bitcast.27), custom_call_target="tpu_custom_call" | custom-call | tf_op jit(solution)/shard_map/pallas_call | solution.py:21
  43.1 2.0 %collective-permute-start.4 = (f32[2,136,128]{2,1,0:T(8,128)S(1)}, f32[2,136,128]{2,1,0:T(8,128)S(1)}, u32[]{:S(2)}, u32[]{:S(2)}) collective-permute-start(f32[2,136,128]{2,1,0:T(8,128)S(1)} %get-tuple-element.19), channel_id=1, source_target_pairs={{0,1},{1,2},{2,3},{3,4},{4,5},{5,6},{6,7},{8,9},{9,10},{10,11},{11... | collective-permute-start | bytes 417800 | tf_op jit(solution)/shard_map/ppermute | solution.py:439
  45.2 1.3 %collective-permute-start.5 = (f32[2,136,128]{2,1,0:T(8,128)S(1)}, f32[2,136,128]{2,1,0:T(8,128)S(1)}, u32[]{:S(2)}, u32[]{:S(2)}) collective-permute-start(f32[2,136,128]{2,1,0:T(8,128)S(1)} %get-tuple-element.20), channel_id=1, source_target_pairs={{1,0},{2,1},{3,2},{4,3},{5,4},{6,5},{7,6},{9,8},{10,9},{11,10},{12... | collective-permute-start | bytes 417800 | tf_op jit(solution)/shard_map/ppermute | solution.py:439
  46.5 0.0 collective-permute-done.2.y_low
  46.5 0.0 collective-permute-done.3.y_high
  46.5 0.0 copy-done.1
  46.5 0.0 copy-done.3
  46.5 7.2 %shard_map.140 = (f32[3264,128]{1,0:T(8,128)S(1)}, f32[3264,128]{1,0:T(8,128)}) custom-call(s32[2]{0:T(128)S(1)} %add_convert_fusion.ends, f32[2048,128]{1,0:T(8,128)S(1)} %bitcast.24, f32[2048,128]{1,0:T(8,128)S(1)} %bitcast.26, f32[96,128]{1,0:T(8,128)S(1)} %slice.62.low.x_low, f32[96,128]{1,0:T(8,128)S(1)} %slice.63.high.x_high, ...), custom_call_target="tpu_custom_call" | custom-call | tf_op jit(solution)/shard_map/pallas_call | solution.py:21
  53.8 0.0 collective-permute-done.4.source_low
  53.8 0.0 collective-permute-done.5.source_high
  53.8 0.0 copy-start.4
  53.8 1.4 %copy-done.4 = f32[3264,128]{1,0:T(8,128)S(1)} copy-done((f32[3264,128]{1,0:T(8,128)S(1)}, f32[3264,128]{1,0:T(8,128)}, u32[]{:S(2)}) %copy-start.4) | copy-done | bytes 1671192
  55.2 0.0 copy-start.9
  55.2 0.0 copy-start.10
  55.2 15.1 %shard_map.142 = (f32[128,16,128]{2,1,0:T(8,128)}, f32[8,4,128]{2,1,0:T(4,128)S(1)}) custom-call(s32[1]{0:T(128)} %bitcast.me, s32[2]{0:T(128)S(1)} %add_convert_fusion.ends, f32[4,8,4,128]{3,2,1,0:T(4,128)S(1)} %bitcast.28, f32[3264,128]{1,0:T(8,128)S(1)} %get-tuple-element.16.opened, f32[3264,128]{1,0:T(8,128)S(1)} %copy-done.4, ...), custom_call_target="tpu_custom_call" | custom-call | tf_op jit(solution)/shard_map/pallas_call | solution.py:21
  70.3 0.6 broadcast_in_dim.5
  71.0 4.6 %all-to-all-start.1 = ((f32[32,4,128]{2,1,0:T(4,128)}), f32[32,4,128]{2,1,0:T(4,128)S(1)}, u32[]{:S(2)}, u32[]{:S(2)}) async-start(f32[32,4,128]{2,1,0:T(4,128)} %bitcast.14), calls=%async_computation.1 | async-start | bytes 131072 | tf_op jit(solution)/shard_map/all_to_all | solution.py:506
  75.6 7.2 %all-to-all-done.1 = f32[32,4,128]{2,1,0:T(4,128)S(1)} async-done(((f32[32,4,128]{2,1,0:T(4,128)}), f32[32,4,128]{2,1,0:T(4,128)S(1)}, u32[]{:S(2)}, u32[]{:S(2)}) %all-to-all-start.1) | async-done | bytes 65568 | tf_op jit(solution)/shard_map/all_to_all | solution.py:506
  82.8 0.0 copy-done.5
  82.8 0.0 copy-done.6
  82.8 0.0 copy-done.7
  82.9 0.0 copy-done.8
  82.9 0.0 copy-done.9
  82.9 0.0 copy-done.10
  82.9 5.2 %shard_map.143 = (f32[3,2048]{1,0:T(4,128)}, f32[3,2048]{1,0:T(4,128)}) custom-call(s32[1]{0:T(128)} %bitcast.me, f32[4,8,4,128]{3,2,1,0:T(4,128)S(1)} %bitcast.29, f32[3,2048]{1,0:T(4,128)S(1)} %copy-done.5, f32[3,2048]{1,0:T(4,128)S(1)} %copy-done.6, s32[64,128]{1,0:T(8,128)S(1)} %bitcast.32, s32[64,128]{1,0:T(8,128)S(1)} %bitcast.33, ...), custom_call_target="tpu_custom_call" | custom-call | tf_op jit(solution)/shard_map/pallas_call | solution.py:21
  (12 shorter events, 0.1 us)
Async XLA Ops:
  3.6 7.6 %collective-permute-start.1 = (f32[146,128]{1,0:T(8,128)S(1)}, f32[146,128]{1,0:T(8,128)S(1)}, u32[]{:S(2)}, u32[]{:S(2)}) collective-permute-start(f32[146,128]{1,0:T(8,128)S(1)} %get-tuple-element.29), channel_id=1, source_target_pairs={{0,24},{8,0},{16,8},{24,16},{1,25},{9,1},{17,9},{25,17},{2,26},{10... | collective-permute-start | bytes 224264 | tf_op jit(solution)/shard_map/ppermute | solution.py:433
  8.7 6.2 %collective-permute-start = (f32[146,128]{1,0:T(8,128)S(1)}, f32[146,128]{1,0:T(8,128)S(1)}, u32[]{:S(2)}, u32[]{:S(2)}) collective-permute-start(f32[146,128]{1,0:T(8,128)S(1)} %get-tuple-element.30), channel_id=1, source_target_pairs={{0,8},{8,16},{16,24},{24,0},{1,9},{9,17},{17,25},{25,1},{2,10},{10... | collective-permute-start | bytes 224264 | tf_op jit(solution)/shard_map/ppermute | solution.py:433
  14.9 1.2 %copy-start = (f32[128,16,128]{2,1,0:T(8,128)S(1)}, f32[128,16,128]{2,1,0:T(8,128)}, u32[]{:S(2)}) copy-start(f32[128,16,128]{2,1,0:T(8,128)} %param.12) | copy-start | bytes 3145732
  16.2 1.2 %copy-start.2 = (f32[128,16,128]{2,1,0:T(8,128)S(1)}, f32[128,16,128]{2,1,0:T(8,128)}, u32[]{:S(2)}) copy-start(f32[128,16,128]{2,1,0:T(8,128)} %param.13) | copy-start | bytes 3145732
  17.4 29.1 %copy-start.1 = (f32[128,16,128]{2,1,0:T(8,128)S(1)}, f32[128,16,128]{2,1,0:T(8,128)}, u32[]{:S(2)}) copy-start(f32[128,16,128]{2,1,0:T(8,128)} %param.12) | copy-start | bytes 3145732
  17.4 29.1 %copy-start.3 = (f32[128,16,128]{2,1,0:T(8,128)S(1)}, f32[128,16,128]{2,1,0:T(8,128)}, u32[]{:S(2)}) copy-start(f32[128,16,128]{2,1,0:T(8,128)} %param.13) | copy-start | bytes 3145732
  18.6 27.9 %collective-permute-start.2 = (f32[6,136,128]{2,1,0:T(8,128)}, f32[6,136,128]{2,1,0:T(8,128)S(1)}, u32[]{:S(2)}, u32[]{:S(2)}) collective-permute-start(f32[6,136,128]{2,1,0:T(8,128)} %get-tuple-element.14), channel_id=1, source_target_pairs={{0,1},{1,2},{2,3},{3,4},{4,5},{5,6},{6,7},{8,9},{9,10},{10,11},{11... | collective-permute-start | bytes 1253384 | tf_op jit(solution)/shard_map/ppermute | solution.py:439
  19.9 26.6 %collective-permute-start.3 = (f32[6,136,128]{2,1,0:T(8,128)}, f32[6,136,128]{2,1,0:T(8,128)S(1)}, u32[]{:S(2)}, u32[]{:S(2)}) collective-permute-start(f32[6,136,128]{2,1,0:T(8,128)} %get-tuple-element.15), channel_id=1, source_target_pairs={{1,0},{2,1},{3,2},{4,3},{5,4},{6,5},{7,6},{9,8},{10,9},{11,10},{12... | collective-permute-start | bytes 1253384 | tf_op jit(solution)/shard_map/ppermute | solution.py:439
  21.9 13.2 %all-to-all-start = ((f32[32,4,128]{2,1,0:T(4,128)}), f32[32,4,128]{2,1,0:T(4,128)S(1)}, u32[]{:S(2)}, u32[]{:S(2)}) async-start(f32[32,4,128]{2,1,0:T(4,128)} %bitcast.5), calls=%async_computation | async-start | bytes 131072 | tf_op jit(solution)/shard_map/all_to_all | solution.py:506
  43.1 10.6 %collective-permute-start.4 = (f32[2,136,128]{2,1,0:T(8,128)S(1)}, f32[2,136,128]{2,1,0:T(8,128)S(1)}, u32[]{:S(2)}, u32[]{:S(2)}) collective-permute-start(f32[2,136,128]{2,1,0:T(8,128)S(1)} %get-tuple-element.19), channel_id=1, source_target_pairs={{0,1},{1,2},{2,3},{3,4},{4,5},{5,6},{6,7},{8,9},{9,10},{10,11},{11... | collective-permute-start | bytes 417800 | tf_op jit(solution)/shard_map/ppermute | solution.py:439
  45.2 8.6 %collective-permute-start.5 = (f32[2,136,128]{2,1,0:T(8,128)S(1)}, f32[2,136,128]{2,1,0:T(8,128)S(1)}, u32[]{:S(2)}, u32[]{:S(2)}) collective-permute-start(f32[2,136,128]{2,1,0:T(8,128)S(1)} %get-tuple-element.20), channel_id=1, source_target_pairs={{1,0},{2,1},{3,2},{4,3},{5,4},{6,5},{7,6},{9,8},{10,9},{11,10},{12... | collective-permute-start | bytes 417800 | tf_op jit(solution)/shard_map/ppermute | solution.py:439
  53.8 1.4 %copy-start.4 = (f32[3264,128]{1,0:T(8,128)S(1)}, f32[3264,128]{1,0:T(8,128)}, u32[]{:S(2)}) copy-start(f32[3264,128]{1,0:T(8,128)} %get-tuple-element.17.kappa) | copy-start | bytes 5013508
  55.2 27.6 %copy-start.5 = (f32[3,2048]{1,0:T(4,128)S(1)}, f32[3,2048]{1,0:T(4,128)}, u32[]{:S(2)}) copy-start(f32[3,2048]{1,0:T(4,128)} %pos.1) | copy-start | bytes 73732
  55.2 27.6 %copy-start.6 = (f32[3,2048]{1,0:T(4,128)S(1)}, f32[3,2048]{1,0:T(4,128)}, u32[]{:S(2)}) copy-start(f32[3,2048]{1,0:T(4,128)} %vel.1) | copy-start | bytes 73732
  55.2 27.6 %copy-start.7 = (s32[8192]{0:T(1024)S(1)}, s32[8192]{0:T(1024)}, u32[]{:S(2)}) copy-start(s32[8192]{0:T(1024)} %param.19) | copy-start | bytes 98308
  55.2 27.6 %copy-start.8 = (s32[8192]{0:T(1024)S(1)}, s32[8192]{0:T(1024)}, u32[]{:S(2)}) copy-start(s32[8192]{0:T(1024)} %param.20) | copy-start | bytes 98308
  55.2 27.7 %copy-start.9 = (f32[8192]{0:T(1024)S(1)}, f32[8192]{0:T(1024)}, u32[]{:S(2)}) copy-start(f32[8192]{0:T(1024)} %param.21) | copy-start | bytes 98308
  55.2 27.6 %copy-start.10 = (s32[8192]{0:T(1024)S(1)}, s32[8192]{0:T(1024)}, u32[]{:S(2)}) copy-start(s32[8192]{0:T(1024)} %param.22) | copy-start | bytes 98308
  71.0 11.9 %all-to-all-start.1 = ((f32[32,4,128]{2,1,0:T(4,128)}), f32[32,4,128]{2,1,0:T(4,128)S(1)}, u32[]{:S(2)}, u32[]{:S(2)}) async-start(f32[32,4,128]{2,1,0:T(4,128)} %bitcast.14), calls=%async_computation.1 | async-start | bytes 131072 | tf_op jit(solution)/shard_map/all_to_all | solution.py:506

commit v3 on v2

--- a/solution.py
+++ b/solution.py
@@ -13,19 +13,40 @@
 LANES = 128
 BOTH = ("cut", "cross")
 VMEM = pl.BlockSpec(memory_space=pltpu.VMEM)
-SMEM = pl.BlockSpec(memory_space=pltpu.SMEM)
-LIMIT = 48 * 1024 * 1024
-
-
-def call(kernel, outs, operands, scratch=(), smem=1):
+LIMIT = 32 * 1024 * 1024
+
+
+def call(kernel, outs, operands, scratch=(), left=0, limit=LIMIT):
     return pl.pallas_call(
         kernel,
         out_shape=outs,
-        in_specs=[SMEM] * smem + [VMEM] * (len(operands) - smem),
+        in_specs=[pl.BlockSpec(memory_space=pltpu.HBM)] * left + [VMEM] * (len(operands) - left),
         out_specs=[VMEM] * len(outs),
         scratch_shapes=list(scratch),
-        compiler_params=pltpu.CompilerParams(vmem_limit_bytes=LIMIT),
+        compiler_params=pltpu.CompilerParams(vmem_limit_bytes=limit),
     )(*operands)
+
+
+class Either:
+    def __init__(self, flag, yes, no):
+        self.flag, self.yes, self.no = flag, yes, no
+        self.shape = yes.shape
+
+    def __getitem__(self, index):
+        yes, no = self.yes[index], self.no[index]
+        return jnp.where(jnp.full(yes.shape, self.flag, I32) > 0, yes, no)
+
+    def part(self, index):
+        return Either(self.flag, self.yes.at[index], self.no.at[index])
+
+
+def is_odd(axis):
+    return lax.rem(lax.axis_index(axis), 2)
+
+
+def low_and_high(axis, even, odd):
+    flag = is_odd(axis)
+    return Either(flag, even, odd), Either(flag, odd, even)
 
 
 def split(value):
@@ -64,7 +85,7 @@
 
 def conduct_pass(temp, kappa, cond, along_z, minus, plus, first, blocks, pitch):
     lanes = temp.shape[1]
-    size = groups_of(blocks, 9)
+    size = groups_of(blocks, 135)
 
     def body(n, unused):
         at = pl.ds(pl.multiple_of((first + n * size) * pitch, 8), size * pitch)
@@ -98,10 +119,11 @@
     lax.fori_loop(0, blocks // size, body, 0)
 
 
-def rim_mask(ends, pitch, lanes):
+def rim_mask(pitch, lanes):
     place = iota((pitch, lanes), 0)
-    below = jnp.where(ends[0] > 0, 1.0, 0.0)
-    above = jnp.where(ends[1] > 0, 1.0, 0.0)
+    side = lax.axis_index("cross")
+    below = jnp.where(side > 0, 1.0, 0.0)
+    above = jnp.where(side < lax.axis_size("cross") - 1, 1.0, 0.0)
     return jnp.where(place < PAD - RIM, above, jnp.where(place < PAD, below, 1.0))
 
 
@@ -127,39 +149,80 @@
         flat[pl.ds(PAD + rows + r, total, stride=pitch), :] = y_high[r, :total, :] * scale
 
 
-def rows_kernel(temp, kappa, low, high, down, up):
-    side = low.shape[0] // 2
-    rows = side // RIM
+def parcel_kernel(
+    temp, kappa, cells, watts, marks, pos, export, sent, even, odd,
+    cell_in, watt_in, mark_in, pos_in, export_in, sems,
+):
+    count = pos.shape[1] // LANES
+    exports = export.shape[0]
+    wide = (even.shape[0] - 3 * count - exports) // 2
+    height = temp.shape[0]
+    moves = [(cells, cell_in), (watts, watt_in), (marks, mark_in), (pos, pos_in), (export, export_in)]
+    tail = (1 - is_odd("cut")) * (height - wide)
+    for n, field in enumerate((temp, kappa)):
+        target = pl.ds(n * wide, wide)
+        for out, start in ((even, tail), (odd, height - wide - tail)):
+            moves.append((field.at[pl.ds(pl.multiple_of(start, 16), wide)], out.at[target]))
+    copies = [pltpu.make_async_copy(*move, sems.at[n]) for n, move in enumerate(moves)]
+    for copy in copies:
+        copy.start()
+    for copy in copies[:3]:
+        copy.wait()
+    power = mark_in[...].astype(F32) * watt_in[...] * 0.5
+    cell = cell_in[...].astype(F32)
+    blocks, groups, double, _ = sent.shape
+    half = double // 2
+    for block in range(blocks):
+        for s in range(groups):
+            sent[block, s, :half, :] = cell[s * half : (s + 1) * half]
+            sent[block, s, half:, :] = power[s * half : (s + 1) * half]
+    for copy in copies[3:5]:
+        copy.wait()
+    for out in (even, odd):
+        for ch in range(3):
+            for r in range(count):
+                at = 2 * wide + ch * count + r
+                out[at : at + 1, :] = pos_in[ch : ch + 1, r * LANES : (r + 1) * LANES]
+        out[2 * wide + 3 * count :, :] = export_in[...].astype(F32)
+    for copy in copies[5:]:
+        copy.wait()
+
+
+def rows_kernel(rows, after, temp, kappa, even_x, odd_x, even, odd):
+    side = RIM * rows
     planes = temp.shape[0] // rows
+    low, high = low_and_high("cut", even_x, odd_x)
+    top = (1 - is_odd("cross")) * (rows - RIM)
     for n, own in enumerate((temp, kappa)):
         for r in range(RIM):
-            for out, row in ((down, r), (up, rows - RIM + r)):
+            for out, first in ((even, top), (odd, rows - RIM - top)):
                 target = n * RIM + r
                 for p in range(RIM):
-                    at = n * side + p * rows + row
-                    out[target, p : p + 1, :] = low[at : at + 1, :]
-                    out[target, RIM + planes + p : RIM + planes + p + 1, :] = high[at : at + 1, :]
-                out[target, RIM : RIM + planes, :] = own[pl.ds(row, planes, stride=rows), :]
+                    at = pl.ds(n * side + p * rows + first + r, 1)
+                    out[target, p : p + 1, :] = low[at, :]
+                    out[target, RIM + planes + p : RIM + planes + p + 1, :] = high[at, :]
+                out[target, RIM : RIM + planes, :] = own[pl.ds(first + r, planes, stride=rows), :]
 
 
 def open_kernel(
-    ends, temp, kappa, x_low, x_high, y_low, y_high,
+    rows, temp, kappa, source, even_x, odd_x, even_y, odd_y,
     spread_temp, spread_kappa, start, cond, along_z, minus, plus,
 ):
     lanes = temp.shape[1]
-    side = x_low.shape[0] // 2
-    rows = side // RIM
+    x_low, x_high = low_and_high("cut", even_x, odd_x)
+    y_low, y_high = low_and_high("cross", even_y, odd_y)
+    side = RIM * rows
     pitch = rows + PAD
     planes = temp.shape[0] // rows
     minus[...], plus[...] = difference_matrices(lanes)
-    fill(start, temp, x_low.at[:side], x_high.at[:side], y_low.at[:RIM], y_high.at[:RIM], rows, pitch, 1.0)
+    fill(start, temp, x_low.part(slice(None, side)), x_high.part(slice(None, side)), y_low.part(slice(None, RIM)), y_high.part(slice(None, RIM)), rows, pitch, 1.0)
     fill(
-        spread_kappa, kappa, x_low.at[side : 2 * side], x_high.at[side : 2 * side],
-        y_low.at[RIM : 2 * RIM], y_high.at[RIM : 2 * RIM], rows, pitch, 0.5,
+        spread_kappa, kappa, x_low.part(slice(side, 2 * side)), x_high.part(slice(side, 2 * side)),
+        y_low.part(slice(RIM, 2 * RIM)), y_high.part(slice(RIM, 2 * RIM)), rows, pitch, 0.5,
     )
     blocks = planes + 2 * RIM + 1
     conduct_pass(start, spread_kappa, cond, along_z, minus, plus, 0, blocks, pitch)
-    mask = rim_mask(ends, pitch, lanes)
+    mask = rim_mask(pitch, lanes)
     for at in (0, blocks - 1):
         spread_temp[at * pitch : (at + 1) * pitch, :] = jnp.zeros((pitch, lanes), F32)
     spread_temp[blocks * pitch :, :] = jnp.zeros((spread_temp.shape[0] - blocks * pitch, lanes), F32)
@@ -167,13 +230,13 @@
     def put(block, size, value):
         value = value.reshape(size, pitch, lanes) * mask[None]
         at = pl.ds(pl.multiple_of(block * pitch, 8), size * pitch)
-        spread_temp[at, :] = value.reshape(size * pitch, lanes)
-
-    flow_pass(start, cond, along_z, 1, blocks - 2, pitch, 7, put)
+        spread_temp[at, :] = value.reshape(size * pitch, lanes) + source[at, :]
+
+    flow_pass(start, cond, along_z, 1, blocks - 2, pitch, 133, put)
 
 
 def close_kernel(
-    me, ends, got, opened, kappa, source_own, source_low, source_high,
+    got, opened, kappa, source_own, even_y, odd_y,
     temp_out, looked, source, now, then, cond, along_z, minus, plus, pieces, turned, found,
 ):
     lanes = kappa.shape[1]
@@ -184,11 +247,15 @@
     minus[...], plus[...] = difference_matrices(lanes)
     wide = RIM - 1
     source[...] = source_own[...]
+    now[...] = opened[...]
+    low, high = low_and_high("cross", even_y, odd_y)
     for r in range(wide):
-        source[pl.ds(PAD - wide + r, total, stride=pitch), :] = source_low[r, :total, :]
-        source[pl.ds(PAD + rows + r, total, stride=pitch), :] = source_high[r, :total, :]
-    now[...] = opened[...] + source[...]
-    mask = rim_mask(ends, pitch, lanes)
+        for first, beside in ((PAD - wide + r, low), (PAD + rows + r, high)):
+            at = pl.ds(first, total, stride=pitch)
+            strip = beside[r, :total, :]
+            source[at, :] = strip
+            now[at, :] = now[at, :] + strip
+    mask = rim_mask(pitch, lanes)
     conduct_pass(now, kappa, cond, along_z, minus, plus, 0, blocks, pitch)
     then[0:pitch, :] = jnp.zeros((pitch, lanes), F32)
     then[(blocks - 1) * pitch :, :] = jnp.zeros((then.shape[0] - (blocks - 1) * pitch, lanes), F32)
@@ -198,7 +265,7 @@
         value = (value + source[at, :]).reshape(size, pitch, lanes) * mask[None]
         then[at, :] = value.reshape(size * pitch, lanes)
 
-    flow_pass(now, cond, along_z, 1, blocks - 2, pitch, 7, middle)
+    flow_pass(now, cond, along_z, 1, blocks - 2, pitch, 133, middle)
     conduct_pass(then, kappa, cond, along_z, minus, plus, 0, blocks, pitch)
 
     def last(block, size, value):
@@ -211,10 +278,10 @@
         pieces[at, lanes:] = low
 
     flow_pass(then, cond, along_z, RIM, planes, pitch, 8, last)
-    lookup(me[0], got, planes * rows, lanes, looked, pieces, turned, found)
-
-
-def deposit_kernel(planes, me, got, source, down, up, spread, across, inside, beside):
+    lookup(lax.axis_index("cut"), got, planes * rows, lanes, looked, pieces, turned, found)
+
+
+def deposit_kernel(planes, got, source, even, odd, spread, across, inside, beside):
     blocks, groups, double, _ = got.shape
     half = double // 2
     lanes = source.shape[1]
@@ -222,7 +289,7 @@
     pitch = rows + PAD
     patch = planes * rows * lanes
     count = groups * half * LANES
-    here = me[0]
+    here = lax.axis_index("cut")
     place = iota((rows, LANES), 0)
     place16 = place.astype(jnp.int16)
     zero = jnp.zeros((rows, LANES), BF16)
@@ -291,9 +358,10 @@
     low = beside[:, 2 * count :] - jnp.int16(planes - wide)
     product(-wide, wide, low, slice(2 * count, 4 * count))
     planes_all = planes + 2 * RIM
+    top = (1 - is_odd("cross")) * (rows - wide)
     for r in range(wide):
-        down[r, :planes_all, :] = source[pl.ds(PAD + r, planes_all, stride=pitch), :]
-        up[r, :planes_all, :] = source[pl.ds(PAD + rows - wide + r, planes_all, stride=pitch), :]
+        for out, first in ((even, top), (odd, rows - wide - top)):
+            out[r, :planes_all, :] = source[pl.ds(PAD + first + r, planes_all, stride=pitch), :]
 
 
 def lookup(me, got, height, lanes, looked, pieces, turned, found):
@@ -347,7 +415,8 @@
     for part in range(2):
         for s in range(groups):
             for h in range(half):
-                looked[s, part * half + h : part * half + h + 1, :] = back[at : at + 1, :]
+                for block in range(blocks):
+                    looked[block, s, part * half + h : part * half + h + 1, :] = back[at : at + 1, :]
                 at += 1
 
 
@@ -363,13 +432,55 @@
     return results
 
 
+def rows_of(ref, ch):
+    return [ref[ch : ch + 1, r * LANES : (r + 1) * LANES] for r in range(ref.shape[1] // LANES)]
+
+
+def stretch_kernel(
+    side, after, pos, acted, other, gap, snapped, even_x, odd_x, base, slope, delta, hot,
+):
+    count = pos.shape[1] // LANES
+    low_ghost, high_ghost = low_and_high("cut", even_x, odd_x)
+
+    def ghosts(ref):
+        places = side + 3 * count
+        tables = [
+            [ref[side + ch * count + r : side + ch * count + r + 1, :] for r in range(count)]
+            for ch in range(3)
+        ]
+        found = pick(tables, ref[places:, :].astype(I32))
+        return [[f[r : r + 1] for r in range(f.shape[0])] for f in found]
+
+    own = [rows_of(pos, ch) for ch in range(3)]
+    low = ghosts(low_ghost)
+    high = ghosts(high_ghost)
+    first = pick(own, acted[...])
+    second = pick([own[ch] + low[ch] + high[ch] for ch in range(3)], other[...])
+    d = [second[ch] - first[ch] for ch in range(3)]
+    dist = jnp.sqrt(d[0] * d[0] + d[1] * d[1] + d[2] * d[2])
+    weight = (1.0 - snapped[...].astype(F32)) / jnp.maximum(dist, 0.3)
+    base[...] = weight * (dist - gap[...])
+    slope[...] = weight * (gap[...] * (0.2 * 0.5))
+    for ch in range(3):
+        delta[ch] = d[ch]
+    place = iota((16, LANES), 0).astype(jnp.int16)
+    one = jnp.ones((16, LANES), BF16)
+    for r in range(acted.shape[0]):
+        lane = jnp.broadcast_to(acted[r : r + 1, :] & (LANES - 1), (16, LANES)).astype(jnp.int16)
+        for t in range(LANES // 16):
+            hot[t * 16 : (t + 1) * 16, r * LANES : (r + 1) * LANES] = jnp.where(
+                lane == place + jnp.int16(t * 16), one, jnp.zeros_like(one)
+            )
+
+
 def bond_kernel(
-    me, back, pos, vel, acted, other, gap, snapped, low_pos, high_pos, low_export, high_export,
-    pos_out, vel_out, force, hot,
+    places, back, pos, vel, acted, other, even_x, odd_x, base, slope, delta, hot,
+    pos_out, vel_out, force,
 ):
     blocks, groups, double, _ = back.shape
     half = double // 2
-    here = me[0]
+    here = lax.axis_index("cut")
+    low_ghost, high_ghost = low_and_high("cut", even_x, odd_x)
 
     def block(distance):
         return lax.rem(here + (blocks + distance), blocks)
@@ -381,36 +492,21 @@
             for h in range(half)
         ]
 
-    def rows_of(ref, ch):
-        return [ref[ch : ch + 1, r * LANES : (r + 1) * LANES] for r in range(ref.shape[1] // LANES)]
-
-    def ghosts(ref, distance, export):
-        tables = [
-            [ref[ch, r : r + 1, :] for r in range(ref.shape[1])] for ch in range(3)
-        ] + [temps(distance)]
-        found = pick(tables, export[...])
-        return [[f[r : r + 1] for r in range(f.shape[0])] for f in found]
-
-    own = [rows_of(pos, ch) for ch in range(3)] + [temps(0)]
-    low = ghosts(low_pos, -1, low_export)
-    high = ghosts(high_pos, 1, high_export)
-    wide = [own[ch] + low[ch] + high[ch] for ch in range(4)]
-    first = pick(own, acted[...])
-    second = pick(wide, other[...])
-    delta = [second[ch] - first[ch] for ch in range(3)]
-    dist = jnp.sqrt(delta[0] * delta[0] + delta[1] * delta[1] + delta[2] * delta[2])
-    relaxed = gap[...] * (1.0 + 0.2 * (0.5 * (first[3] + second[3])))
-    scale = (1.0 - snapped[...].astype(F32)) * (dist - relaxed) / jnp.maximum(dist, 0.3)
-    values = [split(scale * d) for d in delta]
+    def ghosts(distance, ref):
+        found = pick([temps(distance)], ref[places:, :].astype(I32))[0]
+        return [found[r : r + 1] for r in range(found.shape[0])]
+
+    own = temps(0)
+    first = pick([own], acted[...])[0]
+    second = pick([own + ghosts(-1, low_ghost) + ghosts(1, high_ghost)], other[...])[0]
+    scale = base[...] - slope[...] * (first + second)
+    values = [split(scale * delta[ch]) for ch in range(3)]
     values = [piece.astype(F32) for pair in values for piece in pair]
-    high_count = len(own[0])
-    place = iota((LANES, LANES), 0)
+    high_count = len(own)
     high_place = iota((high_count, LANES), 0)
     for r in range(acted.shape[0]):
-        index = acted[r : r + 1, :]
         span = slice(r * LANES, (r + 1) * LANES)
-        hot[:, span] = jnp.where(place == (index & (LANES - 1)), 1.0, 0.0).astype(BF16)
-        at_row = lax.shift_right_logical(index, 7) == high_place
+        at_row = lax.shift_right_logical(acted[r : r + 1, :], 7) == high_place
         for n, value in enumerate(values):
             force[n * high_count : (n + 1) * high_count, span] = jnp.where(
                 at_row, jnp.broadcast_to(value[r : r + 1], (high_count, LANES)), 0.0
@@ -419,8 +515,11 @@
         force[...], hot[...], (((1,), (1,)), ((), ())), preferred_element_type=F32
     )
     for ch in range(3):
-        base = 2 * ch * high_count
-        summed = total[base : base + high_count] + total[base + high_count : base + 2 * high_count]
+        base_row = 2 * ch * high_count
+        summed = (
+            total[base_row : base_row + high_count]
+            + total[base_row + high_count : base_row + 2 * high_count]
+        )
         for r in range(high_count):
             span = slice(r * LANES, (r + 1) * LANES)
             velocity = vel[ch : ch + 1, span] + 0.5 * summed[r : r + 1]
@@ -428,15 +527,15 @@
             pos_out[ch : ch + 1, span] = pos[ch : ch + 1, span] + 0.5 * velocity
 
 
-def ring(block, distance):
-    count = lax.axis_size("cut")
-    return lax.ppermute(block, "cut", [(i, (i + distance) % count) for i in range(count)])
-
-
-def line(block, distance):
-    count = lax.axis_size("cross")
-    pairs = [(i, i + distance) for i in range(count) if 0 <= i + distance < count]
-    return lax.ppermute(block, "cross", pairs)
+def swaps(axis, closed, even, odd):
+    count = lax.axis_size(axis)
+    results = []
+    for first, block in ((0, even), (1, odd)):
+        pairs = []
+        for i in range(first, count if closed else count - 1, 2):
+            pairs += [(i, (i + 1) % count), ((i + 1) % count, i)]
+        results.append(lax.ppermute(block, axis, pairs))
+    return results
 
 
 def per_device(
@@ -460,64 +559,62 @@
     groups = lax.axis_size("cross")
     count = patch_locator.shape[0]
     half = count // groups // LANES
-    me = lax.axis_index("cut").reshape(1).astype(I32)
-    side = lax.axis_index("cross")
-    ends = jnp.stack([side > 0, side < groups - 1]).astype(I32)
     pitch = rows + PAD
     total = planes + 2 * RIM
     flat = jax.ShapeDtypeStruct(((total + 2) * pitch, lanes), F32)
     wide = RIM * rows
 
-    ghost = jnp.concatenate(
+    exports = exported_copies.shape[0] // LANES
+    places = 2 * wide + grain_placements.size // LANES
+    carried = jax.ShapeDtypeStruct((places + exports, LANES), F32)
+    parcel = jax.ShapeDtypeStruct((blocks, groups, 2 * half, LANES), F32)
+    sent, even_x, odd_x = call(
+        parcel_kernel,
+        [parcel, carried, carried],
         [
-            grain_placements.reshape(-1, LANES),
-            exported_copies.astype(F32).reshape(-1, LANES),
+            temp,
+            kappa,
+            patch_locator.reshape(-1, LANES),
+            photon_gain_wattage.reshape(-1, LANES),
+            on_skin_marker.reshape(-1, LANES),
+            grain_placements,
+            exported_copies.reshape(-1, LANES),
         ],
-        axis=0,
-    )
-    place_rows = grain_placements.size // LANES
-    height = planes * rows
-    low = ring(jnp.concatenate([temp[height - wide :], kappa[height - wide :], ghost], axis=0), 1)
-    high = ring(jnp.concatenate([temp[:wide], kappa[:wide], ghost], axis=0), -1)
-
-    def neighbour(block):
-        ghost = block[2 * wide :]
-        return (
-            block[: 2 * wide],
-            ghost[:place_rows].reshape(3, -1, LANES),
-            ghost[place_rows:].astype(I32),
-        )
-
-    x_low, low_pos, low_export = neighbour(low)
-    x_high, high_pos, high_export = neighbour(high)
-
-    power = on_skin_marker.astype(F32) * photon_gain_wattage * 0.5
-    parcel = jnp.concatenate(
         [
-            patch_locator.astype(F32).reshape(groups, half, LANES),
-            power.reshape(groups, half, LANES),
+            pltpu.VMEM((count // LANES, LANES), I32),
+            pltpu.VMEM((count // LANES, LANES), F32),
+            pltpu.VMEM((count // LANES, LANES), I32),
+            pltpu.VMEM(grain_placements.shape, F32),
+            pltpu.VMEM((exports, LANES), I32),
+            pltpu.SemaphoreType.DMA((9,)),
         ],
-        axis=1,
-    )
-
-    def exchange(parcel):
-        sent = jnp.broadcast_to(parcel[None], (blocks,) + parcel.shape)
-        sent = sent.reshape((blocks * groups,) + parcel.shape[1:])
-        got = lax.all_to_all(sent, BOTH, split_axis=0, concat_axis=0, tiled=True)
-        return got.reshape((blocks, groups) + parcel.shape[1:])
-
-    got = exchange(parcel)
+        left=7,
+        limit=None,
+    )
+
+    def exchange(sent):
+        flat = sent.reshape((blocks * groups,) + sent.shape[2:])
+        got = lax.all_to_all(flat, BOTH, split_axis=0, concat_axis=0, tiled=True)
+        return got.reshape(sent.shape)
+
+    got = exchange(sent)
+    even_x, odd_x = swaps("cut", True, even_x, odd_x)
 
     across = jax.ShapeDtypeStruct((2 * RIM, -(-total // 8) * 8, lanes), F32)
-    down, up = call(rows_kernel, [across, across], [temp, kappa, x_low, x_high], smem=0)
-    y_low, y_high = line(up, 1), line(down, -1)
+    even_y, odd_y = call(
+        functools.partial(rows_kernel, rows),
+        [across, across],
+        [got, temp, kappa, even_x, odd_x],
+        left=1,
+    )
+    even_y, odd_y = swaps("cross", False, even_y, odd_y)
 
     strips = jax.ShapeDtypeStruct((RIM - 1,) + across.shape[1:], F32)
     entries = count
-    source, down, up = call(
+    source, even_s, odd_s = call(
         functools.partial(deposit_kernel, planes),
         [flat, strips, strips],
-        [me, got],
+        [got],
         [
             pltpu.VMEM((2 * lanes, 4 * entries), BF16),
             pltpu.VMEM((rows, 4 * entries), BF16),
@@ -525,55 +622,63 @@
             pltpu.VMEM((rows, 4 * entries), jnp.int16),
         ],
     )
-    source_low, source_high = line(up, 1), line(down, -1)
+    even_s, odd_s = swaps("cross", False, even_s, odd_s)
 
     grid = pltpu.VMEM(flat.shape, F32)
     matrix = pltpu.VMEM((2 * lanes, 2 * lanes), BF16)
     opened, kappa = call(
-        open_kernel,
+        functools.partial(open_kernel, rows),
         [flat, flat],
-        [ends, temp, kappa, x_low, x_high, y_low, y_high],
+        [temp, kappa, source, even_x, odd_x, even_y, odd_y],
         [grid, grid, grid, matrix, matrix],
     )
     temp, looked = call(
         close_kernel,
         [
             jax.ShapeDtypeStruct((planes, rows, lanes), F32),
-            jax.ShapeDtypeStruct((groups, 2 * half, LANES), F32),
+            parcel,
         ],
-        [me, ends, got, opened, kappa, source, source_low, source_high],
+        [got, opened, kappa, source, even_s, odd_s],
         [
             grid, grid, grid, grid, grid, matrix, matrix,
             pltpu.VMEM((planes * rows, 2 * lanes), BF16),
             pltpu.VMEM((LANES, LANES), I32),
             pltpu.VMEM((LANES, LANES), F32),
         ],
-        smem=2,
     )
     back = exchange(looked)
-    bonds = tether_acted_grain.shape[0]
+    acted = tether_acted_grain.reshape(-1, LANES)
+    other = tether_other_grain.reshape(-1, LANES)
+    entry = jax.ShapeDtypeStruct(acted.shape, F32)
+    base, slope, delta, hot = call(
+        functools.partial(stretch_kernel, 2 * wide),
+        [
+            entry,
+            entry,
+            jax.ShapeDtypeStruct((3,) + acted.shape, F32),
+            jax.ShapeDtypeStruct((LANES, acted.size), BF16),
+        ],
+        [
+            looked,
+            grain_placements,
+            acted,
+            other,
+            tether_relaxed_gap.reshape(-1, LANES),
+            snapped_marker.reshape(-1, LANES),
+            even_x,
+            odd_x,
+        ],
+        left=1,
+    )
     out = jax.ShapeDtypeStruct(grain_placements.shape, F32)
     positions_new, velocities_new = call(
-        bond_kernel,
+        functools.partial(bond_kernel, places),
         [out, out],
         [
-            me,
-            back,
-            grain_placements,
-            grain_motion_parts,
-            tether_acted_grain.reshape(-1, LANES),
-            tether_other_grain.reshape(-1, LANES),
-            tether_relaxed_gap.reshape(-1, LANES),
-            snapped_marker.reshape(-1, LANES),
-            low_pos,
-            high_pos,
-            low_export,
-            high_export,
+            back, grain_placements, grain_motion_parts, acted, other, even_x, odd_x,
+            base, slope, delta, hot,
         ],
-        [
-            pltpu.VMEM((6 * (count // LANES), bonds), BF16),
-            pltpu.VMEM((LANES, bonds), BF16),
-        ],
+        [pltpu.VMEM((6 * (count // LANES), acted.size), BF16)],
     )
     return (temp, positions_new, velocities_new)
 

time: 88.7 us -> 61.1 us (0.69)
  waiting for transfers between devices: 19.3 us -> 8.93 us
  Pallas kernels: 36.8 us -> 27.4 us
  local copies, waits for them, and re-layouts: 7.5 us -> 0.05 us
  other arithmetic: 2.21 us -> 0 us
  starting transfers between devices: 21.4 us -> 23.6 us
    all_to_all x2, waiting for transfers between devices: 14.5 us -> 4.02 us  [exchange(): got = lax.all_to_all(flat, BOTH, split_axis=0, concat_axis=0, tiled=True)]
    pallas_call x5 -> x7, Pallas kernels: 36.8 us -> 27.4 us  [call(): pl.pallas_call(kernel, out_shape=outs, in_specs=[pl.BlockSpec(memory_spac...]
    all_to_all x2, starting transfers between devices: 10.4 us -> 15 us  [exchange(): got = lax.all_to_all(flat, BOTH, split_axis=0, concat_axis=0, tiled=True)]
    unnamed x22 -> x16, local copies, waits for them, and re-layouts: 3.92 us -> 0.05 us
    ppermute x6, starting transfers between devices: 11 us -> 8.67 us  [swaps(): results.append(lax.ppermute(block, axis, pairs))]
    slice x6 -> x0, local copies, waits for them, and re-layouts: 1.53 us -> none  [the longest x2 1.52 us: per_device(): high = ring(jnp.concatenate([temp[:wide], kappa[:wide], ghost], axis=0), -1)]
    broadcast_in_dim x2 -> x0, local copies, waits for them, and re-layouts: 1.26 us -> none  [exchange(): sent = jnp.broadcast_to(parcel[None], (blocks,) + parcel.shape)]
  transfers between devices with their start and end apart: 8 -> 8, of which waited for: 4 -> 3; matrix products, arithmetic and copies ran while one was open for 2% -> 0% of each run, Pallas kernels for 17% -> 22%
where the time goes in v3:
time: 61.1 us; the launch traced here: 60.9 us
  Pallas kernels  27.4 us (45%)
  starting transfers between devices  23.6 us (39%)
  waiting for transfers between devices  8.93 us (15%)
  between operations  0.85 us (1%)
    pallas_call x7, Pallas kernels, call(): pl.pallas_call(kernel, out_shape=outs, in_specs=[pl.BlockSpec(memory_spac...  27.4 us
    all_to_all x2, starting transfers between devices, exchange(): got = lax.all_to_all(flat, BOTH, split_axis=0, concat_axis=0, tiled=True)  15 us
    ppermute x6, starting transfers between devices, swaps(): results.append(lax.ppermute(block, axis, pairs))  8.67 us
    ppermute x6, waiting for transfers between devices, swaps(): results.append(lax.ppermute(block, axis, pairs))  4.91 us
    all_to_all x2, waiting for transfers between devices, exchange(): got = lax.all_to_all(flat, BOTH, split_axis=0, concat_axis=0, tiled=True)  4.02 us
  transfers between devices with their start and end apart: 8, of which 3 were waited for; matrix products, arithmetic and copies ran while one was open for 0% of the time, Pallas kernels for 22%

profile of v3, /device:TPU:0, one launch (start us, length us, event | category | flops | bytes accessed | tf_op | source)
XLA Modules:
  0.0 60.9 jit_solution(12276938608287852750)
XLA Ops:
  0.6 0.0 copy-start.1
  0.6 0.0 copy-start
  0.7 1.7 %shard_map.139 = (f32[4,8,4,128]{3,2,1,0:T(4,128)}, f32[146,128]{1,0:T(8,128)}, f32[146,128]{1,0:T(8,128)}) custom-call(f32[2048,128]{1,0:T(8,128)} %bitcast.14, f32[2048,128]{1,0:T(8,128)} %bitcast.17, s32[16,128]{1,0:T(8,128)} %bitcast.31, f32[16,128]{1,0:T(8,128)} %bitcast.32, s32[16,128]{1,0:T(8,128)} %bitcast.33, f32[3,2048]{1,0:T(4,128)} %pos.5, ...), custom_call_target="tpu_custom_call" | custom-call | tf_op jit(solution)/shard_map/pallas_call | solution.py:20
  2.4 7.3 %all-to-all-start = ((f32[32,4,128]{2,1,0:T(4,128)}), f32[32,4,128]{2,1,0:T(4,128)S(1)}, u32[]{:S(2)}, u32[]{:S(2)}) async-start(f32[32,4,128]{2,1,0:T(4,128)} %bitcast.30), calls=%async_computation | async-start | bytes 131072 | tf_op jit(solution)/shard_map/all_to_all | solution.py:597
  9.7 1.8 %collective-permute-start = (f32[146,128]{1,0:T(8,128)}, f32[146,128]{1,0:T(8,128)S(1)}, u32[]{:S(2)}, u32[]{:S(2)}) collective-permute-start(f32[146,128]{1,0:T(8,128)} %get-tuple-element.23), channel_id=1, source_target_pairs={{0,8},{8,0},{16,24},{24,16},{1,9},{9,1},{17,25},{25,17},{2,10},{10... | collective-permute-start | bytes 224264 | tf_op jit(solution)/shard_map/ppermute | solution.py:537
  11.6 2.4 %collective-permute-start.1 = (f32[146,128]{1,0:T(8,128)}, f32[146,128]{1,0:T(8,128)S(1)}, u32[]{:S(2)}, u32[]{:S(2)}) collective-permute-start(f32[146,128]{1,0:T(8,128)} %get-tuple-element.24), channel_id=1, source_target_pairs={{8,16},{16,8},{24,0},{0,24},{9,17},{17,9},{25,1},{1,25},{10,18},{1... | collective-permute-start | bytes 224264 | tf_op jit(solution)/shard_map/ppermute | solution.py:537
  13.9 1.4 %collective-permute-done.even_x = f32[146,128]{1,0:T(8,128)S(1)} collective-permute-done((f32[146,128]{1,0:T(8,128)}, f32[146,128]{1,0:T(8,128)S(1)}, u32[]{:S(2)}, u32[]{:S(2)}) %collective-permute-start) | collective-permute-done | bytes 74784 | tf_op jit(solution)/shard_map/ppermute | solution.py:537
  15.3 3.5 %collective-permute-done.1.odd_x = f32[146,128]{1,0:T(8,128)S(1)} collective-permute-done((f32[146,128]{1,0:T(8,128)}, f32[146,128]{1,0:T(8,128)S(1)}, u32[]{:S(2)}, u32[]{:S(2)}) %collective-permute-start.1) | collective-permute-done | bytes 74784 | tf_op jit(solution)/shard_map/ppermute | solution.py:537
  18.8 0.0 all-to-all-done
  18.8 0.0 copy-done.1
  18.8 0.0 copy-done
  18.8 0.4 shard_map.141
  19.2 0.1 collective-permute-start.2
  19.3 0.7 %collective-permute-start.3 = (f32[6,136,128]{2,1,0:T(8,128)S(1)}, f32[6,136,128]{2,1,0:T(8,128)S(1)}, u32[]{:S(2)}, u32[]{:S(2)}) collective-permute-start(f32[6,136,128]{2,1,0:T(8,128)S(1)} %get-tuple-element.26), channel_id=1, source_target_pairs={{1,2},{2,1},{3,4},{4,3},{5,6},{6,5},{9,10},{10,9},{11,12},{12,11},... | collective-permute-start | bytes 1253384 | tf_op jit(solution)/shard_map/ppermute | solution.py:537
  20.0 8.1 %shard_map.140 = (f32[3264,128]{1,0:T(8,128)S(1)}, f32[2,136,128]{2,1,0:T(8,128)S(1)}, f32[2,136,128]{2,1,0:T(8,128)S(1)}) custom-call(f32[4,8,4,128]{3,2,1,0:T(4,128)S(1)} %bitcast.21), custom_call_target="tpu_custom_call" | custom-call | tf_op jit(solution)/shard_map/pallas_call | solution.py:20
  28.1 2.9 %collective-permute-start.4 = (f32[2,136,128]{2,1,0:T(8,128)S(1)}, f32[2,136,128]{2,1,0:T(8,128)S(1)}, u32[]{:S(2)}, u32[]{:S(2)}) collective-permute-start(f32[2,136,128]{2,1,0:T(8,128)S(1)} %get-tuple-element.29), channel_id=1, source_target_pairs={{0,1},{1,0},{2,3},{3,2},{4,5},{5,4},{6,7},{7,6},{8,9},{9,8},{10,11... | collective-permute-start | bytes 417800 | tf_op jit(solution)/shard_map/ppermute | solution.py:537
  30.9 0.8 %collective-permute-start.5 = (f32[2,136,128]{2,1,0:T(8,128)S(1)}, f32[2,136,128]{2,1,0:T(8,128)S(1)}, u32[]{:S(2)}, u32[]{:S(2)}) collective-permute-start(f32[2,136,128]{2,1,0:T(8,128)S(1)} %get-tuple-element.30), channel_id=1, source_target_pairs={{1,2},{2,1},{3,4},{4,3},{5,6},{6,5},{9,10},{10,9},{11,12},{12,11},... | collective-permute-start | bytes 417800 | tf_op jit(solution)/shard_map/ppermute | solution.py:537
  31.8 0.0 collective-permute-done.2.even_y
  31.8 0.0 collective-permute-done.3.odd_y
  31.8 2.5 %shard_map.142 = (f32[3264,128]{1,0:T(8,128)S(1)}, f32[3264,128]{1,0:T(8,128)S(1)}) custom-call(f32[2048,128]{1,0:T(8,128)S(1)} %bitcast.16, f32[2048,128]{1,0:T(8,128)S(1)} %bitcast.19, f32[3264,128]{1,0:T(8,128)S(1)} %get-tuple-element.22.source.source_own, f32[146,128]{1,0:T(8,128)S(1)} %collective-permute-done.even_x, ...), custom_call_target="tpu_custom_call" | custom-call | tf_op jit(solution)/shard_map/pallas_call | solution.py:20
  34.3 0.0 collective-permute-done.4.even_y
  34.3 0.0 collective-permute-done.5.odd_y
  34.3 0.0 copy-start.2
  34.3 0.0 copy-start.3
  34.3 0.0 copy-start.4
  34.4 0.0 copy-start.6
  34.4 0.0 copy-start.7
  34.4 0.0 copy-start.5
  34.4 9.6 %shard_map.143 = (f32[128,16,128]{2,1,0:T(8,128)}, f32[4,8,4,128]{3,2,1,0:T(4,128)}) custom-call(f32[4,8,4,128]{3,2,1,0:T(4,128)S(1)} %bitcast.22, f32[3264,128]{1,0:T(8,128)S(1)} %get-tuple-element.27.opened, f32[3264,128]{1,0:T(8,128)S(1)} %get-tuple-element.28.kappa, f32[3264,128]{1,0:T(8,128)S(1)} %get-tuple-element.22.source.source_own, ...), custom_call_target="tpu_custom_call" | custom-call | tf_op jit(solution)/shard_map/pallas_call | solution.py:20
  44.0 7.7 %all-to-all-start.1 = ((f32[32,4,128]{2,1,0:T(4,128)}), f32[32,4,128]{2,1,0:T(4,128)S(1)}, u32[]{:S(2)}, u32[]{:S(2)}) async-start(f32[32,4,128]{2,1,0:T(4,128)} %bitcast.8), calls=%async_computation.1 | async-start | bytes 131072 | tf_op jit(solution)/shard_map/all_to_all | solution.py:597
  51.6 0.0 copy-done.2
  51.7 0.0 copy-done.3
  51.7 0.0 copy-done.4
  51.7 0.0 copy-done.6
  51.7 0.0 copy-done.7
  51.7 3.1 %shard_map.144 = (f32[64,128]{1,0:T(8,128)S(1)}, f32[64,128]{1,0:T(8,128)S(1)}, f32[3,64,128]{2,1,0:T(8,128)S(1)}, bf16[128,8192]{1,0:T(8,128)(2,1)S(1)}) custom-call(f32[4,8,4,128]{3,2,1,0:T(4,128)} %get-tuple-element.32.after, f32[3,2048]{1,0:T(4,128)S(1)} %copy-done.2, s32[64,128]{1,0:T(8,128)S(1)} %bitcast.24, s32[64,128]{1,0:T(8,128)S(1)} %bitcast.26, ...), custom_call_target="tpu_custom_call" | custom-call | tf_op jit(solution)/shard_map/pallas_call | solution.py:20
  54.8 4.0 %all-to-all-done.1 = f32[32,4,128]{2,1,0:T(4,128)S(1)} async-done(((f32[32,4,128]{2,1,0:T(4,128)}), f32[32,4,128]{2,1,0:T(4,128)S(1)}, u32[]{:S(2)}, u32[]{:S(2)}) %all-to-all-start.1) | async-done | bytes 65568 | tf_op jit(solution)/shard_map/all_to_all | solution.py:597
  58.8 0.0 copy-done.5
  58.8 2.0 %shard_map.145 = (f32[3,2048]{1,0:T(4,128)}, f32[3,2048]{1,0:T(4,128)}) custom-call(f32[4,8,4,128]{3,2,1,0:T(4,128)S(1)} %bitcast.23, f32[3,2048]{1,0:T(4,128)S(1)} %copy-done.2, f32[3,2048]{1,0:T(4,128)S(1)} %copy-done.5, s32[64,128]{1,0:T(8,128)S(1)} %bitcast.25, s32[64,128]{1,0:T(8,128)S(1)} %bitcast.27, f32[146,128]{1,0:T(8,128)S(1)} %collective-permute-done.even_x, ...), custom_call_target="tpu_custom_call" | custom-call | tf_op jit(solution)/shard_map/pallas_call | solution.py:20
Async XLA Ops:
  0.6 18.2 %copy-start.1 = (f32[128,16,128]{2,1,0:T(8,128)S(1)}, f32[128,16,128]{2,1,0:T(8,128)}, u32[]{:S(2)}) copy-start(f32[128,16,128]{2,1,0:T(8,128)} %param.13) | copy-start | bytes 3145732
  0.6 18.2 %copy-start = (f32[128,16,128]{2,1,0:T(8,128)S(1)}, f32[128,16,128]{2,1,0:T(8,128)}, u32[]{:S(2)}) copy-start(f32[128,16,128]{2,1,0:T(8,128)} %param.12) | copy-start | bytes 3145732
  2.4 16.4 %all-to-all-start = ((f32[32,4,128]{2,1,0:T(4,128)}), f32[32,4,128]{2,1,0:T(4,128)S(1)}, u32[]{:S(2)}, u32[]{:S(2)}) async-start(f32[32,4,128]{2,1,0:T(4,128)} %bitcast.30), calls=%async_computation | async-start | bytes 131072 | tf_op jit(solution)/shard_map/all_to_all | solution.py:597
  9.7 5.6 %collective-permute-start = (f32[146,128]{1,0:T(8,128)}, f32[146,128]{1,0:T(8,128)S(1)}, u32[]{:S(2)}, u32[]{:S(2)}) collective-permute-start(f32[146,128]{1,0:T(8,128)} %get-tuple-element.23), channel_id=1, source_target_pairs={{0,8},{8,0},{16,24},{24,16},{1,9},{9,1},{17,25},{25,17},{2,10},{10... | collective-permute-start | bytes 224264 | tf_op jit(solution)/shard_map/ppermute | solution.py:537
  11.6 7.3 %collective-permute-start.1 = (f32[146,128]{1,0:T(8,128)}, f32[146,128]{1,0:T(8,128)S(1)}, u32[]{:S(2)}, u32[]{:S(2)}) collective-permute-start(f32[146,128]{1,0:T(8,128)} %get-tuple-element.24), channel_id=1, source_target_pairs={{8,16},{16,8},{24,0},{0,24},{9,17},{17,9},{25,1},{1,25},{10,18},{1... | collective-permute-start | bytes 224264 | tf_op jit(solution)/shard_map/ppermute | solution.py:537
  19.2 12.6 %collective-permute-start.2 = (f32[6,136,128]{2,1,0:T(8,128)S(1)}, f32[6,136,128]{2,1,0:T(8,128)S(1)}, u32[]{:S(2)}, u32[]{:S(2)}) collective-permute-start(f32[6,136,128]{2,1,0:T(8,128)S(1)} %get-tuple-element.25), channel_id=1, source_target_pairs={{0,1},{1,0},{2,3},{3,2},{4,5},{5,4},{6,7},{7,6},{8,9},{9,8},{10,11... | collective-permute-start | bytes 1253384 | tf_op jit(solution)/shard_map/ppermute | solution.py:537
  19.3 12.5 %collective-permute-start.3 = (f32[6,136,128]{2,1,0:T(8,128)S(1)}, f32[6,136,128]{2,1,0:T(8,128)S(1)}, u32[]{:S(2)}, u32[]{:S(2)}) collective-permute-start(f32[6,136,128]{2,1,0:T(8,128)S(1)} %get-tuple-element.26), channel_id=1, source_target_pairs={{1,2},{2,1},{3,4},{4,3},{5,6},{6,5},{9,10},{10,9},{11,12},{12,11},... | collective-permute-start | bytes 1253384 | tf_op jit(solution)/shard_map/ppermute | solution.py:537
  28.1 6.2 %collective-permute-start.4 = (f32[2,136,128]{2,1,0:T(8,128)S(1)}, f32[2,136,128]{2,1,0:T(8,128)S(1)}, u32[]{:S(2)}, u32[]{:S(2)}) collective-permute-start(f32[2,136,128]{2,1,0:T(8,128)S(1)} %get-tuple-element.29), channel_id=1, source_target_pairs={{0,1},{1,0},{2,3},{3,2},{4,5},{5,4},{6,7},{7,6},{8,9},{9,8},{10,11... | collective-permute-start | bytes 417800 | tf_op jit(solution)/shard_map/ppermute | solution.py:537
  30.9 3.4 %collective-permute-start.5 = (f32[2,136,128]{2,1,0:T(8,128)S(1)}, f32[2,136,128]{2,1,0:T(8,128)S(1)}, u32[]{:S(2)}, u32[]{:S(2)}) collective-permute-start(f32[2,136,128]{2,1,0:T(8,128)S(1)} %get-tuple-element.30), channel_id=1, source_target_pairs={{1,2},{2,1},{3,4},{4,3},{5,6},{6,5},{9,10},{10,9},{11,12},{12,11},... | collective-permute-start | bytes 417800 | tf_op jit(solution)/shard_map/ppermute | solution.py:537
  34.3 17.3 %copy-start.2 = (f32[3,2048]{1,0:T(4,128)S(1)}, f32[3,2048]{1,0:T(4,128)}, u32[]{:S(2)}) copy-start(f32[3,2048]{1,0:T(4,128)} %pos.5) | copy-start | bytes 73732
  34.3 17.3 %copy-start.3 = (s32[8192]{0:T(1024)S(1)}, s32[8192]{0:T(1024)}, u32[]{:S(2)}) copy-start(s32[8192]{0:T(1024)} %param.19) | copy-start | bytes 98308
  34.3 17.3 %copy-start.4 = (s32[8192]{0:T(1024)S(1)}, s32[8192]{0:T(1024)}, u32[]{:S(2)}) copy-start(s32[8192]{0:T(1024)} %param.20) | copy-start | bytes 98308
  34.4 17.3 %copy-start.6 = (f32[8192]{0:T(1024)S(1)}, f32[8192]{0:T(1024)}, u32[]{:S(2)}) copy-start(f32[8192]{0:T(1024)} %param.21) | copy-start | bytes 98308
  34.4 17.3 %copy-start.7 = (s32[8192]{0:T(1024)S(1)}, s32[8192]{0:T(1024)}, u32[]{:S(2)}) copy-start(s32[8192]{0:T(1024)} %param.22) | copy-start | bytes 98308
  34.4 24.4 %copy-start.5 = (f32[3,2048]{1,0:T(4,128)S(1)}, f32[3,2048]{1,0:T(4,128)}, u32[]{:S(2)}) copy-start(f32[3,2048]{1,0:T(4,128)} %vel.1) | copy-start | bytes 73732
  44.0 14.9 %all-to-all-start.1 = ((f32[32,4,128]{2,1,0:T(4,128)}), f32[32,4,128]{2,1,0:T(4,128)S(1)}, u32[]{:S(2)}, u32[]{:S(2)}) async-start(f32[32,4,128]{2,1,0:T(4,128)} %bitcast.8), calls=%async_computation.1 | async-start | bytes 131072 | tf_op jit(solution)/shard_map/all_to_all | solution.py:597

commit v4 on v3

--- a/solution.py
+++ b/solution.py
@@ -60,6 +60,7 @@
 
 RIM = 3
 PAD = 8
+QUARTERS = 4
 
 
 def groups_of(count, most):
@@ -150,13 +151,17 @@
 
 
 def parcel_kernel(
-    temp, kappa, cells, watts, marks, pos, export, sent, even, odd,
+    temp, kappa, cells, watts, marks, pos, export, sent, even, odd, code,
     cell_in, watt_in, mark_in, pos_in, export_in, sems,
 ):
     count = pos.shape[1] // LANES
     exports = export.shape[0]
-    wide = (even.shape[0] - 3 * count - exports) // 2
-    height = temp.shape[0]
+    wide = (even.shape[0] - 4 * count - exports) // 2
+    height, lanes = temp.shape
+    patch = height * lanes
+    half, groups, _ = code.shape
+    cap = half * LANES
+    quarter = cap // QUARTERS
     moves = [(cells, cell_in), (watts, watt_in), (marks, mark_in), (pos, pos_in), (export, export_in)]
     tail = (1 - is_odd("cut")) * (height - wide)
     for n, field in enumerate((temp, kappa)):
@@ -168,14 +173,72 @@
         copy.start()
     for copy in copies[:3]:
         copy.wait()
-    power = mark_in[...].astype(F32) * watt_in[...] * 0.5
-    cell = cell_in[...].astype(F32)
-    blocks, groups, double, _ = sent.shape
-    half = double // 2
-    for block in range(blocks):
-        for s in range(groups):
-            sent[block, s, :half, :] = cell[s * half : (s + 1) * half]
-            sent[block, s, half:, :] = power[s * half : (s + 1) * half]
+
+    def by_group(ref):
+        return jnp.concatenate([ref[pl.ds(h, groups, stride=half), :] for h in range(half)], axis=1)
+
+    cell = by_group(cell_in)
+    power = by_group(mark_in).astype(F32) * by_group(watt_in) * 0.5
+    upper = cell >= patch
+    cell = jnp.where(upper, cell - patch, cell)
+    share = cell // (patch // QUARTERS)
+    kind = jnp.where(upper, share + QUARTERS, share)
+    members = [jnp.where(kind == k, 1.0, 0.0) for k in range(2 * QUARTERS)]
+    earlier = jnp.where(iota((cap, cap), 0) < iota((cap, cap), 1), 1.0, 0.0).astype(BF16)
+    before = jnp.dot(
+        jnp.concatenate(members, axis=0).astype(BF16), earlier, preferred_element_type=F32
+    )
+    rank = jnp.zeros((groups, cap), F32)
+    most = jnp.zeros((groups, 1), F32)
+    for k, member in enumerate(members):
+        ahead = before[k * groups : (k + 1) * groups]
+        rank = rank + member * ahead
+        most = jnp.maximum(most, ahead[:, cap - 1 :] + member[:, cap - 1 :])
+    fits = jnp.broadcast_to(most, (groups, cap)) <= quarter
+    region = share ^ is_odd("cross")
+    slot = jnp.where(fits, region * quarter + rank.astype(I32), iota((groups, cap), 1))
+    mark = jnp.where(upper, slot + cap, slot)
+    for h in range(half):
+        code[h] = mark[:, h * LANES : (h + 1) * LANES]
+    number = cell + 1
+    digits = [number & 255, lax.shift_right_logical(number, 8) & 255, lax.shift_right_logical(number, 16)]
+    digits = [d.astype(F32) for d in digits]
+    top = power.astype(BF16).astype(F32)
+    middle = (power - top).astype(BF16).astype(F32)
+    digits += [top, middle, power - top - middle]
+    stacked = [jnp.where(upper, 0.0, d) for d in digits] + [jnp.where(upper, d, 0.0) for d in digits]
+    stacked = jnp.concatenate(stacked, axis=0).astype(BF16)
+    place = iota((16, cap), 0).astype(jnp.int16)
+    one = jnp.ones((16, cap), BF16)
+    of_group = iota((stacked.shape[0], cap), 0) & (groups - 1)
+    moved = jnp.zeros(stacked.shape, F32)
+    for j in range(groups):
+        goes = jnp.broadcast_to(slot[j : j + 1], (16, cap)).astype(jnp.int16)
+        swap = jnp.concatenate(
+            [
+                jnp.where(goes == place + jnp.int16(t * 16), one, jnp.zeros_like(one))
+                for t in range(cap // 16)
+            ],
+            axis=0,
+        )
+        result = lax.dot_general(
+            stacked, swap, (((1,), (1,)), ((), ())), preferred_element_type=F32
+        )
+        moved = jnp.where(of_group == j, result, moved)
+    sign = jnp.where(fits, 1.0, -1.0)
+    blocks = sent.shape[0] // (groups * 4 * half)
+    for kind in range(2):
+        part = [
+            moved[(6 * kind + n) * groups : (6 * kind + n + 1) * groups] for n in range(6)
+        ]
+        numbers = (part[0] + 256.0 * part[1] + 65536.0 * part[2]) * sign
+        powers = part[3] + part[4] + part[5]
+        for n, value in enumerate((numbers, powers)):
+            for h in range(half):
+                row = kind * 2 * half + n * half + h
+                for block in range(blocks):
+                    at = pl.ds(block * groups * 4 * half + row, groups, stride=4 * half)
+                    sent[at, :] = value[:, h * LANES : (h + 1) * LANES]
     for copy in copies[3:5]:
         copy.wait()
     for out in (even, odd):
@@ -183,7 +246,10 @@
             for r in range(count):
                 at = 2 * wide + ch * count + r
                 out[at : at + 1, :] = pos_in[ch : ch + 1, r * LANES : (r + 1) * LANES]
-        out[2 * wide + 3 * count :, :] = export_in[...].astype(F32)
+        at = 2 * wide + 3 * count
+        for h in range(half):
+            out[pl.ds(at + h, groups, stride=half), :] = code[h].astype(F32)
+        out[at + count :, :] = export_in[...].astype(F32)
     for copy in copies[5:]:
         copy.wait()
 
@@ -281,82 +347,119 @@
     lookup(lax.axis_index("cut"), got, planes * rows, lanes, looked, pieces, turned, found)
 
 
-def deposit_kernel(planes, got, source, even, odd, spread, across, inside, beside):
-    blocks, groups, double, _ = got.shape
-    half = double // 2
+def paired(got, block, kind, row, s):
+    at = kind * (got.shape[2] // 2) + row
+    first = got[block, s, pl.ds(at, 1), :]
+    second = got[block, s + 1, pl.ds(at, 1), :]
+    left = iota((1, LANES), 1) < LANES // 2
+    return jnp.where(left, first, second), jnp.where(left, second, first)
+
+
+def cell_of(number):
+    return jnp.abs(number).astype(I32) - 1
+
+
+def unsorted(got):
+    half = got.shape[2] // 4
+    lowest = jnp.minimum(got[:, :, :half, :], got[:, :, 2 * half : 3 * half, :])
+    return jnp.min(lowest) < 0.0
+
+
+def deposit_kernel(planes, got, source, even, odd, spread, across, plane_of):
+    blocks, groups, rows_sent, _ = got.shape
+    half = rows_sent // 4
     lanes = source.shape[1]
     rows = across.shape[0]
     pitch = rows + PAD
-    patch = planes * rows * lanes
-    count = groups * half * LANES
     here = lax.axis_index("cut")
     place = iota((rows, LANES), 0)
     place16 = place.astype(jnp.int16)
     zero = jnp.zeros((rows, LANES), BF16)
-    order = (1, 0, blocks - 1, blocks - 2)
-
-    for part, distance in enumerate(order):
-        block = lax.rem(here + distance, blocks)
-
-        def body(s, unused, part=part, block=block):
+    pairs = groups // 2
+    tile = planes // QUARTERS
+    region = 2 * pairs * LANES
+    inside = QUARTERS * region
+    wide = RIM - 1
+
+    def block(distance):
+        return lax.rem(here + (blocks + distance), blocks)
+
+    def fill_columns(at, number, power):
+        span = pl.ds(pl.multiple_of(at, LANES), LANES)
+        cell = cell_of(jnp.broadcast_to(number, (rows, LANES)))
+        high, low = split(jnp.broadcast_to(power, (rows, LANES)))
+        lane = (cell & (lanes - 1)).astype(jnp.int16)
+        for t in range(lanes // rows):
+            hit = lane == place16 + jnp.int16(t * rows)
+            spread[t * rows : (t + 1) * rows, span] = jnp.where(hit, high, zero)
+            spread[lanes + t * rows : lanes + (t + 1) * rows, span] = jnp.where(hit, low, zero)
+        row = lax.shift_right_arithmetic(cell, 7)
+        across[:, span] = jnp.where((row & (rows - 1)) == place, 1.0, 0.0).astype(BF16)
+        plane_of[:, span] = lax.shift_right_arithmetic(row, rows.bit_length() - 1).astype(jnp.int16)
+
+    def sides(pair, quarter_high, quarter_low):
+        for n, (distance, kind) in enumerate(((1, 0), (0, 1), (-1, 0), (-2, 1))):
+            share = quarter_high if n < 2 else quarter_low
+            h, which = share // 2, share % 2
+            number = paired(got, block(distance), kind, h, 2 * pair)[which]
+            power = paired(got, block(distance), kind, half + h, 2 * pair)[which]
+            fill_columns(inside + (n * pairs + pair) * LANES, number, power)
+
+    def fill_pair(pair, unused):
+        for part in range(2):
             for h in range(half):
-                at = pl.multiple_of((s * half + h) * LANES, LANES)
-                span = pl.ds(part * count + at, LANES)
-                cell = jnp.broadcast_to(got[block, s, h : h + 1, :], (rows, LANES)).astype(I32)
-                power = jnp.broadcast_to(got[block, s, half + h : half + h + 1, :], (rows, LANES))
-                high, low = split(power)
-                lane = (cell & (lanes - 1)).astype(jnp.int16)
-                for t in range(lanes // rows):
-                    hit = lane == place16 + jnp.int16(t * rows)
-                    spread[t * rows : (t + 1) * rows, span] = jnp.where(hit, high, zero)
-                    spread[lanes + t * rows : lanes + (t + 1) * rows, span] = jnp.where(hit, low, zero)
-                upper = cell >= patch
-                row = lax.shift_right_logical(jnp.where(upper, cell - patch, cell), 7)
-                across[:, span] = jnp.where((row & (rows - 1)) == place, 1.0, 0.0).astype(BF16)
-                plane = row // rows
-                own = jnp.where(upper, -1, plane).astype(jnp.int16)
-                on = jnp.where(upper, plane, -1).astype(jnp.int16)
-                if part == 0:
-                    beside[:, span] = own
-                elif part == 1:
-                    inside[:, pl.ds(at, LANES)] = own
-                    beside[:, span] = on
-                elif part == 2:
-                    inside[:, pl.ds(count + at, LANES)] = on
-                    beside[:, span] = own
-                else:
-                    beside[:, span] = on
-            return unused
-
-        lax.fori_loop(0, groups, body, 0)
-
+                numbers = paired(got, block(-part), part, h, 2 * pair)
+                powers = paired(got, block(-part), part, half + h, 2 * pair)
+                for which in range(2):
+                    at = (2 * h + which) * region + (part * pairs + pair) * LANES
+                    fill_columns(at, numbers[which], powers[which])
+        sides(pair, 0, QUARTERS - 1)
+        return unused
+
+    lax.fori_loop(0, pairs, fill_pair, 0)
     source[...] = jnp.zeros(source.shape, F32)
 
-    def product(first, tile, where_x, columns):
+    def product(first, base, count, columns, added=False):
         where_y = across[:, columns]
+        where_x = plane_of[:, columns] - jnp.asarray(base, I32).astype(jnp.int16)
         nothing = jnp.zeros_like(where_y)
         hot = jnp.concatenate(
-            [jnp.where(where_x == jnp.int16(x), where_y, nothing) for x in range(tile)], axis=0
+            [jnp.where(where_x == jnp.int16(x), where_y, nothing) for x in range(count)], axis=0
         )
         both = lax.dot_general(
             hot, spread[:, columns], (((1,), (1,)), ((), ())), preferred_element_type=F32
         )
         value = both[:, :lanes] + both[:, lanes:]
-        for n in range(tile):
+        for n in range(count):
             at = pl.ds(pl.multiple_of((first + n + RIM) * pitch + PAD, 8), rows)
-            source[at, :] = value[n * rows : (n + 1) * rows]
-
-    tile = 32
-
-    def body(m, unused):
-        product(m * tile, tile, inside[...] - (m * tile).astype(jnp.int16), slice(count, 3 * count))
-        return unused
-
-    lax.fori_loop(0, planes // tile, body, 0)
-    wide = RIM - 1
-    product(planes, wide, beside[:, : 2 * count], slice(0, 2 * count))
-    low = beside[:, 2 * count :] - jnp.int16(planes - wide)
-    product(-wide, wide, low, slice(2 * count, 4 * count))
+            part = value[n * rows : (n + 1) * rows]
+            source[at, :] = source[at, :] + part if added else part
+
+    for q in range(QUARTERS):
+        product(q * tile, q * tile, tile, slice(q * region, (q + 1) * region))
+
+    def outside(added):
+        product(planes, 0, wide, slice(inside, inside + region), added)
+        product(-wide, planes - wide, wide, slice(inside + region, inside + 2 * region), added)
+
+    outside(False)
+
+    @pl.when(unsorted(got))
+    def _():
+        def whole(m, unused):
+            product(m * tile, m * tile, tile, slice(0, inside))
+            return unused
+
+        lax.fori_loop(0, QUARTERS, whole, 0)
+        for step in range(1, QUARTERS):
+
+            def others(pair, unused, step=step):
+                sides(pair, step, QUARTERS - 1 - step)
+                return unused
+
+            lax.fori_loop(0, pairs, others, 0)
+            outside(True)
+
     planes_all = planes + 2 * RIM
     top = (1 - is_odd("cross")) * (rows - wide)
     for r in range(wide):
@@ -365,63 +468,81 @@
 
 
 def lookup(me, got, height, lanes, looked, pieces, turned, found):
-    blocks, groups, double, _ = got.shape
-    half = double // 2
-    patch = height * lanes
-    chunks = []
-    for block, upper in ((me, False), (lax.rem(me + blocks - 1, blocks), True)):
-        for s in range(groups):
+    blocks, groups, rows_sent, _ = got.shape
+    half = rows_sent // 4
+    pairs = groups // 2
+    chunks = [[] for _ in range(QUARTERS)]
+    for part in range(2):
+        block = lax.rem(me + (blocks - part), blocks)
+        for pair in range(pairs):
             for h in range(half):
-                cell = got[block, s, h : h + 1, :].astype(I32)
-                if upper:
-                    cell = jnp.where(cell >= patch, cell - patch, -1)
-                else:
-                    cell = jnp.where(cell < patch, cell, -1)
-                chunks.append(cell)
-    count = len(chunks)
+                for which, number in enumerate(paired(got, block, part, h, 2 * pair)):
+                    chunks[2 * h + which].append(cell_of(number))
+    each = len(chunks[0])
+    count = each * QUARTERS
+    chunks = [chunk for share in chunks for chunk in share]
     chunks.append(jnp.zeros((LANES - count, LANES), I32))
     turned[...] = jnp.concatenate(chunks, axis=0).T
     lane = iota((LANES, LANES), 1)
     found[...] = jnp.zeros((LANES, LANES), F32)
-    width = 4
-    for first in range(0, count, width):
+    one = jnp.ones((LANES, LANES), BF16)
+
+    def search(first, number, base, size):
         hots = []
         cells = []
-        for k in range(first, first + width):
+        for k in range(first, first + number):
             cell = jnp.broadcast_to(turned[:, k : k + 1], (LANES, LANES))
             cells.append(cell)
             row = lax.shift_right_arithmetic(cell, 7).astype(jnp.int16)
-            one = jnp.ones((LANES, LANES), BF16)
             hots.append(
                 jnp.concatenate(
                     [
                         jnp.where(
-                            row == (lane + r * LANES).astype(jnp.int16), one, jnp.zeros_like(one)
+                            row == (lane + (base + r)).astype(jnp.int16), one, jnp.zeros_like(one)
                         )
-                        for r in range(height // LANES)
+                        for r in range(0, size, LANES)
                     ],
                     axis=1,
                 )
             )
-        both = jnp.dot(jnp.concatenate(hots, axis=0), pieces[...], preferred_element_type=F32)
+        both = jnp.dot(
+            jnp.concatenate(hots, axis=0),
+            pieces[base : base + size, :],
+            preferred_element_type=F32,
+        )
         value = both[:, :lanes] + both[:, lanes:]
-        for n in range(width):
+        for n in range(number):
             picked = jnp.take_along_axis(
                 value[n * LANES : (n + 1) * LANES], cells[n] & (lanes - 1), axis=1
             )
             found[...] = jnp.where(lane == first + n, picked, found[...])
+
+    for q in range(QUARTERS):
+        search(q * each, each, q * (height // QUARTERS), height // QUARTERS)
+
+    @pl.when(unsorted(got))
+    def _():
+        for first in range(0, count, 4):
+            search(first, 4, 0, height)
+
     back = found[...].T
-    at = 0
+    left = iota((1, LANES), 1) < LANES // 2
     for part in range(2):
-        for s in range(groups):
+        for pair in range(pairs):
             for h in range(half):
-                for block in range(blocks):
-                    looked[block, s, part * half + h : part * half + h + 1, :] = back[at : at + 1, :]
-                at += 1
-
-
-def pick(tables, index):
-    row = lax.shift_right_logical(index, 7)
+                n = part * pairs + pair
+                a = back[2 * h * each + n : 2 * h * each + n + 1, :]
+                b = back[(2 * h + 1) * each + n : (2 * h + 1) * each + n + 1, :]
+                for s, value in ((0, jnp.where(left, a, b)), (1, jnp.where(left, b, a))):
+                    row = (2 * pair + s) * 2 * half + part * half + h
+                    for block in range(blocks):
+                        at = block * groups * 2 * half + row
+                        looked[at : at + 1, :] = value
+
+
+def pick(tables, index, row=None):
+    if row is None:
+        row = lax.shift_right_logical(index, 7)
     lane = index & (LANES - 1)
     results = [jnp.zeros(index.shape, F32) for _ in tables]
     for r in range(len(tables[0])):
@@ -437,23 +558,28 @@
 
 
 def stretch_kernel(
-    side, after, pos, acted, other, gap, snapped, even_x, odd_x, base, slope, delta, hot,
+    side, half, after, pos, acted, other, gap, snapped, even_x, odd_x, base, slope, delta, hot, ghost,
 ):
     count = pos.shape[1] // LANES
     low_ghost, high_ghost = low_and_high("cut", even_x, odd_x)
 
-    def ghosts(ref):
-        places = side + 3 * count
+    def ghosts(n, ref):
+        places = side + 4 * count
         tables = [
             [ref[side + ch * count + r : side + ch * count + r + 1, :] for r in range(count)]
-            for ch in range(3)
+            for ch in range(4)
         ]
-        found = pick(tables, ref[places:, :].astype(I32))
+        index = ref[places:, :].astype(I32)
+        found = pick(tables, index)
+        code = found.pop().astype(I32)
+        group = index // (half * LANES)
+        ghost[n, 0] = group * (2 * half) + lax.shift_right_logical(code, 7)
+        ghost[n, 1] = code & (LANES - 1)
         return [[f[r : r + 1] for r in range(f.shape[0])] for f in found]
 
     own = [rows_of(pos, ch) for ch in range(3)]
-    low = ghosts(low_ghost)
-    high = ghosts(high_ghost)
+    low = ghosts(0, low_ghost)
+    high = ghosts(1, high_ghost)
     first = pick(own, acted[...])
     second = pick([own[ch] + low[ch] + high[ch] for ch in range(3)], other[...])
     d = [second[ch] - first[ch] for ch in range(3)]
@@ -474,31 +600,39 @@
 
 
 def bond_kernel(
-    places, back, pos, vel, acted, other, even_x, odd_x, base, slope, delta, hot,
-    pos_out, vel_out, force,
+    blocks, back, code, pos, vel, acted, other, ghost, base, slope, delta, hot, pos_out, vel_out, force,
 ):
-    blocks, groups, double, _ = back.shape
-    half = double // 2
+    half, groups, _ = code.shape
     here = lax.axis_index("cut")
-    low_ghost, high_ghost = low_and_high("cut", even_x, odd_x)
-
-    def block(distance):
-        return lax.rem(here + (blocks + distance), blocks)
-
-    def temps(distance):
-        return [
-            back[block(distance), j, h : h + 1, :] + back[block(distance + 1), j, half + h : half + h + 1, :]
-            for j in range(groups)
-            for h in range(half)
-        ]
-
-    def ghosts(distance, ref):
-        found = pick([temps(distance)], ref[places:, :].astype(I32))[0]
+    double = 2 * half
+
+    def slots(distance):
+        found = []
+        for kind in range(2):
+            block = lax.rem(here + (blocks + distance + kind), blocks)
+            for h in range(half):
+                first = block * groups * double + kind * half + h
+                found.append(back[pl.ds(first, groups, stride=double), :])
+        return found
+
+    def ghosts(n, distance):
+        rows = slots(distance)
+        table = [rows[k][j : j + 1] for j in range(groups) for k in range(double)]
+        found = pick([table], ghost[n, 1], ghost[n, 0])[0]
         return [found[r : r + 1] for r in range(found.shape[0])]
 
-    own = temps(0)
+    rows = slots(0)
+    temps = []
+    for h in range(half):
+        index = code[h]
+        temp = jnp.zeros(index.shape, F32)
+        for k in range(double):
+            value = jnp.take_along_axis(rows[k], index & (LANES - 1), axis=1)
+            temp = jnp.where(lax.shift_right_logical(index, 7) == k, value, temp)
+        temps.append(temp)
+    own = [temps[h][j : j + 1] for j in range(groups) for h in range(half)]
     first = pick([own], acted[...])[0]
-    second = pick([own + ghosts(-1, low_ghost) + ghosts(1, high_ghost)], other[...])[0]
+    second = pick([own + ghosts(0, -1) + ghosts(1, 1)], other[...])[0]
     scale = base[...] - slope[...] * (first + second)
     values = [split(scale * delta[ch]) for ch in range(3)]
     values = [piece.astype(F32) for pair in values for piece in pair]
@@ -565,12 +699,16 @@
     wide = RIM * rows
 
     exports = exported_copies.shape[0] // LANES
-    places = 2 * wide + grain_placements.size // LANES
-    carried = jax.ShapeDtypeStruct((places + exports, LANES), F32)
-    parcel = jax.ShapeDtypeStruct((blocks, groups, 2 * half, LANES), F32)
-    sent, even_x, odd_x = call(
+    carried = jax.ShapeDtypeStruct((2 * wide + 4 * (count // LANES) + exports, LANES), F32)
+    devices = blocks * groups
+    sent, even_x, odd_x, code = call(
         parcel_kernel,
-        [parcel, carried, carried],
+        [
+            jax.ShapeDtypeStruct((devices * 4 * half, LANES), F32),
+            carried,
+            carried,
+            jax.ShapeDtypeStruct((half, groups, LANES), I32),
+        ],
         [
             temp,
             kappa,
@@ -593,11 +731,10 @@
     )
 
     def exchange(sent):
-        flat = sent.reshape((blocks * groups,) + sent.shape[2:])
-        got = lax.all_to_all(flat, BOTH, split_axis=0, concat_axis=0, tiled=True)
-        return got.reshape(sent.shape)
-
-    got = exchange(sent)
+        sent = sent.reshape(devices, -1, LANES)
+        return lax.all_to_all(sent, BOTH, split_axis=0, concat_axis=0, tiled=True)
+
+    got = exchange(sent).reshape(blocks, groups, 4 * half, LANES)
     even_x, odd_x = swaps("cut", True, even_x, odd_x)
 
     across = jax.ShapeDtypeStruct((2 * RIM, -(-total // 8) * 8, lanes), F32)
@@ -610,16 +747,15 @@
     even_y, odd_y = swaps("cross", False, even_y, odd_y)
 
     strips = jax.ShapeDtypeStruct((RIM - 1,) + across.shape[1:], F32)
-    entries = count
+    entries = 2 * count + 4 * count // QUARTERS
     source, even_s, odd_s = call(
         functools.partial(deposit_kernel, planes),
         [flat, strips, strips],
         [got],
         [
-            pltpu.VMEM((2 * lanes, 4 * entries), BF16),
-            pltpu.VMEM((rows, 4 * entries), BF16),
-            pltpu.VMEM((rows, 2 * entries), jnp.int16),
-            pltpu.VMEM((rows, 4 * entries), jnp.int16),
+            pltpu.VMEM((2 * lanes, entries), BF16),
+            pltpu.VMEM((rows, entries), BF16),
+            pltpu.VMEM((rows, entries), jnp.int16),
         ],
     )
     even_s, odd_s = swaps("cross", False, even_s, odd_s)
@@ -636,7 +772,7 @@
         close_kernel,
         [
             jax.ShapeDtypeStruct((planes, rows, lanes), F32),
-            parcel,
+            jax.ShapeDtypeStruct((devices * 2 * half, LANES), F32),
         ],
         [got, opened, kappa, source, even_s, odd_s],
         [
@@ -646,17 +782,18 @@
             pltpu.VMEM((LANES, LANES), F32),
         ],
     )
-    back = exchange(looked)
+    back = exchange(looked).reshape(looked.shape)
     acted = tether_acted_grain.reshape(-1, LANES)
     other = tether_other_grain.reshape(-1, LANES)
     entry = jax.ShapeDtypeStruct(acted.shape, F32)
-    base, slope, delta, hot = call(
-        functools.partial(stretch_kernel, 2 * wide),
+    base, slope, delta, hot, ghost = call(
+        functools.partial(stretch_kernel, 2 * wide, half),
         [
             entry,
             entry,
             jax.ShapeDtypeStruct((3,) + acted.shape, F32),
             jax.ShapeDtypeStruct((LANES, acted.size), BF16),
+            jax.ShapeDtypeStruct((2, 2, exports, LANES), I32),
         ],
         [
             looked,
@@ -672,10 +809,10 @@
     )
     out = jax.ShapeDtypeStruct(grain_placements.shape, F32)
     positions_new, velocities_new = call(
-        functools.partial(bond_kernel, places),
+        functools.partial(bond_kernel, blocks),
         [out, out],
         [
-            back, grain_placements, grain_motion_parts, acted, other, even_x, odd_x,
+            back, code, grain_placements, grain_motion_parts, acted, other, ghost,
             base, slope, delta, hot,
         ],
         [pltpu.VMEM((6 * (count // LANES), acted.size), BF16)],

time: 61.1 us -> 58 us (0.949)
  Pallas kernels: 27.4 us -> 20.8 us
  starting transfers between devices: 23.6 us -> 25.8 us
  waiting for transfers between devices: 8.93 us -> 10.3 us
    pallas_call x7, Pallas kernels: 27.4 us -> 20.8 us  [call(): pl.pallas_call(kernel, out_shape=outs, in_specs=[pl.BlockSpec(memory_spac...]
    all_to_all x2, starting transfers between devices: 15 us -> 17.1 us  [exchange(): return lax.all_to_all(sent, BOTH, split_axis=0, concat_axis=0, tiled=True)]
    ppermute x6, waiting for transfers between devices: 4.91 us -> 6.31 us  [swaps(): results.append(lax.ppermute(block, axis, pairs))]
  transfers between devices with their start and end apart: 8 -> 8, of which waited for: 3 -> 3; matrix products, arithmetic and copies ran while one was open for 0% -> 0% of each run, Pallas kernels for 22% -> 14%
where the time goes in v4:
time: 58 us; the launch traced here: 57.8 us
  starting transfers between devices  25.8 us (44%)
  Pallas kernels  20.8 us (36%)
  waiting for transfers between devices  10.3 us (18%)
  between operations  0.85 us (1%)
    pallas_call x7, Pallas kernels, call(): pl.pallas_call(kernel, out_shape=outs, in_specs=[pl.BlockSpec(memory_spac...  20.8 us
    all_to_all x2, starting transfers between devices, exchange(): return lax.all_to_all(sent, BOTH, split_axis=0, concat_axis=0, tiled=True)  17.1 us
    ppermute x6, starting transfers between devices, swaps(): results.append(lax.ppermute(block, axis, pairs))  8.68 us
    ppermute x6, waiting for transfers between devices, swaps(): results.append(lax.ppermute(block, axis, pairs))  6.31 us
    all_to_all x2, waiting for transfers between devices, exchange(): return lax.all_to_all(sent, BOTH, split_axis=0, concat_axis=0, tiled=True)  3.98 us
  transfers between devices with their start and end apart: 8, of which 3 were waited for; matrix products, arithmetic and copies ran while one was open for 0% of the time, Pallas kernels for 14%

profile of v4, /device:TPU:0, one launch (start us, length us, event | category | flops | bytes accessed | tf_op | source)
XLA Modules:
  0.0 57.8 jit_solution(8813775522091522367)
XLA Ops:
  0.6 0.0 copy-start.1
  0.6 0.0 copy-start
  0.7 2.4 %shard_map.139 = (f32[256,128]{1,0:T(8,128)}, f32[162,128]{1,0:T(8,128)}, f32[162,128]{1,0:T(8,128)}, s32[2,8,128]{2,1,0:T(8,128)}) custom-call(f32[2048,128]{1,0:T(8,128)} %bitcast.14, f32[2048,128]{1,0:T(8,128)} %bitcast.17, s32[16,128]{1,0:T(8,128)} %bitcast.31, f32[16,128]{1,0:T(8,128)} %bitcast.32, s32[16,128]{1,0:T(8,128)} %bitcast.33, f32[3,2048]{1,0:T(4,128)} %pos.5, ...), custom_call_target="tpu_custom_call" | custom-call | tf_op jit(solution)/shard_map/pallas_call | solution.py:20
  3.1 7.3 %all-to-all-start = ((f32[32,8,128]{2,1,0:T(8,128)}), f32[32,8,128]{2,1,0:T(8,128)S(1)}, u32[]{:S(2)}, u32[]{:S(2)}) async-start(f32[32,8,128]{2,1,0:T(8,128)} %bitcast.30), calls=%async_computation | async-start | bytes 262144 | tf_op jit(solution)/shard_map/all_to_all | solution.py:735
  10.4 1.8 %collective-permute-start = (f32[162,128]{1,0:T(8,128)}, f32[162,128]{1,0:T(8,128)S(1)}, u32[]{:S(2)}, u32[]{:S(2)}) collective-permute-start(f32[162,128]{1,0:T(8,128)} %get-tuple-element.25), channel_id=1, source_target_pairs={{0,8},{8,0},{16,24},{24,16},{1,9},{9,1},{17,25},{25,17},{2,10},{10... | collective-permute-start | bytes 248840 | tf_op jit(solution)/shard_map/ppermute | solution.py:671
  12.2 2.4 %collective-permute-start.1 = (f32[162,128]{1,0:T(8,128)}, f32[162,128]{1,0:T(8,128)S(1)}, u32[]{:S(2)}, u32[]{:S(2)}) collective-permute-start(f32[162,128]{1,0:T(8,128)} %get-tuple-element.26), channel_id=1, source_target_pairs={{8,16},{16,8},{24,0},{0,24},{9,17},{17,9},{25,1},{1,25},{10,18},{1... | collective-permute-start | bytes 248840 | tf_op jit(solution)/shard_map/ppermute | solution.py:671
  14.6 2.5 %collective-permute-done.even_x = f32[162,128]{1,0:T(8,128)S(1)} collective-permute-done((f32[162,128]{1,0:T(8,128)}, f32[162,128]{1,0:T(8,128)S(1)}, u32[]{:S(2)}, u32[]{:S(2)}) %collective-permute-start) | collective-permute-done | bytes 82976 | tf_op jit(solution)/shard_map/ppermute | solution.py:671
  17.1 3.8 %collective-permute-done.1.odd_x = f32[162,128]{1,0:T(8,128)S(1)} collective-permute-done((f32[162,128]{1,0:T(8,128)}, f32[162,128]{1,0:T(8,128)S(1)}, u32[]{:S(2)}, u32[]{:S(2)}) %collective-permute-start.1) | collective-permute-done | bytes 82976 | tf_op jit(solution)/shard_map/ppermute | solution.py:671
  20.9 0.0 all-to-all-done
  20.9 0.0 copy-done.1
  20.9 0.0 copy-done
  20.9 0.4 shard_map.141
  21.2 0.1 collective-permute-start.2
  21.3 0.7 %collective-permute-start.3 = (f32[6,136,128]{2,1,0:T(8,128)S(1)}, f32[6,136,128]{2,1,0:T(8,128)S(1)}, u32[]{:S(2)}, u32[]{:S(2)}) collective-permute-start(f32[6,136,128]{2,1,0:T(8,128)S(1)} %get-tuple-element.28), channel_id=1, source_target_pairs={{1,2},{2,1},{3,4},{4,3},{5,6},{6,5},{9,10},{10,9},{11,12},{12,11},... | collective-permute-start | bytes 1253384 | tf_op jit(solution)/shard_map/ppermute | solution.py:671
  22.0 2.7 %shard_map.140 = (f32[3264,128]{1,0:T(8,128)S(1)}, f32[2,136,128]{2,1,0:T(8,128)S(1)}, f32[2,136,128]{2,1,0:T(8,128)S(1)}) custom-call(f32[4,8,8,128]{3,2,1,0:T(8,128)S(1)} %bitcast.21), custom_call_target="tpu_custom_call" | custom-call | tf_op jit(solution)/shard_map/pallas_call | solution.py:20
  24.7 2.9 %collective-permute-start.4 = (f32[2,136,128]{2,1,0:T(8,128)S(1)}, f32[2,136,128]{2,1,0:T(8,128)S(1)}, u32[]{:S(2)}, u32[]{:S(2)}) collective-permute-start(f32[2,136,128]{2,1,0:T(8,128)S(1)} %get-tuple-element.31), channel_id=1, source_target_pairs={{0,1},{1,0},{2,3},{3,2},{4,5},{5,4},{6,7},{7,6},{8,9},{9,8},{10,11... | collective-permute-start | bytes 417800 | tf_op jit(solution)/shard_map/ppermute | solution.py:671
  27.6 0.8 %collective-permute-start.5 = (f32[2,136,128]{2,1,0:T(8,128)S(1)}, f32[2,136,128]{2,1,0:T(8,128)S(1)}, u32[]{:S(2)}, u32[]{:S(2)}) collective-permute-start(f32[2,136,128]{2,1,0:T(8,128)S(1)} %get-tuple-element.32), channel_id=1, source_target_pairs={{1,2},{2,1},{3,4},{4,3},{5,6},{6,5},{9,10},{10,9},{11,12},{12,11},... | collective-permute-start | bytes 417800 | tf_op jit(solution)/shard_map/ppermute | solution.py:671
  28.4 0.0 collective-permute-done.2.even_y
  28.5 0.0 collective-permute-done.3.odd_y
  28.5 2.5 %shard_map.142 = (f32[3264,128]{1,0:T(8,128)S(1)}, f32[3264,128]{1,0:T(8,128)S(1)}) custom-call(f32[2048,128]{1,0:T(8,128)S(1)} %bitcast.16, f32[2048,128]{1,0:T(8,128)S(1)} %bitcast.19, f32[3264,128]{1,0:T(8,128)S(1)} %get-tuple-element.24.source.source_own, f32[162,128]{1,0:T(8,128)S(1)} %collective-permute-done.even_x, ...), custom_call_target="tpu_custom_call" | custom-call | tf_op jit(solution)/shard_map/pallas_call | solution.py:20
  31.0 0.0 collective-permute-done.4.even_y
  31.0 0.0 collective-permute-done.5.odd_y
  31.0 0.0 copy-start.2
  31.0 0.0 copy-start.3
  31.0 0.0 copy-start.4
  31.0 0.0 copy-start.6
  31.0 0.0 copy-start.7
  31.0 0.0 copy-start.5
  31.1 0.0 copy-start.8
  31.1 7.6 %shard_map.143 = (f32[128,16,128]{2,1,0:T(8,128)}, f32[128,128]{1,0:T(8,128)}) custom-call(f32[4,8,8,128]{3,2,1,0:T(8,128)S(1)} %bitcast.22, f32[3264,128]{1,0:T(8,128)S(1)} %get-tuple-element.29.opened, f32[3264,128]{1,0:T(8,128)S(1)} %get-tuple-element.30.kappa, f32[3264,128]{1,0:T(8,128)S(1)} %get-tuple-element.24.source.source_own, ...), custom_call_target="tpu_custom_call" | custom-call | tf_op jit(solution)/shard_map/pallas_call | solution.py:20
  38.7 9.8 %all-to-all-start.1 = ((f32[32,4,128]{2,1,0:T(4,128)}), f32[32,4,128]{2,1,0:T(4,128)S(1)}, u32[]{:S(2)}, u32[]{:S(2)}) async-start(f32[32,4,128]{2,1,0:T(4,128)} %bitcast.8), calls=%async_computation.1 | async-start | bytes 131072 | tf_op jit(solution)/shard_map/all_to_all | solution.py:735
  48.5 0.0 copy-done.2
  48.5 0.0 copy-done.3
  48.5 0.0 copy-done.4
  48.5 0.0 copy-done.6
  48.5 0.0 copy-done.7
  48.6 3.2 %shard_map.144 = (f32[64,128]{1,0:T(8,128)S(1)}, f32[64,128]{1,0:T(8,128)S(1)}, f32[3,64,128]{2,1,0:T(8,128)S(1)}, bf16[128,8192]{1,0:T(8,128)(2,1)S(1)}, s32[2,2,2,128]{3,2,1,0:T(2,128)S(1)}) custom-call(f32[128,128]{1,0:T(8,128)} %get-tuple-element.34.after, f32[3,2048]{1,0:T(4,128)S(1)} %copy-done.2, s32[64,128]{1,0:T(8,128)S(1)} %bitcast.24, ...), custom_call_target="tpu_custom_call" | custom-call | tf_op jit(solution)/shard_map/pallas_call | solution.py:20
  51.7 4.0 %all-to-all-done.1 = f32[32,4,128]{2,1,0:T(4,128)S(1)} async-done(((f32[32,4,128]{2,1,0:T(4,128)}), f32[32,4,128]{2,1,0:T(4,128)S(1)}, u32[]{:S(2)}, u32[]{:S(2)}) %all-to-all-start.1) | async-done | bytes 65568 | tf_op jit(solution)/shard_map/all_to_all | solution.py:735
  55.7 0.0 copy-done.5
  55.7 0.0 copy-done.8
  55.7 2.1 %shard_map.145 = (f32[3,2048]{1,0:T(4,128)}, f32[3,2048]{1,0:T(4,128)}) custom-call(f32[128,128]{1,0:T(8,128)S(1)} %bitcast.23, s32[2,8,128]{2,1,0:T(8,128)S(1)} %copy-done.8, f32[3,2048]{1,0:T(4,128)S(1)} %copy-done.2, f32[3,2048]{1,0:T(4,128)S(1)} %copy-done.5, s32[64,128]{1,0:T(8,128)S(1)} %bitcast.25, s32[64,128]{1,0:T(8,128)S(1)} %bitcast.27, ...), custom_call_target="tpu_custom_call" | custom-call | tf_op jit(solution)/shard_map/pallas_call | solution.py:20
Async XLA Ops:
  0.6 20.2 %copy-start.1 = (f32[128,16,128]{2,1,0:T(8,128)S(1)}, f32[128,16,128]{2,1,0:T(8,128)}, u32[]{:S(2)}) copy-start(f32[128,16,128]{2,1,0:T(8,128)} %param.13) | copy-start | bytes 3145732
  0.6 20.2 %copy-start = (f32[128,16,128]{2,1,0:T(8,128)S(1)}, f32[128,16,128]{2,1,0:T(8,128)}, u32[]{:S(2)}) copy-start(f32[128,16,128]{2,1,0:T(8,128)} %param.12) | copy-start | bytes 3145732
  3.1 17.8 %all-to-all-start = ((f32[32,8,128]{2,1,0:T(8,128)}), f32[32,8,128]{2,1,0:T(8,128)S(1)}, u32[]{:S(2)}, u32[]{:S(2)}) async-start(f32[32,8,128]{2,1,0:T(8,128)} %bitcast.30), calls=%async_computation | async-start | bytes 262144 | tf_op jit(solution)/shard_map/all_to_all | solution.py:735
  10.4 6.7 %collective-permute-start = (f32[162,128]{1,0:T(8,128)}, f32[162,128]{1,0:T(8,128)S(1)}, u32[]{:S(2)}, u32[]{:S(2)}) collective-permute-start(f32[162,128]{1,0:T(8,128)} %get-tuple-element.25), channel_id=1, source_target_pairs={{0,8},{8,0},{16,24},{24,16},{1,9},{9,1},{17,25},{25,17},{2,10},{10... | collective-permute-start | bytes 248840 | tf_op jit(solution)/shard_map/ppermute | solution.py:671
  12.2 8.7 %collective-permute-start.1 = (f32[162,128]{1,0:T(8,128)}, f32[162,128]{1,0:T(8,128)S(1)}, u32[]{:S(2)}, u32[]{:S(2)}) collective-permute-start(f32[162,128]{1,0:T(8,128)} %get-tuple-element.26), channel_id=1, source_target_pairs={{8,16},{16,8},{24,0},{0,24},{9,17},{17,9},{25,1},{1,25},{10,18},{1... | collective-permute-start | bytes 248840 | tf_op jit(solution)/shard_map/ppermute | solution.py:671
  21.2 7.2 %collective-permute-start.2 = (f32[6,136,128]{2,1,0:T(8,128)S(1)}, f32[6,136,128]{2,1,0:T(8,128)S(1)}, u32[]{:S(2)}, u32[]{:S(2)}) collective-permute-start(f32[6,136,128]{2,1,0:T(8,128)S(1)} %get-tuple-element.27), channel_id=1, source_target_pairs={{0,1},{1,0},{2,3},{3,2},{4,5},{5,4},{6,7},{7,6},{8,9},{9,8},{10,11... | collective-permute-start | bytes 1253384 | tf_op jit(solution)/shard_map/ppermute | solution.py:671
  21.3 7.1 %collective-permute-start.3 = (f32[6,136,128]{2,1,0:T(8,128)S(1)}, f32[6,136,128]{2,1,0:T(8,128)S(1)}, u32[]{:S(2)}, u32[]{:S(2)}) collective-permute-start(f32[6,136,128]{2,1,0:T(8,128)S(1)} %get-tuple-element.28), channel_id=1, source_target_pairs={{1,2},{2,1},{3,4},{4,3},{5,6},{6,5},{9,10},{10,9},{11,12},{12,11},... | collective-permute-start | bytes 1253384 | tf_op jit(solution)/shard_map/ppermute | solution.py:671
  24.7 6.2 %collective-permute-start.4 = (f32[2,136,128]{2,1,0:T(8,128)S(1)}, f32[2,136,128]{2,1,0:T(8,128)S(1)}, u32[]{:S(2)}, u32[]{:S(2)}) collective-permute-start(f32[2,136,128]{2,1,0:T(8,128)S(1)} %get-tuple-element.31), channel_id=1, source_target_pairs={{0,1},{1,0},{2,3},{3,2},{4,5},{5,4},{6,7},{7,6},{8,9},{9,8},{10,11... | collective-permute-start | bytes 417800 | tf_op jit(solution)/shard_map/ppermute | solution.py:671
  27.6 3.4 %collective-permute-start.5 = (f32[2,136,128]{2,1,0:T(8,128)S(1)}, f32[2,136,128]{2,1,0:T(8,128)S(1)}, u32[]{:S(2)}, u32[]{:S(2)}) collective-permute-start(f32[2,136,128]{2,1,0:T(8,128)S(1)} %get-tuple-element.32), channel_id=1, source_target_pairs={{1,2},{2,1},{3,4},{4,3},{5,6},{6,5},{9,10},{10,9},{11,12},{12,11},... | collective-permute-start | bytes 417800 | tf_op jit(solution)/shard_map/ppermute | solution.py:671
  31.0 17.5 %copy-start.2 = (f32[3,2048]{1,0:T(4,128)S(1)}, f32[3,2048]{1,0:T(4,128)}, u32[]{:S(2)}) copy-start(f32[3,2048]{1,0:T(4,128)} %pos.5) | copy-start | bytes 73732
  31.0 17.5 %copy-start.3 = (s32[8192]{0:T(1024)S(1)}, s32[8192]{0:T(1024)}, u32[]{:S(2)}) copy-start(s32[8192]{0:T(1024)} %param.19) | copy-start | bytes 98308
  31.0 17.5 %copy-start.4 = (s32[8192]{0:T(1024)S(1)}, s32[8192]{0:T(1024)}, u32[]{:S(2)}) copy-start(s32[8192]{0:T(1024)} %param.20) | copy-start | bytes 98308
  31.0 17.5 %copy-start.6 = (f32[8192]{0:T(1024)S(1)}, f32[8192]{0:T(1024)}, u32[]{:S(2)}) copy-start(f32[8192]{0:T(1024)} %param.21) | copy-start | bytes 98308
  31.0 17.5 %copy-start.7 = (s32[8192]{0:T(1024)S(1)}, s32[8192]{0:T(1024)}, u32[]{:S(2)}) copy-start(s32[8192]{0:T(1024)} %param.22) | copy-start | bytes 98308
  31.0 24.6 %copy-start.5 = (f32[3,2048]{1,0:T(4,128)S(1)}, f32[3,2048]{1,0:T(4,128)}, u32[]{:S(2)}) copy-start(f32[3,2048]{1,0:T(4,128)} %vel.1) | copy-start | bytes 73732
  31.1 24.6 %copy-start.8 = (s32[2,8,128]{2,1,0:T(8,128)S(1)}, s32[2,8,128]{2,1,0:T(8,128)}, u32[]{:S(2)}) copy-start(s32[2,8,128]{2,1,0:T(8,128)} %get-tuple-element.35.code) | copy-start | bytes 24580
  38.7 17.0 %all-to-all-start.1 = ((f32[32,4,128]{2,1,0:T(4,128)}), f32[32,4,128]{2,1,0:T(4,128)S(1)}, u32[]{:S(2)}, u32[]{:S(2)}) async-start(f32[32,4,128]{2,1,0:T(4,128)} %bitcast.8), calls=%async_computation.1 | async-start | bytes 131072 | tf_op jit(solution)/shard_map/all_to_all | solution.py:735

commit v5 on v4

--- a/solution.py
+++ b/solution.py
@@ -16,12 +16,12 @@
 LIMIT = 32 * 1024 * 1024
 
 
-def call(kernel, outs, operands, scratch=(), left=0, limit=LIMIT):
+def call(kernel, outs, operands, scratch=(), left=0, limit=LIMIT, outs_left=0):
     return pl.pallas_call(
         kernel,
         out_shape=outs,
         in_specs=[pl.BlockSpec(memory_space=pltpu.HBM)] * left + [VMEM] * (len(operands) - left),
-        out_specs=[VMEM] * len(outs),
+        out_specs=[pl.BlockSpec(memory_space=pltpu.HBM)] * outs_left + [VMEM] * (len(outs) - outs_left),
         scratch_shapes=list(scratch),
         compiler_params=pltpu.CompilerParams(vmem_limit_bytes=limit),
     )(*operands)
@@ -104,20 +104,28 @@
 def flow_pass(temp, cond, along_z, first, blocks, pitch, most, put):
     size = groups_of(blocks, most)
 
-    def body(n, unused):
-        block = first + n * size
-        base = pl.multiple_of(block * pitch, 8)
-        at = pl.ds(base, size * pitch)
-        t = temp[at, :]
-        c = cond[at, :]
-        net = along_z[at, :]
-        for shift in (pitch, -pitch, 1, -1):
-            beside = pl.ds(base + shift, size * pitch)
-            net = net + (c + cond[beside, :]) * (temp[beside, :] - t)
-        put(block, size, t + net)
-        return unused
-
-    lax.fori_loop(0, blocks // size, body, 0)
+    def rows_at(ref, base):
+        return ref[pl.ds(base, pitch), :]
+
+    def body(n, carried):
+        t, c, flux = carried
+        for k in range(size):
+            block = first + n * size + k
+            base = pl.multiple_of(block * pitch, 8)
+            t_next = rows_at(temp, base + pitch)
+            c_next = rows_at(cond, base + pitch)
+            onward = (c + c_next) * (t_next - t)
+            net = rows_at(along_z, base) + (onward - flux)
+            for shift in (1, -1):
+                net = net + (c + rows_at(cond, base + shift)) * (rows_at(temp, base + shift) - t)
+            put(block, t + net)
+            t, c, flux = t_next, c_next, onward
+        return t, c, flux
+
+    base = first * pitch
+    t, c = rows_at(temp, base), rows_at(cond, base)
+    flux = (c + rows_at(cond, base - pitch)) * (t - rows_at(temp, base - pitch))
+    lax.fori_loop(0, blocks // size, body, (t, c, flux))
 
 
 def rim_mask(pitch, lanes):
@@ -128,9 +136,9 @@
     return jnp.where(place < PAD - RIM, above, jnp.where(place < PAD, below, 1.0))
 
 
-def fill(flat, own, x_low, x_high, y_low, y_high, rows, pitch, scale):
+def fill(flat, own, x_low, x_high, y_low, y_high, corner_low, corner_high, rows, scale):
+    pitch = rows + PAD
     planes = own.shape[0] // rows
-    total = planes + 2 * RIM
     flat[...] = jnp.zeros(flat.shape, F32)
 
     def place(p, part):
@@ -146,8 +154,13 @@
 
     lax.fori_loop(0, planes, body, 0, unroll=8)
     for r in range(RIM):
-        flat[pl.ds(PAD - RIM + r, total, stride=pitch), :] = y_low[r, :total, :] * scale
-        flat[pl.ds(PAD + rows + r, total, stride=pitch), :] = y_high[r, :total, :] * scale
+        below = PAD - RIM + r
+        flat[pl.ds(RIM * pitch + below, planes, stride=pitch), :] = y_low[r, :, :] * scale
+        flat[pl.ds((RIM + 1) * pitch + r, planes, stride=pitch), :] = y_high[r, :, :] * scale
+        for n in range(2 * RIM):
+            p = n if n < RIM else n + planes
+            flat[p * pitch + below : p * pitch + below + 1, :] = corner_low[r, n : n + 1, :] * scale
+            flat[(p + 1) * pitch + r : (p + 1) * pitch + r + 1, :] = corner_high[r, n : n + 1, :] * scale
 
 
 def parcel_kernel(
@@ -254,97 +267,103 @@
         copy.wait()
 
 
-def rows_kernel(rows, after, temp, kappa, even_x, odd_x, even, odd):
-    side = RIM * rows
+def rows_kernel(rows, after, temp, kappa, even, odd):
     planes = temp.shape[0] // rows
-    low, high = low_and_high("cut", even_x, odd_x)
     top = (1 - is_odd("cross")) * (rows - RIM)
     for n, own in enumerate((temp, kappa)):
         for r in range(RIM):
             for out, first in ((even, top), (odd, rows - RIM - top)):
-                target = n * RIM + r
-                for p in range(RIM):
-                    at = pl.ds(n * side + p * rows + first + r, 1)
-                    out[target, p : p + 1, :] = low[at, :]
-                    out[target, RIM + planes + p : RIM + planes + p + 1, :] = high[at, :]
-                out[target, RIM : RIM + planes, :] = own[pl.ds(first + r, planes, stride=rows), :]
-
-
-def open_kernel(
-    rows, temp, kappa, source, even_x, odd_x, even_y, odd_y,
-    spread_temp, spread_kappa, start, cond, along_z, minus, plus,
+                out[n * RIM + r] = own[pl.ds(first + r, planes, stride=rows), :]
+
+
+def corner_kernel(rows, even_s, odd_s, even_x, odd_x, even, odd):
+    side = RIM * rows
+    low, high = low_and_high("cut", even_x, odd_x)
+    top = (1 - is_odd("cross")) * (rows - RIM)
+    base = even_s.shape[0]
+    for out, strips, first in ((even, even_s, top), (odd, odd_s, rows - RIM - top)):
+        out[:base, :] = strips[...]
+        for n in range(2 * RIM):
+            for p in range(RIM):
+                at = pl.ds(n // RIM * side + p * rows + first + n % RIM, 1)
+                to = base + n * PAD + p
+                out[to : to + 1, :] = low[at, :]
+                out[to + RIM : to + RIM + 1, :] = high[at, :]
+            out[base + n * PAD + 2 * RIM : base + (n + 1) * PAD, :] = jnp.zeros((PAD - 2 * RIM, LANES), F32)
+
+
+class Rows:
+    def __init__(self, ref, base, size):
+        self.ref, self.base, self.size = ref, base, size
+
+    def __getitem__(self, index):
+        r, at, lanes = index
+        first = self.base + r * self.size
+        return self.ref[first + (at.start or 0) : first + (self.size if at.stop is None else at.stop), :]
+
+
+def heat_kernel(
+    got, temp, kappa_own, source_own, even_x, odd_x, even_y, odd_y, even_s, odd_s,
+    temp_out, looked, source, kappa, now, then, cond, along_z, minus, plus, pieces, result, sem,
 ):
     lanes = temp.shape[1]
-    x_low, x_high = low_and_high("cut", even_x, odd_x)
-    y_low, y_high = low_and_high("cross", even_y, odd_y)
-    side = RIM * rows
-    pitch = rows + PAD
-    planes = temp.shape[0] // rows
-    minus[...], plus[...] = difference_matrices(lanes)
-    fill(start, temp, x_low.part(slice(None, side)), x_high.part(slice(None, side)), y_low.part(slice(None, RIM)), y_high.part(slice(None, RIM)), rows, pitch, 1.0)
-    fill(
-        spread_kappa, kappa, x_low.part(slice(side, 2 * side)), x_high.part(slice(side, 2 * side)),
-        y_low.part(slice(RIM, 2 * RIM)), y_high.part(slice(RIM, 2 * RIM)), rows, pitch, 0.5,
-    )
-    blocks = planes + 2 * RIM + 1
-    conduct_pass(start, spread_kappa, cond, along_z, minus, plus, 0, blocks, pitch)
-    mask = rim_mask(pitch, lanes)
-    for at in (0, blocks - 1):
-        spread_temp[at * pitch : (at + 1) * pitch, :] = jnp.zeros((pitch, lanes), F32)
-    spread_temp[blocks * pitch :, :] = jnp.zeros((spread_temp.shape[0] - blocks * pitch, lanes), F32)
-
-    def put(block, size, value):
-        value = value.reshape(size, pitch, lanes) * mask[None]
-        at = pl.ds(pl.multiple_of(block * pitch, 8), size * pitch)
-        spread_temp[at, :] = value.reshape(size * pitch, lanes) + source[at, :]
-
-    flow_pass(start, cond, along_z, 1, blocks - 2, pitch, 133, put)
-
-
-def close_kernel(
-    got, opened, kappa, source_own, even_y, odd_y,
-    temp_out, looked, source, now, then, cond, along_z, minus, plus, pieces, turned, found,
-):
-    lanes = kappa.shape[1]
-    planes, rows, _ = temp_out.shape
+    planes, rows, _ = result.shape
     pitch = rows + PAD
     total = planes + 2 * RIM
     blocks = total + 1
+    side = RIM * rows
+    wide = RIM - 1
+    x_low, x_high = low_and_high("cut", even_x, odd_x)
+    y_low, y_high = low_and_high("cross", even_y, odd_y)
+    s_low, s_high = low_and_high("cross", even_s, odd_s)
+    height = -(-total // 8) * 8
     minus[...], plus[...] = difference_matrices(lanes)
-    wide = RIM - 1
+    for n, (flat, own, scale) in enumerate(((now, temp, 1.0), (kappa, kappa_own, 0.5))):
+        beside = [half.part(slice(n * side, (n + 1) * side)) for half in (x_low, x_high)]
+        strips = [half.part(slice(n * RIM, (n + 1) * RIM)) for half in (y_low, y_high)]
+        corners = [Rows(half, wide * height + n * RIM * PAD, PAD) for half in (s_low, s_high)]
+        fill(flat, own, *beside, *strips, *corners, rows, scale)
     source[...] = source_own[...]
-    now[...] = opened[...]
-    low, high = low_and_high("cross", even_y, odd_y)
-    for r in range(wide):
-        for first, beside in ((PAD - wide + r, low), (PAD + rows + r, high)):
-            at = pl.ds(first, total, stride=pitch)
-            strip = beside[r, :total, :]
-            source[at, :] = strip
-            now[at, :] = now[at, :] + strip
+    for first, half in ((PAD - wide, s_low), (PAD + rows, s_high)):
+        strips = Rows(half, 0, height)
+        for r in range(wide):
+            source[pl.ds(first + r, total, stride=pitch), :] = strips[r, :total, :]
     mask = rim_mask(pitch, lanes)
     conduct_pass(now, kappa, cond, along_z, minus, plus, 0, blocks, pitch)
     then[0:pitch, :] = jnp.zeros((pitch, lanes), F32)
     then[(blocks - 1) * pitch :, :] = jnp.zeros((then.shape[0] - (blocks - 1) * pitch, lanes), F32)
 
-    def middle(block, size, value):
-        at = pl.ds(pl.multiple_of(block * pitch, 8), size * pitch)
-        value = (value + source[at, :]).reshape(size, pitch, lanes) * mask[None]
-        then[at, :] = value.reshape(size * pitch, lanes)
-
-    flow_pass(now, cond, along_z, 1, blocks - 2, pitch, 133, middle)
+    def opening(block, value):
+        at = pl.ds(pl.multiple_of(block * pitch, 8), pitch)
+        then[at, :] = (value + source[at, :]) * mask
+
+    flow_pass(now, cond, along_z, 1, blocks - 2, pitch, 1000, opening)
+    now[0:pitch, :] = jnp.zeros((pitch, lanes), F32)
+    now[(blocks - 1) * pitch :, :] = jnp.zeros((now.shape[0] - (blocks - 1) * pitch, lanes), F32)
     conduct_pass(then, kappa, cond, along_z, minus, plus, 0, blocks, pitch)
 
-    def last(block, size, value):
-        at = pl.ds(pl.multiple_of(block * pitch, 8), size * pitch)
-        value = (value + source[at, :]).reshape(size, pitch, lanes)[:, PAD:]
-        temp_out[pl.ds(block - RIM, size)] = value
-        high, low = split(value.reshape(size * rows, lanes))
-        at = pl.ds(pl.multiple_of((block - RIM) * rows, rows), size * rows)
-        pieces[at, :lanes] = high
-        pieces[at, lanes:] = low
-
-    flow_pass(then, cond, along_z, RIM, planes, pitch, 8, last)
-    lookup(lax.axis_index("cut"), got, planes * rows, lanes, looked, pieces, turned, found)
+    def middle(block, value):
+        at = pl.ds(pl.multiple_of(block * pitch, 8), pitch)
+        now[at, :] = (value + source[at, :]) * mask
+
+    flow_pass(then, cond, along_z, 1, blocks - 2, pitch, 1000, middle)
+    conduct_pass(now, kappa, cond, along_z, minus, plus, 0, blocks, pitch)
+
+    def last(block, value):
+        at = pl.ds(pl.multiple_of(block * pitch, 8), pitch)
+        result[block - RIM] = (value + source[at, :])[PAD:]
+
+    flow_pass(now, cond, along_z, RIM, planes, pitch, 1000, last)
+    copy = pltpu.make_async_copy(result, temp_out, sem)
+    copy.start()
+    height = planes * rows
+    for first in range(0, planes, lanes // rows):
+        turned = result[first : first + lanes // rows].reshape(lanes, lanes).T
+        high, low = split(turned)
+        pieces[:lanes, first * rows : first * rows + lanes] = high
+        pieces[lanes:, first * rows : first * rows + lanes] = low
+    lookup(lax.axis_index("cut"), got, height, lanes, rows, looked, pieces)
+    copy.wait()
 
 
 def paired(got, block, kind, row, s):
@@ -464,80 +483,76 @@
     top = (1 - is_odd("cross")) * (rows - wide)
     for r in range(wide):
         for out, first in ((even, top), (odd, rows - wide - top)):
-            out[r, :planes_all, :] = source[pl.ds(PAD + first + r, planes_all, stride=pitch), :]
-
-
-def lookup(me, got, height, lanes, looked, pieces, turned, found):
+            at = r * (out.shape[0] // wide)
+            out[at : at + planes_all, :] = source[pl.ds(PAD + first + r, planes_all, stride=pitch), :]
+
+
+def lookup(me, got, height, lanes, rows, looked, pieces):
     blocks, groups, rows_sent, _ = got.shape
     half = rows_sent // 4
     pairs = groups // 2
-    chunks = [[] for _ in range(QUARTERS)]
-    for part in range(2):
-        block = lax.rem(me + (blocks - part), blocks)
-        for pair in range(pairs):
-            for h in range(half):
-                for which, number in enumerate(paired(got, block, part, h, 2 * pair)):
-                    chunks[2 * h + which].append(cell_of(number))
-    each = len(chunks[0])
-    count = each * QUARTERS
-    chunks = [chunk for share in chunks for chunk in share]
-    chunks.append(jnp.zeros((LANES - count, LANES), I32))
-    turned[...] = jnp.concatenate(chunks, axis=0).T
-    lane = iota((LANES, LANES), 1)
-    found[...] = jnp.zeros((LANES, LANES), F32)
-    one = jnp.ones((LANES, LANES), BF16)
-
-    def search(first, number, base, size):
+    shift = rows.bit_length() - 1
+    place = iota((rows, LANES), 0)
+    lane_place = iota((lanes, LANES), 0)
+    zero = jnp.zeros((rows, LANES), BF16)
+
+    def search(numbers, base, size):
         hots = []
-        cells = []
-        for k in range(first, first + number):
-            cell = jnp.broadcast_to(turned[:, k : k + 1], (LANES, LANES))
-            cells.append(cell)
-            row = lax.shift_right_arithmetic(cell, 7).astype(jnp.int16)
+        for number in numbers:
+            row = lax.shift_right_arithmetic(cell_of(jnp.broadcast_to(number, (rows, LANES))), 7)
+            plane = lax.shift_right_arithmetic(row, shift).astype(jnp.int16)
+            hot_row = jnp.where((row & (rows - 1)) == place, 1.0, 0.0).astype(BF16)
             hots.append(
                 jnp.concatenate(
                     [
-                        jnp.where(
-                            row == (lane + (base + r)).astype(jnp.int16), one, jnp.zeros_like(one)
-                        )
-                        for r in range(0, size, LANES)
+                        jnp.where(plane == jnp.int16(x), hot_row, zero)
+                        for x in range(base // rows, (base + size) // rows)
                     ],
-                    axis=1,
+                    axis=0,
                 )
             )
         both = jnp.dot(
-            jnp.concatenate(hots, axis=0),
-            pieces[base : base + size, :],
+            pieces[:, base : base + size],
+            jnp.concatenate(hots, axis=1),
             preferred_element_type=F32,
         )
-        value = both[:, :lanes] + both[:, lanes:]
-        for n in range(number):
-            picked = jnp.take_along_axis(
-                value[n * LANES : (n + 1) * LANES], cells[n] & (lanes - 1), axis=1
-            )
-            found[...] = jnp.where(lane == first + n, picked, found[...])
-
-    for q in range(QUARTERS):
-        search(q * each, each, q * (height // QUARTERS), height // QUARTERS)
+        value = both[:lanes] + both[lanes:]
+        results = []
+        for n, number in enumerate(numbers):
+            lane = cell_of(jnp.broadcast_to(number, (lanes, LANES))) & (lanes - 1)
+            part = jnp.where(lane == lane_place, value[:, n * LANES : (n + 1) * LANES], 0.0)
+            results.append(jnp.sum(part, axis=0, keepdims=True))
+        return results
+
+    left = iota((1, LANES), 1) < LANES // 2
+
+    def run(full):
+        for h in range(half):
+            found = []
+            for which in range(2):
+                numbers = []
+                for part in range(2):
+                    block = lax.rem(me + (blocks - part), blocks)
+                    for pair in range(pairs):
+                        numbers.append(paired(got, block, part, h, 2 * pair)[which])
+                size = height // QUARTERS
+                found.append(
+                    search(numbers, 0, height) if full else search(numbers, (2 * h + which) * size, size)
+                )
+            for part in range(2):
+                for pair in range(pairs):
+                    a, b = (f[part * pairs + pair] for f in found)
+                    for s, value in ((0, jnp.where(left, a, b)), (1, jnp.where(left, b, a))):
+                        row = (2 * pair + s) * 2 * half + part * half + h
+                        for block in range(blocks):
+                            at = block * groups * 2 * half + row
+                            looked[at : at + 1, :] = value
+
+    run(False)
 
     @pl.when(unsorted(got))
     def _():
-        for first in range(0, count, 4):
-            search(first, 4, 0, height)
-
-    back = found[...].T
-    left = iota((1, LANES), 1) < LANES // 2
-    for part in range(2):
-        for pair in range(pairs):
-            for h in range(half):
-                n = part * pairs + pair
-                a = back[2 * h * each + n : 2 * h * each + n + 1, :]
-                b = back[(2 * h + 1) * each + n : (2 * h + 1) * each + n + 1, :]
-                for s, value in ((0, jnp.where(left, a, b)), (1, jnp.where(left, b, a))):
-                    row = (2 * pair + s) * 2 * half + part * half + h
-                    for block in range(blocks):
-                        at = block * groups * 2 * half + row
-                        looked[at : at + 1, :] = value
+        run(True)
 
 
 def pick(tables, index, row=None):
@@ -737,16 +752,13 @@
     got = exchange(sent).reshape(blocks, groups, 4 * half, LANES)
     even_x, odd_x = swaps("cut", True, even_x, odd_x)
 
-    across = jax.ShapeDtypeStruct((2 * RIM, -(-total // 8) * 8, lanes), F32)
+    strips = jax.ShapeDtypeStruct((2 * RIM, planes, lanes), F32)
     even_y, odd_y = call(
-        functools.partial(rows_kernel, rows),
-        [across, across],
-        [got, temp, kappa, even_x, odd_x],
-        left=1,
+        functools.partial(rows_kernel, rows), [strips, strips], [sent, temp, kappa], left=1
     )
     even_y, odd_y = swaps("cross", False, even_y, odd_y)
 
-    strips = jax.ShapeDtypeStruct((RIM - 1,) + across.shape[1:], F32)
+    strips = jax.ShapeDtypeStruct(((RIM - 1) * (-(-total // 8) * 8), lanes), F32)
     entries = 2 * count + 4 * count // QUARTERS
     source, even_s, odd_s = call(
         functools.partial(deposit_kernel, planes),
@@ -758,29 +770,28 @@
             pltpu.VMEM((rows, entries), jnp.int16),
         ],
     )
+    corners = jax.ShapeDtypeStruct((strips.shape[0] + 2 * RIM * PAD, lanes), F32)
+    even_s, odd_s = call(
+        functools.partial(corner_kernel, rows), [corners, corners], [even_s, odd_s, even_x, odd_x]
+    )
     even_s, odd_s = swaps("cross", False, even_s, odd_s)
 
     grid = pltpu.VMEM(flat.shape, F32)
     matrix = pltpu.VMEM((2 * lanes, 2 * lanes), BF16)
-    opened, kappa = call(
-        functools.partial(open_kernel, rows),
-        [flat, flat],
-        [temp, kappa, source, even_x, odd_x, even_y, odd_y],
-        [grid, grid, grid, matrix, matrix],
-    )
     temp, looked = call(
-        close_kernel,
+        heat_kernel,
         [
             jax.ShapeDtypeStruct((planes, rows, lanes), F32),
             jax.ShapeDtypeStruct((devices * 2 * half, LANES), F32),
         ],
-        [got, opened, kappa, source, even_s, odd_s],
+        [got, temp, kappa, source, even_x, odd_x, even_y, odd_y, even_s, odd_s],
         [
-            grid, grid, grid, grid, grid, matrix, matrix,
-            pltpu.VMEM((planes * rows, 2 * lanes), BF16),
-            pltpu.VMEM((LANES, LANES), I32),
-            pltpu.VMEM((LANES, LANES), F32),
+            grid, grid, grid, grid, grid, grid, matrix, matrix,
+            pltpu.VMEM((2 * lanes, planes * rows), BF16),
+            pltpu.VMEM((planes, rows, lanes), F32),
+            pltpu.SemaphoreType.DMA,
         ],
+        outs_left=1,
     )
     back = exchange(looked).reshape(looked.shape)
     acted = tether_acted_grain.reshape(-1, LANES)

time: 58 us -> 54.3 us (0.936)
  waiting for transfers between devices: 10.3 us -> 6.39 us
  Pallas kernels: 20.8 us -> 19.8 us
  local copies, waits for them, and re-layouts: 0.05 us -> 0.99 us
    ppermute x6, waiting for transfers between devices: 6.31 us -> 1.05 us  [swaps(): results.append(lax.ppermute(block, axis, pairs))]
    all_to_all x2, starting transfers between devices: 17.1 us -> 19.2 us  [exchange(): return lax.all_to_all(sent, BOTH, split_axis=0, concat_axis=0, tiled=True)]
    ppermute x6, starting transfers between devices: 8.68 us -> 6.84 us  [swaps(): results.append(lax.ppermute(block, axis, pairs))]
    all_to_all x2, waiting for transfers between devices: 3.98 us -> 5.34 us  [exchange(): return lax.all_to_all(sent, BOTH, split_axis=0, concat_axis=0, tiled=True)]
    pallas_call x7, Pallas kernels: 20.8 us -> 19.8 us  [call(): pl.pallas_call(kernel, out_shape=outs, in_specs=[pl.BlockSpec(memory_spac...]
    unnamed x18 -> x24, local copies, waits for them, and re-layouts: 0.05 us -> 0.99 us
  transfers between devices with their start and end apart: 8 -> 8, of which waited for: 3 -> 4; matrix products, arithmetic and copies ran while one was open for 0% -> 0% of each run, Pallas kernels for 14% -> 13%
where the time goes in v5:
time: 54.3 us; the launch traced here: 54.1 us
  starting transfers between devices  26 us (48%)
  Pallas kernels  19.8 us (36%)
  waiting for transfers between devices  6.39 us (12%)
  local copies, waits for them, and re-layouts  0.99 us (2%)
  between operations  0.86 us (2%)
    pallas_call x7, Pallas kernels, call(): pl.pallas_call(kernel, out_shape=outs, in_specs=[pl.BlockSpec(memory_spac...  19.8 us
    all_to_all x2, starting transfers between devices, exchange(): return lax.all_to_all(sent, BOTH, split_axis=0, concat_axis=0, tiled=True)  19.2 us
    ppermute x6, starting transfers between devices, swaps(): results.append(lax.ppermute(block, axis, pairs))  6.84 us
    all_to_all x2, waiting for transfers between devices, exchange(): return lax.all_to_all(sent, BOTH, split_axis=0, concat_axis=0, tiled=True)  5.34 us
  transfers between devices with their start and end apart: 8, of which 4 were waited for; matrix products, arithmetic and copies ran while one was open for 0% of the time, Pallas kernels for 13%

profile of v5, /device:TPU:0, one launch (start us, length us, event | category | flops | bytes accessed | tf_op | source)
XLA Modules:
  0.0 54.1 jit_solution(10416497984971072645)
XLA Ops:
  0.6 0.0 copy-start.1
  0.6 0.0 copy-start
  0.7 2.4 %shard_map.139 = (f32[256,128]{1,0:T(8,128)}, f32[162,128]{1,0:T(8,128)}, f32[162,128]{1,0:T(8,128)}, s32[2,8,128]{2,1,0:T(8,128)}) custom-call(f32[2048,128]{1,0:T(8,128)} %bitcast.14, f32[2048,128]{1,0:T(8,128)} %bitcast.17, s32[16,128]{1,0:T(8,128)} %bitcast.30, f32[16,128]{1,0:T(8,128)} %bitcast.31, s32[16,128]{1,0:T(8,128)} %bitcast.32, f32[3,2048]{1,0:T(4,128)} %pos.5, ...), custom_call_target="tpu_custom_call" | custom-call | tf_op jit(solution)/shard_map/pallas_call | solution.py:20
  3.0 0.0 copy-start.11
  3.1 0.0 copy-start.10
  3.1 7.3 %all-to-all-start = ((f32[32,8,128]{2,1,0:T(8,128)}), f32[32,8,128]{2,1,0:T(8,128)S(1)}, u32[]{:S(2)}, u32[]{:S(2)}) async-start(f32[32,8,128]{2,1,0:T(8,128)} %bitcast.22), calls=%async_computation | async-start | bytes 262144 | tf_op jit(solution)/shard_map/all_to_all | solution.py:750
  10.4 0.0 copy-done.1
  10.4 0.0 copy-done
  10.4 0.0 copy-start.2
  10.4 0.9 %copy-done.2 = f32[256,128]{1,0:T(8,128)S(1)} copy-done((f32[256,128]{1,0:T(8,128)S(1)}, f32[256,128]{1,0:T(8,128)}, u32[]{:S(2)}) %copy-start.2) | copy-done | bytes 131096
  11.3 1.2 %shard_map.141 = (f32[6,128,128]{2,1,0:T(8,128)}, f32[6,128,128]{2,1,0:T(8,128)}) custom-call(f32[256,128]{1,0:T(8,128)S(1)} %copy-done.2, f32[2048,128]{1,0:T(8,128)S(1)} %bitcast.15, f32[2048,128]{1,0:T(8,128)S(1)} %bitcast.18), custom_call_target="tpu_custom_call" | custom-call | tf_op jit(solution)/shard_map/pallas_call | solution.py:20
  12.5 0.3 collective-permute-start.2
  12.8 0.7 %collective-permute-start.3 = (f32[6,128,128]{2,1,0:T(8,128)}, f32[6,128,128]{2,1,0:T(8,128)S(1)}, u32[]{:S(2)}, u32[]{:S(2)}) collective-permute-start(f32[6,128,128]{2,1,0:T(8,128)} %get-tuple-element.28), channel_id=1, source_target_pairs={{1,2},{2,1},{3,4},{4,3},{5,6},{6,5},{9,10},{10,9},{11,12},{12,11},... | collective-permute-start | bytes 1179656 | tf_op jit(solution)/shard_map/ppermute | solution.py:686
  13.5 0.0 copy-done.11
  13.5 1.7 %collective-permute-start = (f32[162,128]{1,0:T(8,128)S(1)}, f32[162,128]{1,0:T(8,128)S(1)}, u32[]{:S(2)}, u32[]{:S(2)}) collective-permute-start(f32[162,128]{1,0:T(8,128)S(1)} %copy-done.11), channel_id=1, source_target_pairs={{0,8},{8,0},{16,24},{24,16},{1,9},{9,1},{17,25},{25,17},{2,10},{10... | collective-permute-start | bytes 248840 | tf_op jit(solution)/shard_map/ppermute | solution.py:686
  15.2 0.0 copy-done.10
  15.2 2.4 %collective-permute-start.1 = (f32[162,128]{1,0:T(8,128)S(1)}, f32[162,128]{1,0:T(8,128)S(1)}, u32[]{:S(2)}, u32[]{:S(2)}) collective-permute-start(f32[162,128]{1,0:T(8,128)S(1)} %copy-done.10), channel_id=1, source_target_pairs={{8,16},{16,8},{24,0},{0,24},{9,17},{17,9},{25,1},{1,25},{10,18},{1... | collective-permute-start | bytes 248840 | tf_op jit(solution)/shard_map/ppermute | solution.py:686
  17.6 1.1 %all-to-all-done = f32[32,8,128]{2,1,0:T(8,128)S(1)} async-done(((f32[32,8,128]{2,1,0:T(8,128)}), f32[32,8,128]{2,1,0:T(8,128)S(1)}, u32[]{:S(2)}, u32[]{:S(2)}) %all-to-all-start) | async-done | bytes 131104 | tf_op jit(solution)/shard_map/all_to_all | solution.py:750
  18.7 2.7 %shard_map.140 = (f32[3264,128]{1,0:T(8,128)S(1)}, f32[272,128]{1,0:T(8,128)S(1)}, f32[272,128]{1,0:T(8,128)S(1)}) custom-call(f32[4,8,8,128]{3,2,1,0:T(8,128)S(1)} %bitcast.20), custom_call_target="tpu_custom_call" | custom-call | tf_op jit(solution)/shard_map/pallas_call | solution.py:20
  21.4 0.0 collective-permute-done.even_x
  21.4 0.7 %collective-permute-done.1.odd_x = f32[162,128]{1,0:T(8,128)S(1)} collective-permute-done((f32[162,128]{1,0:T(8,128)S(1)}, f32[162,128]{1,0:T(8,128)S(1)}, u32[]{:S(2)}, u32[]{:S(2)}) %collective-permute-start.1) | collective-permute-done | bytes 82976 | tf_op jit(solution)/shard_map/ppermute | solution.py:686
  22.1 0.1 shard_map.142
  22.2 1.2 %collective-permute-start.4 = (f32[320,128]{1,0:T(8,128)S(1)}, f32[320,128]{1,0:T(8,128)S(1)}, u32[]{:S(2)}, u32[]{:S(2)}) collective-permute-start(f32[320,128]{1,0:T(8,128)S(1)} %get-tuple-element.31), channel_id=1, source_target_pairs={{0,1},{1,0},{2,3},{3,2},{4,5},{5,4},{6,7},{7,6},{8,9},{9,8},{10,11... | collective-permute-start | bytes 491528 | tf_op jit(solution)/shard_map/ppermute | solution.py:686
  23.3 0.7 %collective-permute-start.5 = (f32[320,128]{1,0:T(8,128)S(1)}, f32[320,128]{1,0:T(8,128)S(1)}, u32[]{:S(2)}, u32[]{:S(2)}) collective-permute-start(f32[320,128]{1,0:T(8,128)S(1)} %get-tuple-element.32), channel_id=1, source_target_pairs={{1,2},{2,1},{3,4},{4,3},{5,6},{6,5},{9,10},{10,9},{11,12},{12,11},... | collective-permute-start | bytes 491528 | tf_op jit(solution)/shard_map/ppermute | solution.py:686
  24.0 0.0 collective-permute-done.2.even_y
  24.0 0.0 collective-permute-done.3.odd_y
  24.0 0.3 collective-permute-done.4.even_s
  24.4 0.0 collective-permute-done.5.odd_s
  24.4 0.0 copy-start.3
  24.4 0.0 copy-start.4
  24.4 0.0 copy-start.5
  24.4 0.0 copy-start.7
  24.4 0.0 copy-start.8
  24.4 0.0 copy-start.6
  24.4 0.0 copy-start.9
  24.4 8.2 %shard_map.143 = (f32[128,16,128]{2,1,0:T(8,128)}, f32[128,128]{1,0:T(8,128)}) custom-call(f32[4,8,8,128]{3,2,1,0:T(8,128)S(1)} %bitcast.21, f32[2048,128]{1,0:T(8,128)S(1)} %bitcast.16, f32[2048,128]{1,0:T(8,128)S(1)} %bitcast.19, f32[3264,128]{1,0:T(8,128)S(1)} %get-tuple-element.24.source_own, f32[162,128]{1,0:T(8,128)S(1)} %collective-permute-done.even_x, ...), custom_call_target="tpu_custom_call" | custom-call | tf_op jit(solution)/shard_map/pallas_call | solution.py:20
  32.6 11.9 %all-to-all-start.1 = ((f32[32,4,128]{2,1,0:T(4,128)}), f32[32,4,128]{2,1,0:T(4,128)S(1)}, u32[]{:S(2)}, u32[]{:S(2)}) async-start(f32[32,4,128]{2,1,0:T(4,128)} %bitcast.8), calls=%async_computation.1 | async-start | bytes 131072 | tf_op jit(solution)/shard_map/all_to_all | solution.py:750
  44.5 0.0 copy-done.3
  44.6 0.0 copy-done.4
  44.6 0.0 copy-done.5
  44.6 0.0 copy-done.7
  44.6 0.0 copy-done.8
  44.6 3.2 %shard_map.144 = (f32[64,128]{1,0:T(8,128)S(1)}, f32[64,128]{1,0:T(8,128)S(1)}, f32[3,64,128]{2,1,0:T(8,128)S(1)}, bf16[128,8192]{1,0:T(8,128)(2,1)S(1)}, s32[2,2,2,128]{3,2,1,0:T(2,128)S(1)}) custom-call(f32[128,128]{1,0:T(8,128)} %get-tuple-element.34.after, f32[3,2048]{1,0:T(4,128)S(1)} %copy-done.3, s32[64,128]{1,0:T(8,128)S(1)} %bitcast.24, ...), custom_call_target="tpu_custom_call" | custom-call | tf_op jit(solution)/shard_map/pallas_call | solution.py:20
  47.8 4.2 %all-to-all-done.1 = f32[32,4,128]{2,1,0:T(4,128)S(1)} async-done(((f32[32,4,128]{2,1,0:T(4,128)}), f32[32,4,128]{2,1,0:T(4,128)S(1)}, u32[]{:S(2)}, u32[]{:S(2)}) %all-to-all-start.1) | async-done | bytes 65568 | tf_op jit(solution)/shard_map/all_to_all | solution.py:750
  52.0 0.0 copy-done.6
  52.0 0.0 copy-done.9
  52.0 2.1 %shard_map.145 = (f32[3,2048]{1,0:T(4,128)}, f32[3,2048]{1,0:T(4,128)}) custom-call(f32[128,128]{1,0:T(8,128)S(1)} %bitcast.23, s32[2,8,128]{2,1,0:T(8,128)S(1)} %copy-done.9, f32[3,2048]{1,0:T(4,128)S(1)} %copy-done.3, f32[3,2048]{1,0:T(4,128)S(1)} %copy-done.6, s32[64,128]{1,0:T(8,128)S(1)} %bitcast.25, s32[64,128]{1,0:T(8,128)S(1)} %bitcast.27, ...), custom_call_target="tpu_custom_call" | custom-call | tf_op jit(solution)/shard_map/pallas_call | solution.py:20
Async XLA Ops:
  0.6 9.7 %copy-start.1 = (f32[128,16,128]{2,1,0:T(8,128)S(1)}, f32[128,16,128]{2,1,0:T(8,128)}, u32[]{:S(2)}) copy-start(f32[128,16,128]{2,1,0:T(8,128)} %param.13) | copy-start | bytes 3145732
  0.6 9.7 %copy-start = (f32[128,16,128]{2,1,0:T(8,128)S(1)}, f32[128,16,128]{2,1,0:T(8,128)}, u32[]{:S(2)}) copy-start(f32[128,16,128]{2,1,0:T(8,128)} %param.12) | copy-start | bytes 3145732
  3.0 10.4 %copy-start.11 = (f32[162,128]{1,0:T(8,128)S(1)}, f32[162,128]{1,0:T(8,128)}, u32[]{:S(2)}) copy-start(f32[162,128]{1,0:T(8,128)} %get-tuple-element.25) | copy-start | bytes 248836
  3.1 12.1 %copy-start.10 = (f32[162,128]{1,0:T(8,128)S(1)}, f32[162,128]{1,0:T(8,128)}, u32[]{:S(2)}) copy-start(f32[162,128]{1,0:T(8,128)} %get-tuple-element.26) | copy-start | bytes 248836
  3.1 15.6 %all-to-all-start = ((f32[32,8,128]{2,1,0:T(8,128)}), f32[32,8,128]{2,1,0:T(8,128)S(1)}, u32[]{:S(2)}, u32[]{:S(2)}) async-start(f32[32,8,128]{2,1,0:T(8,128)} %bitcast.22), calls=%async_computation | async-start | bytes 262144 | tf_op jit(solution)/shard_map/all_to_all | solution.py:750
  10.4 0.9 %copy-start.2 = (f32[256,128]{1,0:T(8,128)S(1)}, f32[256,128]{1,0:T(8,128)}, u32[]{:S(2)}) copy-start(f32[256,128]{1,0:T(8,128)} %get-tuple-element.23.after) | copy-start | bytes 393220
  12.5 11.5 %collective-permute-start.2 = (f32[6,128,128]{2,1,0:T(8,128)}, f32[6,128,128]{2,1,0:T(8,128)S(1)}, u32[]{:S(2)}, u32[]{:S(2)}) collective-permute-start(f32[6,128,128]{2,1,0:T(8,128)} %get-tuple-element.27), channel_id=1, source_target_pairs={{0,1},{1,0},{2,3},{3,2},{4,5},{5,4},{6,7},{7,6},{8,9},{9,8},{10,11... | collective-permute-start | bytes 1179656 | tf_op jit(solution)/shard_map/ppermute | solution.py:686
  12.8 11.2 %collective-permute-start.3 = (f32[6,128,128]{2,1,0:T(8,128)}, f32[6,128,128]{2,1,0:T(8,128)S(1)}, u32[]{:S(2)}, u32[]{:S(2)}) collective-permute-start(f32[6,128,128]{2,1,0:T(8,128)} %get-tuple-element.28), channel_id=1, source_target_pairs={{1,2},{2,1},{3,4},{4,3},{5,6},{6,5},{9,10},{10,9},{11,12},{12,11},... | collective-permute-start | bytes 1179656 | tf_op jit(solution)/shard_map/ppermute | solution.py:686
  13.5 8.0 %collective-permute-start = (f32[162,128]{1,0:T(8,128)S(1)}, f32[162,128]{1,0:T(8,128)S(1)}, u32[]{:S(2)}, u32[]{:S(2)}) collective-permute-start(f32[162,128]{1,0:T(8,128)S(1)} %copy-done.11), channel_id=1, source_target_pairs={{0,8},{8,0},{16,24},{24,16},{1,9},{9,1},{17,25},{25,17},{2,10},{10... | collective-permute-start | bytes 248840 | tf_op jit(solution)/shard_map/ppermute | solution.py:686
  15.2 6.9 %collective-permute-start.1 = (f32[162,128]{1,0:T(8,128)S(1)}, f32[162,128]{1,0:T(8,128)S(1)}, u32[]{:S(2)}, u32[]{:S(2)}) collective-permute-start(f32[162,128]{1,0:T(8,128)S(1)} %copy-done.10), channel_id=1, source_target_pairs={{8,16},{16,8},{24,0},{0,24},{9,17},{17,9},{25,1},{1,25},{10,18},{1... | collective-permute-start | bytes 248840 | tf_op jit(solution)/shard_map/ppermute | solution.py:686
  22.2 2.2 %collective-permute-start.4 = (f32[320,128]{1,0:T(8,128)S(1)}, f32[320,128]{1,0:T(8,128)S(1)}, u32[]{:S(2)}, u32[]{:S(2)}) collective-permute-start(f32[320,128]{1,0:T(8,128)S(1)} %get-tuple-element.31), channel_id=1, source_target_pairs={{0,1},{1,0},{2,3},{3,2},{4,5},{5,4},{6,7},{7,6},{8,9},{9,8},{10,11... | collective-permute-start | bytes 491528 | tf_op jit(solution)/shard_map/ppermute | solution.py:686
  23.3 1.0 %collective-permute-start.5 = (f32[320,128]{1,0:T(8,128)S(1)}, f32[320,128]{1,0:T(8,128)S(1)}, u32[]{:S(2)}, u32[]{:S(2)}) collective-permute-start(f32[320,128]{1,0:T(8,128)S(1)} %get-tuple-element.32), channel_id=1, source_target_pairs={{1,2},{2,1},{3,4},{4,3},{5,6},{6,5},{9,10},{10,9},{11,12},{12,11},... | collective-permute-start | bytes 491528 | tf_op jit(solution)/shard_map/ppermute | solution.py:686
  24.4 20.2 %copy-start.3 = (f32[3,2048]{1,0:T(4,128)S(1)}, f32[3,2048]{1,0:T(4,128)}, u32[]{:S(2)}) copy-start(f32[3,2048]{1,0:T(4,128)} %pos.5) | copy-start | bytes 73732
  24.4 20.2 %copy-start.4 = (s32[8192]{0:T(1024)S(1)}, s32[8192]{0:T(1024)}, u32[]{:S(2)}) copy-start(s32[8192]{0:T(1024)} %param.19) | copy-start | bytes 98308
  24.4 20.2 %copy-start.5 = (s32[8192]{0:T(1024)S(1)}, s32[8192]{0:T(1024)}, u32[]{:S(2)}) copy-start(s32[8192]{0:T(1024)} %param.20) | copy-start | bytes 98308
  24.4 20.2 %copy-start.7 = (f32[8192]{0:T(1024)S(1)}, f32[8192]{0:T(1024)}, u32[]{:S(2)}) copy-start(f32[8192]{0:T(1024)} %param.21) | copy-start | bytes 98308
  24.4 20.2 %copy-start.8 = (s32[8192]{0:T(1024)S(1)}, s32[8192]{0:T(1024)}, u32[]{:S(2)}) copy-start(s32[8192]{0:T(1024)} %param.22) | copy-start | bytes 98308
  24.4 27.6 %copy-start.6 = (f32[3,2048]{1,0:T(4,128)S(1)}, f32[3,2048]{1,0:T(4,128)}, u32[]{:S(2)}) copy-start(f32[3,2048]{1,0:T(4,128)} %vel.1) | copy-start | bytes 73732
  24.4 27.5 %copy-start.9 = (s32[2,8,128]{2,1,0:T(8,128)S(1)}, s32[2,8,128]{2,1,0:T(8,128)}, u32[]{:S(2)}) copy-start(s32[2,8,128]{2,1,0:T(8,128)} %get-tuple-element.35.code) | copy-start | bytes 24580
  32.6 19.3 %all-to-all-start.1 = ((f32[32,4,128]{2,1,0:T(4,128)}), f32[32,4,128]{2,1,0:T(4,128)S(1)}, u32[]{:S(2)}, u32[]{:S(2)}) async-start(f32[32,4,128]{2,1,0:T(4,128)} %bitcast.8), calls=%async_computation.1 | async-start | bytes 131072 | tf_op jit(solution)/shard_map/all_to_all | solution.py:750

commit v6 on v5

--- a/solution.py
+++ b/solution.py
@@ -136,7 +136,7 @@
     return jnp.where(place < PAD - RIM, above, jnp.where(place < PAD, below, 1.0))
 
 
-def fill(flat, own, x_low, x_high, y_low, y_high, corner_low, corner_high, rows, scale):
+def fill(flat, own, x_low, x_high, y_low, y_high, rows, scale):
     pitch = rows + PAD
     planes = own.shape[0] // rows
     flat[...] = jnp.zeros(flat.shape, F32)
@@ -157,15 +157,22 @@
         below = PAD - RIM + r
         flat[pl.ds(RIM * pitch + below, planes, stride=pitch), :] = y_low[r, :, :] * scale
         flat[pl.ds((RIM + 1) * pitch + r, planes, stride=pitch), :] = y_high[r, :, :] * scale
-        for n in range(2 * RIM):
-            p = n if n < RIM else n + planes
-            flat[p * pitch + below : p * pitch + below + 1, :] = corner_low[r, n : n + 1, :] * scale
-            flat[(p + 1) * pitch + r : (p + 1) * pitch + r + 1, :] = corner_high[r, n : n + 1, :] * scale
+
+
+def fill_corners(flat, first, low, high, rows, scale):
+    pitch = rows + PAD
+    for n in range(2 * RIM):
+        block = n if n < RIM else first + n - RIM
+        for r in range(RIM):
+            below = block * pitch + PAD - RIM + r
+            above = (block + 1) * pitch + r
+            flat[below : below + 1, :] = low[r, n : n + 1, :] * scale
+            flat[above : above + 1, :] = high[r, n : n + 1, :] * scale
 
 
 def parcel_kernel(
-    temp, kappa, cells, watts, marks, pos, export, sent, even, odd, code,
-    cell_in, watt_in, mark_in, pos_in, export_in, sems,
+    rows, temp, kappa, cells, watts, marks, pos, export, sent, even, odd, even_y, odd_y, code,
+    cell_in, watt_in, mark_in, pos_in, export_in, temp_in, kappa_in, sems,
 ):
     count = pos.shape[1] // LANES
     exports = export.shape[0]
@@ -181,6 +188,7 @@
         target = pl.ds(n * wide, wide)
         for out, start in ((even, tail), (odd, height - wide - tail)):
             moves.append((field.at[pl.ds(pl.multiple_of(start, 16), wide)], out.at[target]))
+    moves += [(temp, temp_in), (kappa, kappa_in)]
     copies = [pltpu.make_async_copy(*move, sems.at[n]) for n, move in enumerate(moves)]
     for copy in copies:
         copy.start()
@@ -265,15 +273,11 @@
         out[at + count :, :] = export_in[...].astype(F32)
     for copy in copies[5:]:
         copy.wait()
-
-
-def rows_kernel(rows, after, temp, kappa, even, odd):
-    planes = temp.shape[0] // rows
     top = (1 - is_odd("cross")) * (rows - RIM)
-    for n, own in enumerate((temp, kappa)):
+    for n, own in enumerate((temp_in, kappa_in)):
         for r in range(RIM):
-            for out, first in ((even, top), (odd, rows - RIM - top)):
-                out[n * RIM + r] = own[pl.ds(first + r, planes, stride=rows), :]
+            for out, first in ((even_y, top), (odd_y, rows - RIM - top)):
+                out[n * RIM + r] = own[pl.ds(first + r, height // rows, stride=rows), :]
 
 
 def corner_kernel(rows, even_s, odd_s, even_x, odd_x, even, odd):
@@ -302,42 +306,87 @@
         return self.ref[first + (at.start or 0) : first + (self.size if at.stop is None else at.stop), :]
 
 
-def heat_kernel(
-    got, temp, kappa_own, source_own, even_x, odd_x, even_y, odd_y, even_s, odd_s,
-    temp_out, looked, source, kappa, now, then, cond, along_z, minus, plus, pieces, result, sem,
+ENDS = 2 * RIM
+
+
+def open_kernel(
+    rows, after, temp, kappa_own, even_x, odd_x, even_y, odd_y,
+    opened, kappa, ends, now, cond, along_z, minus, plus,
 ):
     lanes = temp.shape[1]
+    pitch = rows + PAD
+    planes = temp.shape[0] // rows
+    blocks = planes + 2 * RIM + 1
+    side = RIM * rows
+    x_low, x_high = low_and_high("cut", even_x, odd_x)
+    y_low, y_high = low_and_high("cross", even_y, odd_y)
+    minus[...], plus[...] = difference_matrices(lanes)
+    for n, (flat, own, scale) in enumerate(((now, temp, 1.0), (kappa, kappa_own, 0.5))):
+        beside = [half.part(slice(n * side, (n + 1) * side)) for half in (x_low, x_high)]
+        strips = [half.part(slice(n * RIM, (n + 1) * RIM)) for half in (y_low, y_high)]
+        fill(flat, own, *beside, *strips, rows, scale)
+    size = ENDS * pitch
+    ends[:size, :] = now[:size, :]
+    ends[size:, :] = now[(blocks - ENDS) * pitch : blocks * pitch, :]
+    conduct_pass(now, kappa, cond, along_z, minus, plus, 0, blocks, pitch)
+    opened[0:pitch, :] = jnp.zeros((pitch, lanes), F32)
+    opened[(blocks - 1) * pitch :, :] = jnp.zeros((opened.shape[0] - (blocks - 1) * pitch, lanes), F32)
+
+    def put(block, value):
+        opened[pl.ds(pl.multiple_of(block * pitch, 8), pitch), :] = value
+
+    flow_pass(now, cond, along_z, 1, blocks - 2, pitch, 1000, put)
+
+
+def heat_kernel(
+    got, opened, kappa_in, ends_in, source_own, even_s, odd_s,
+    temp_out, looked, source, kappa, ends, ends_kappa, now, then, cond, along_z, minus, plus, pieces,
+    result, sem,
+):
+    lanes = kappa.shape[1]
     planes, rows, _ = result.shape
     pitch = rows + PAD
     total = planes + 2 * RIM
     blocks = total + 1
-    side = RIM * rows
     wide = RIM - 1
-    x_low, x_high = low_and_high("cut", even_x, odd_x)
-    y_low, y_high = low_and_high("cross", even_y, odd_y)
     s_low, s_high = low_and_high("cross", even_s, odd_s)
     height = -(-total // 8) * 8
     minus[...], plus[...] = difference_matrices(lanes)
-    for n, (flat, own, scale) in enumerate(((now, temp, 1.0), (kappa, kappa_own, 0.5))):
-        beside = [half.part(slice(n * side, (n + 1) * side)) for half in (x_low, x_high)]
-        strips = [half.part(slice(n * RIM, (n + 1) * RIM)) for half in (y_low, y_high)]
-        corners = [Rows(half, wide * height + n * RIM * PAD, PAD) for half in (s_low, s_high)]
-        fill(flat, own, *beside, *strips, *corners, rows, scale)
     source[...] = source_own[...]
     for first, half in ((PAD - wide, s_low), (PAD + rows, s_high)):
         strips = Rows(half, 0, height)
         for r in range(wide):
             source[pl.ds(first + r, total, stride=pitch), :] = strips[r, :total, :]
     mask = rim_mask(pitch, lanes)
-    conduct_pass(now, kappa, cond, along_z, minus, plus, 0, blocks, pitch)
-    then[0:pitch, :] = jnp.zeros((pitch, lanes), F32)
-    then[(blocks - 1) * pitch :, :] = jnp.zeros((then.shape[0] - (blocks - 1) * pitch, lanes), F32)
-
-    def opening(block, value):
-        at = pl.ds(pl.multiple_of(block * pitch, 8), pitch)
-        then[at, :] = (value + source[at, :]) * mask
-
-    flow_pass(now, cond, along_z, 1, blocks - 2, pitch, 1000, opening)
+
+    corners = [
+        [Rows(half, wide * height + n * RIM * PAD, PAD) for half in (s_low, s_high)] for n in range(2)
+    ]
+    size = ENDS * pitch
+    last_end = blocks - ENDS
+    ends[: 2 * size, :] = ends_in[...]
+    ends[2 * size :, :] = jnp.zeros((pitch, lanes), F32)
+    fill_corners(ends, 2 * ENDS - RIM - 1, *corners[0], rows, 1.0)
+    kappa[...] = kappa_in[...]
+    fill_corners(kappa, blocks - RIM - 1, *corners[1], rows, 0.5)
+    ends_kappa[:size, :] = kappa[:size, :]
+    ends_kappa[size : 2 * size, :] = kappa[last_end * pitch : blocks * pitch, :]
+    conduct_pass(ends, ends_kappa, cond, along_z, minus, plus, 0, 2 * ENDS, pitch)
+    then[...] = opened[...]
+    for first, to in ((1, 1), (ENDS + 1, last_end + 1)):
+
+        def again(block, value, first=first, to=to):
+            at = pl.ds((block - first + to) * pitch, pitch)
+            then[at, :] = value
+
+        flow_pass(ends, cond, along_z, first, ENDS - 2, pitch, 1000, again)
+
+    def add_source(n, unused):
+        at = pl.ds(pl.multiple_of(n * pitch, 8), pitch)
+        then[at, :] = (then[at, :] + source[at, :]) * mask
+        return unused
+
+    lax.fori_loop(1, blocks - 1, add_source, 0, unroll=7)
     now[0:pitch, :] = jnp.zeros((pitch, lanes), F32)
     now[(blocks - 1) * pitch :, :] = jnp.zeros((now.shape[0] - (blocks - 1) * pitch, lanes), F32)
     conduct_pass(then, kappa, cond, along_z, minus, plus, 0, blocks, pitch)
@@ -716,12 +765,16 @@
     exports = exported_copies.shape[0] // LANES
     carried = jax.ShapeDtypeStruct((2 * wide + 4 * (count // LANES) + exports, LANES), F32)
     devices = blocks * groups
-    sent, even_x, odd_x, code = call(
-        parcel_kernel,
+    strips = jax.ShapeDtypeStruct((2 * RIM, planes, lanes), F32)
+    whole = pltpu.VMEM(temp.shape, F32)
+    sent, even_x, odd_x, even_y, odd_y, code = call(
+        functools.partial(parcel_kernel, rows),
         [
             jax.ShapeDtypeStruct((devices * 4 * half, LANES), F32),
             carried,
             carried,
+            strips,
+            strips,
             jax.ShapeDtypeStruct((half, groups, LANES), I32),
         ],
         [
@@ -739,7 +792,9 @@
             pltpu.VMEM((count // LANES, LANES), I32),
             pltpu.VMEM(grain_placements.shape, F32),
             pltpu.VMEM((exports, LANES), I32),
-            pltpu.SemaphoreType.DMA((9,)),
+            whole,
+            whole,
+            pltpu.SemaphoreType.DMA((11,)),
         ],
         left=7,
         limit=None,
@@ -752,10 +807,6 @@
     got = exchange(sent).reshape(blocks, groups, 4 * half, LANES)
     even_x, odd_x = swaps("cut", True, even_x, odd_x)
 
-    strips = jax.ShapeDtypeStruct((2 * RIM, planes, lanes), F32)
-    even_y, odd_y = call(
-        functools.partial(rows_kernel, rows), [strips, strips], [sent, temp, kappa], left=1
-    )
     even_y, odd_y = swaps("cross", False, even_y, odd_y)
 
     strips = jax.ShapeDtypeStruct(((RIM - 1) * (-(-total // 8) * 8), lanes), F32)
@@ -774,19 +825,29 @@
     even_s, odd_s = call(
         functools.partial(corner_kernel, rows), [corners, corners], [even_s, odd_s, even_x, odd_x]
     )
+    sent_strips = even_s
     even_s, odd_s = swaps("cross", False, even_s, odd_s)
 
     grid = pltpu.VMEM(flat.shape, F32)
     matrix = pltpu.VMEM((2 * lanes, 2 * lanes), BF16)
+    ends = jax.ShapeDtypeStruct((2 * ENDS * pitch, lanes), F32)
+    opened, kappa, ends = call(
+        functools.partial(open_kernel, rows),
+        [flat, flat, ends],
+        [sent_strips, temp, kappa, even_x, odd_x, even_y, odd_y],
+        [grid, grid, grid, matrix, matrix],
+        left=1,
+    )
+    ends_grid = pltpu.VMEM((2 * ENDS * pitch + pitch, lanes), F32)
     temp, looked = call(
         heat_kernel,
         [
             jax.ShapeDtypeStruct((planes, rows, lanes), F32),
             jax.ShapeDtypeStruct((devices * 2 * half, LANES), F32),
         ],
-        [got, temp, kappa, source, even_x, odd_x, even_y, odd_y, even_s, odd_s],
+        [got, opened, kappa, ends, source, even_s, odd_s],
         [
-            grid, grid, grid, grid, grid, grid, matrix, matrix,
+            grid, grid, ends_grid, ends_grid, grid, grid, grid, grid, matrix, matrix,
             pltpu.VMEM((2 * lanes, planes * rows), BF16),
             pltpu.VMEM((planes, rows, lanes), F32),
             pltpu.SemaphoreType.DMA,

time: 54.3 us -> 51.5 us (0.948)
  starting transfers between devices: 26 us -> 22.9 us
  waiting for transfers between devices: 6.39 us -> 7.38 us
  local copies, waits for them, and re-layouts: 0.99 us -> 0.05 us
    all_to_all x2, starting transfers between devices: 19.2 us -> 13 us  [exchange(): return lax.all_to_all(sent, BOTH, split_axis=0, concat_axis=0, tiled=True)]
    ppermute x6, starting transfers between devices: 6.84 us -> 9.89 us  [swaps(): results.append(lax.ppermute(block, axis, pairs))]
    all_to_all x2, waiting for transfers between devices: 5.34 us -> 7.36 us  [exchange(): return lax.all_to_all(sent, BOTH, split_axis=0, concat_axis=0, tiled=True)]
    ppermute x6, waiting for transfers between devices: 1.05 us -> 0.02 us  [swaps(): results.append(lax.ppermute(block, axis, pairs))]
    unnamed x24 -> x18, local copies, waits for them, and re-layouts: 0.99 us -> 0.05 us
  transfers between devices with their start and end apart: 8 -> 8, of which waited for: 4 -> 2; matrix products, arithmetic and copies ran while one was open for 0% -> 0% of each run, Pallas kernels for 13% -> 16%
where the time goes in v6:
time: 51.5 us; the launch traced here: 51.3 us
  starting transfers between devices  22.9 us (44%)
  Pallas kernels  20.1 us (39%)
  waiting for transfers between devices  7.38 us (14%)
  between operations  0.86 us (2%)
    pallas_call x7, Pallas kernels, call(): pl.pallas_call(kernel, out_shape=outs, in_specs=[pl.BlockSpec(memory_spac...  20.1 us
    all_to_all x2, starting transfers between devices, exchange(): return lax.all_to_all(sent, BOTH, split_axis=0, concat_axis=0, tiled=True)  13 us
    ppermute x6, starting transfers between devices, swaps(): results.append(lax.ppermute(block, axis, pairs))  9.89 us
    all_to_all x2, waiting for transfers between devices, exchange(): return lax.all_to_all(sent, BOTH, split_axis=0, concat_axis=0, tiled=True)  7.36 us
  transfers between devices with their start and end apart: 8, of which 2 were waited for; matrix products, arithmetic and copies ran while one was open for 0% of the time, Pallas kernels for 16%

profile of v6, /device:TPU:0, one launch (start us, length us, event | category | flops | bytes accessed | tf_op | source)
XLA Modules:
  0.0 51.3 jit_solution(6871782007332484188)
XLA Ops:
  0.6 0.0 copy-start.1
  0.6 0.0 copy-start
  0.7 3.2 %shard_map.139 = (f32[256,128]{1,0:T(8,128)}, f32[162,128]{1,0:T(8,128)}, f32[162,128]{1,0:T(8,128)}, f32[6,128,128]{2,1,0:T(8,128)}, f32[6,128,128]{2,1,0:T(8,128)}, /*index=5*/s32[2,8,128]{2,1,0:T(8,128)}) custom-call(f32[2048,128]{1,0:T(8,128)} %bitcast.14, f32[2048,128]{1,0:T(8,128)} %bitcast.16, s32[16,128]{1,0:T(8,128)} %bitcast.28, ...), custom_call_target="tpu_custom_call" | custom-call | tf_op jit(solution)/shard_map/pallas_call | solution.py:20
  3.8 7.3 %all-to-all-start = ((f32[32,8,128]{2,1,0:T(8,128)}), f32[32,8,128]{2,1,0:T(8,128)S(1)}, u32[]{:S(2)}, u32[]{:S(2)}) async-start(f32[32,8,128]{2,1,0:T(8,128)} %bitcast.27), calls=%async_computation | async-start | bytes 262144 | tf_op jit(solution)/shard_map/all_to_all | solution.py:805
  11.1 0.3 collective-permute-start.2
  11.5 0.7 %collective-permute-start.3 = (f32[6,128,128]{2,1,0:T(8,128)}, f32[6,128,128]{2,1,0:T(8,128)S(1)}, u32[]{:S(2)}, u32[]{:S(2)}) collective-permute-start(f32[6,128,128]{2,1,0:T(8,128)} %get-tuple-element.33), channel_id=1, source_target_pairs={{1,2},{2,1},{3,4},{4,3},{5,6},{6,5},{9,10},{10,9},{11,12},{12,11},... | collective-permute-start | bytes 1179656 | tf_op jit(solution)/shard_map/ppermute | solution.py:735
  12.1 1.7 %collective-permute-start = (f32[162,128]{1,0:T(8,128)}, f32[162,128]{1,0:T(8,128)S(1)}, u32[]{:S(2)}, u32[]{:S(2)}) collective-permute-start(f32[162,128]{1,0:T(8,128)} %get-tuple-element.29), channel_id=1, source_target_pairs={{0,8},{8,0},{16,24},{24,16},{1,9},{9,1},{17,25},{25,17},{2,10},{10... | collective-permute-start | bytes 248840 | tf_op jit(solution)/shard_map/ppermute | solution.py:735
  13.9 2.4 %collective-permute-start.1 = (f32[162,128]{1,0:T(8,128)}, f32[162,128]{1,0:T(8,128)S(1)}, u32[]{:S(2)}, u32[]{:S(2)}) collective-permute-start(f32[162,128]{1,0:T(8,128)} %get-tuple-element.30), channel_id=1, source_target_pairs={{8,16},{16,8},{24,0},{0,24},{9,17},{17,9},{25,1},{1,25},{10,18},{1... | collective-permute-start | bytes 248840 | tf_op jit(solution)/shard_map/ppermute | solution.py:735
  16.2 3.2 %all-to-all-done = f32[32,8,128]{2,1,0:T(8,128)S(1)} async-done(((f32[32,8,128]{2,1,0:T(8,128)}), f32[32,8,128]{2,1,0:T(8,128)S(1)}, u32[]{:S(2)}, u32[]{:S(2)}) %all-to-all-start) | async-done | bytes 131104 | tf_op jit(solution)/shard_map/all_to_all | solution.py:805
  19.4 2.7 %shard_map.140 = (f32[3264,128]{1,0:T(8,128)S(1)}, f32[272,128]{1,0:T(8,128)S(1)}, f32[272,128]{1,0:T(8,128)S(1)}) custom-call(f32[4,8,8,128]{3,2,1,0:T(8,128)S(1)} %bitcast.18), custom_call_target="tpu_custom_call" | custom-call | tf_op jit(solution)/shard_map/pallas_call | solution.py:20
  22.1 0.0 collective-permute-done.even_x
  22.1 0.0 collective-permute-done.1.odd_x
  22.1 0.1 shard_map.141
  22.2 0.7 %collective-permute-start.5 = (f32[320,128]{1,0:T(8,128)S(1)}, f32[320,128]{1,0:T(8,128)S(1)}, u32[]{:S(2)}, u32[]{:S(2)}) collective-permute-start(f32[320,128]{1,0:T(8,128)S(1)} %get-tuple-element.38), channel_id=1, source_target_pairs={{1,2},{2,1},{3,4},{4,3},{5,6},{6,5},{9,10},{10,9},{11,12},{12,11},... | collective-permute-start | bytes 491528 | tf_op jit(solution)/shard_map/ppermute | solution.py:735
  22.9 4.1 %collective-permute-start.4 = (f32[320,128]{1,0:T(8,128)S(1)}, f32[320,128]{1,0:T(8,128)S(1)}, u32[]{:S(2)}, u32[]{:S(2)}) collective-permute-start(f32[320,128]{1,0:T(8,128)S(1)} %get-tuple-element.31.after), channel_id=1, source_target_pairs={{0,1},{1,0},{2,3},{3,2},{4,5},{5,4},{6,7},{7,6},{8,9},{9,8},{10,11... | collective-permute-start | bytes 491528 | tf_op jit(solution)/shard_map/ppermute | solution.py:735
  27.0 0.0 collective-permute-done.2.even_y
  27.0 0.0 collective-permute-done.3.odd_y
  27.0 0.0 copy-done.1
  27.0 0.0 copy-done
  27.0 2.3 %shard_map.142 = (f32[3264,128]{1,0:T(8,128)S(1)}, f32[3264,128]{1,0:T(8,128)S(1)}, f32[288,128]{1,0:T(8,128)S(1)}) custom-call(f32[320,128]{1,0:T(8,128)S(1)} %get-tuple-element.31.after, f32[2048,128]{1,0:T(8,128)S(1)} %bitcast.15, f32[2048,128]{1,0:T(8,128)S(1)} %bitcast.17, f32[162,128]{1,0:T(8,128)S(1)} %collective-permute-done.even_x, ...), custom_call_target="tpu_custom_call" | custom-call | tf_op jit(solution)/shard_map/pallas_call | solution.py:20
  29.3 0.0 collective-permute-done.5.odd_s
  29.3 0.0 collective-permute-done.4.even_s
  29.3 0.0 copy-start.2
  29.3 0.0 copy-start.3
  29.3 0.0 copy-start.4
  29.4 0.0 copy-start.6
  29.4 0.0 copy-start.7
  29.4 0.0 copy-start.5
  29.4 0.0 copy-start.8
  29.4 6.6 %shard_map.143 = (f32[128,16,128]{2,1,0:T(8,128)}, f32[128,128]{1,0:T(8,128)}) custom-call(f32[4,8,8,128]{3,2,1,0:T(8,128)S(1)} %bitcast.19, f32[3264,128]{1,0:T(8,128)S(1)} %get-tuple-element.34.opened, f32[3264,128]{1,0:T(8,128)S(1)} %get-tuple-element.35.kappa_in, f32[288,128]{1,0:T(8,128)S(1)} %get-tuple-element.36.ends_in, ...), custom_call_target="tpu_custom_call" | custom-call | tf_op jit(solution)/shard_map/pallas_call | solution.py:20
  36.0 5.7 %all-to-all-start.1 = ((f32[32,4,128]{2,1,0:T(4,128)}), f32[32,4,128]{2,1,0:T(4,128)S(1)}, u32[]{:S(2)}, u32[]{:S(2)}) async-start(f32[32,4,128]{2,1,0:T(4,128)} %bitcast.8), calls=%async_computation.1 | async-start | bytes 131072 | tf_op jit(solution)/shard_map/all_to_all | solution.py:805
  41.8 0.0 copy-done.2
  41.8 0.0 copy-done.3
  41.8 0.0 copy-done.4
  41.8 0.0 copy-done.6
  41.8 0.0 copy-done.7
  41.8 3.2 %shard_map.144 = (f32[64,128]{1,0:T(8,128)S(1)}, f32[64,128]{1,0:T(8,128)S(1)}, f32[3,64,128]{2,1,0:T(8,128)S(1)}, bf16[128,8192]{1,0:T(8,128)(2,1)S(1)}, s32[2,2,2,128]{3,2,1,0:T(2,128)S(1)}) custom-call(f32[128,128]{1,0:T(8,128)} %get-tuple-element.40.after, f32[3,2048]{1,0:T(4,128)S(1)} %copy-done.2, s32[64,128]{1,0:T(8,128)S(1)} %bitcast.21, ...), custom_call_target="tpu_custom_call" | custom-call | tf_op jit(solution)/shard_map/pallas_call | solution.py:20
  45.0 4.2 %all-to-all-done.1 = f32[32,4,128]{2,1,0:T(4,128)S(1)} async-done(((f32[32,4,128]{2,1,0:T(4,128)}), f32[32,4,128]{2,1,0:T(4,128)S(1)}, u32[]{:S(2)}, u32[]{:S(2)}) %all-to-all-start.1) | async-done | bytes 65568 | tf_op jit(solution)/shard_map/all_to_all | solution.py:805
  49.2 0.0 copy-done.5
  49.2 0.0 copy-done.8
  49.2 2.1 %shard_map.145 = (f32[3,2048]{1,0:T(4,128)}, f32[3,2048]{1,0:T(4,128)}) custom-call(f32[128,128]{1,0:T(8,128)S(1)} %bitcast.20, s32[2,8,128]{2,1,0:T(8,128)S(1)} %copy-done.8, f32[3,2048]{1,0:T(4,128)S(1)} %copy-done.2, f32[3,2048]{1,0:T(4,128)S(1)} %copy-done.5, s32[64,128]{1,0:T(8,128)S(1)} %bitcast.22, s32[64,128]{1,0:T(8,128)S(1)} %bitcast.24, ...), custom_call_target="tpu_custom_call" | custom-call | tf_op jit(solution)/shard_map/pallas_call | solution.py:20
Async XLA Ops:
  0.6 26.4 %copy-start.1 = (f32[128,16,128]{2,1,0:T(8,128)S(1)}, f32[128,16,128]{2,1,0:T(8,128)}, u32[]{:S(2)}) copy-start(f32[128,16,128]{2,1,0:T(8,128)} %param.13) | copy-start | bytes 3145732
  0.6 26.4 %copy-start = (f32[128,16,128]{2,1,0:T(8,128)S(1)}, f32[128,16,128]{2,1,0:T(8,128)}, u32[]{:S(2)}) copy-start(f32[128,16,128]{2,1,0:T(8,128)} %param.12) | copy-start | bytes 3145732
  3.8 15.6 %all-to-all-start = ((f32[32,8,128]{2,1,0:T(8,128)}), f32[32,8,128]{2,1,0:T(8,128)S(1)}, u32[]{:S(2)}, u32[]{:S(2)}) async-start(f32[32,8,128]{2,1,0:T(8,128)} %bitcast.27), calls=%async_computation | async-start | bytes 262144 | tf_op jit(solution)/shard_map/all_to_all | solution.py:805
  11.1 15.9 %collective-permute-start.2 = (f32[6,128,128]{2,1,0:T(8,128)}, f32[6,128,128]{2,1,0:T(8,128)S(1)}, u32[]{:S(2)}, u32[]{:S(2)}) collective-permute-start(f32[6,128,128]{2,1,0:T(8,128)} %get-tuple-element.32), channel_id=1, source_target_pairs={{0,1},{1,0},{2,3},{3,2},{4,5},{5,4},{6,7},{7,6},{8,9},{9,8},{10,11... | collective-permute-start | bytes 1179656 | tf_op jit(solution)/shard_map/ppermute | solution.py:735
  11.5 15.5 %collective-permute-start.3 = (f32[6,128,128]{2,1,0:T(8,128)}, f32[6,128,128]{2,1,0:T(8,128)S(1)}, u32[]{:S(2)}, u32[]{:S(2)}) collective-permute-start(f32[6,128,128]{2,1,0:T(8,128)} %get-tuple-element.33), channel_id=1, source_target_pairs={{1,2},{2,1},{3,4},{4,3},{5,6},{6,5},{9,10},{10,9},{11,12},{12,11},... | collective-permute-start | bytes 1179656 | tf_op jit(solution)/shard_map/ppermute | solution.py:735
  12.1 10.0 %collective-permute-start = (f32[162,128]{1,0:T(8,128)}, f32[162,128]{1,0:T(8,128)S(1)}, u32[]{:S(2)}, u32[]{:S(2)}) collective-permute-start(f32[162,128]{1,0:T(8,128)} %get-tuple-element.29), channel_id=1, source_target_pairs={{0,8},{8,0},{16,24},{24,16},{1,9},{9,1},{17,25},{25,17},{2,10},{10... | collective-permute-start | bytes 248840 | tf_op jit(solution)/shard_map/ppermute | solution.py:735
  13.9 8.2 %collective-permute-start.1 = (f32[162,128]{1,0:T(8,128)}, f32[162,128]{1,0:T(8,128)S(1)}, u32[]{:S(2)}, u32[]{:S(2)}) collective-permute-start(f32[162,128]{1,0:T(8,128)} %get-tuple-element.30), channel_id=1, source_target_pairs={{8,16},{16,8},{24,0},{0,24},{9,17},{17,9},{25,1},{1,25},{10,18},{1... | collective-permute-start | bytes 248840 | tf_op jit(solution)/shard_map/ppermute | solution.py:735
  22.2 7.1 %collective-permute-start.5 = (f32[320,128]{1,0:T(8,128)S(1)}, f32[320,128]{1,0:T(8,128)S(1)}, u32[]{:S(2)}, u32[]{:S(2)}) collective-permute-start(f32[320,128]{1,0:T(8,128)S(1)} %get-tuple-element.38), channel_id=1, source_target_pairs={{1,2},{2,1},{3,4},{4,3},{5,6},{6,5},{9,10},{10,9},{11,12},{12,11},... | collective-permute-start | bytes 491528 | tf_op jit(solution)/shard_map/ppermute | solution.py:735
  22.9 6.4 %collective-permute-start.4 = (f32[320,128]{1,0:T(8,128)S(1)}, f32[320,128]{1,0:T(8,128)S(1)}, u32[]{:S(2)}, u32[]{:S(2)}) collective-permute-start(f32[320,128]{1,0:T(8,128)S(1)} %get-tuple-element.31.after), channel_id=1, source_target_pairs={{0,1},{1,0},{2,3},{3,2},{4,5},{5,4},{6,7},{7,6},{8,9},{9,8},{10,11... | collective-permute-start | bytes 491528 | tf_op jit(solution)/shard_map/ppermute | solution.py:735
  29.3 12.5 %copy-start.2 = (f32[3,2048]{1,0:T(4,128)S(1)}, f32[3,2048]{1,0:T(4,128)}, u32[]{:S(2)}) copy-start(f32[3,2048]{1,0:T(4,128)} %pos.5) | copy-start | bytes 73732
  29.3 12.5 %copy-start.3 = (s32[8192]{0:T(1024)S(1)}, s32[8192]{0:T(1024)}, u32[]{:S(2)}) copy-start(s32[8192]{0:T(1024)} %param.19) | copy-start | bytes 98308
  29.3 12.5 %copy-start.4 = (s32[8192]{0:T(1024)S(1)}, s32[8192]{0:T(1024)}, u32[]{:S(2)}) copy-start(s32[8192]{0:T(1024)} %param.20) | copy-start | bytes 98308
  29.4 12.5 %copy-start.6 = (f32[8192]{0:T(1024)S(1)}, f32[8192]{0:T(1024)}, u32[]{:S(2)}) copy-start(f32[8192]{0:T(1024)} %param.21) | copy-start | bytes 98308
  29.4 12.5 %copy-start.7 = (s32[8192]{0:T(1024)S(1)}, s32[8192]{0:T(1024)}, u32[]{:S(2)}) copy-start(s32[8192]{0:T(1024)} %param.22) | copy-start | bytes 98308
  29.4 19.8 %copy-start.5 = (f32[3,2048]{1,0:T(4,128)S(1)}, f32[3,2048]{1,0:T(4,128)}, u32[]{:S(2)}) copy-start(f32[3,2048]{1,0:T(4,128)} %vel.1) | copy-start | bytes 73732
  29.4 19.8 %copy-start.8 = (s32[2,8,128]{2,1,0:T(8,128)S(1)}, s32[2,8,128]{2,1,0:T(8,128)}, u32[]{:S(2)}) copy-start(s32[2,8,128]{2,1,0:T(8,128)} %get-tuple-element.41.code) | copy-start | bytes 24580
  36.0 13.2 %all-to-all-start.1 = ((f32[32,4,128]{2,1,0:T(4,128)}), f32[32,4,128]{2,1,0:T(4,128)S(1)}, u32[]{:S(2)}, u32[]{:S(2)}) async-start(f32[32,4,128]{2,1,0:T(4,128)} %bitcast.8), calls=%async_computation.1 | async-start | bytes 131072 | tf_op jit(solution)/shard_map/all_to_all | solution.py:805

commit v7 on v6

--- a/solution.py
+++ b/solution.py
@@ -176,7 +176,7 @@
 ):
     count = pos.shape[1] // LANES
     exports = export.shape[0]
-    wide = (even.shape[0] - 4 * count - exports) // 2
+    wide = (even.shape[0] - 4 * exports) // 2
     height, lanes = temp.shape
     patch = height * lanes
     half, groups, _ = code.shape
@@ -262,15 +262,17 @@
                     sent[at, :] = value[:, h * LANES : (h + 1) * LANES]
     for copy in copies[3:5]:
         copy.wait()
+    index = export_in[...]
+    codes = [
+        mark[j : j + 1, h * LANES : (h + 1) * LANES].astype(F32)
+        for j in range(groups)
+        for h in range(half)
+    ]
+    ghost = pick([rows_of(pos_in, ch) for ch in range(3)] + [codes], index)
+    ghost[3] = (index // cap * (2 * cap) + ghost[3].astype(I32)).astype(F32)
     for out in (even, odd):
-        for ch in range(3):
-            for r in range(count):
-                at = 2 * wide + ch * count + r
-                out[at : at + 1, :] = pos_in[ch : ch + 1, r * LANES : (r + 1) * LANES]
-        at = 2 * wide + 3 * count
-        for h in range(half):
-            out[pl.ds(at + h, groups, stride=half), :] = code[h].astype(F32)
-        out[at + count :, :] = export_in[...].astype(F32)
+        for n, value in enumerate(ghost):
+            out[2 * wide + n * exports : 2 * wide + (n + 1) * exports, :] = value
     for copy in copies[5:]:
         copy.wait()
     top = (1 - is_odd("cross")) * (rows - RIM)
@@ -372,21 +374,20 @@
     ends_kappa[:size, :] = kappa[:size, :]
     ends_kappa[size : 2 * size, :] = kappa[last_end * pitch : blocks * pitch, :]
     conduct_pass(ends, ends_kappa, cond, along_z, minus, plus, 0, 2 * ENDS, pitch)
-    then[...] = opened[...]
+    then[0:pitch, :] = jnp.zeros((pitch, lanes), F32)
+    then[(blocks - 1) * pitch :, :] = jnp.zeros((then.shape[0] - (blocks - 1) * pitch, lanes), F32)
+    for n in range(1, blocks - 1):
+        if not (1 <= n < ENDS - 1 or last_end + 1 <= n):
+            at = pl.ds(n * pitch, pitch)
+            then[at, :] = (opened[at, :] + source[at, :]) * mask
     for first, to in ((1, 1), (ENDS + 1, last_end + 1)):
 
         def again(block, value, first=first, to=to):
             at = pl.ds((block - first + to) * pitch, pitch)
-            then[at, :] = value
+            then[at, :] = (value + source[at, :]) * mask
 
         flow_pass(ends, cond, along_z, first, ENDS - 2, pitch, 1000, again)
 
-    def add_source(n, unused):
-        at = pl.ds(pl.multiple_of(n * pitch, 8), pitch)
-        then[at, :] = (then[at, :] + source[at, :]) * mask
-        return unused
-
-    lax.fori_loop(1, blocks - 1, add_source, 0, unroll=7)
     now[0:pitch, :] = jnp.zeros((pitch, lanes), F32)
     now[(blocks - 1) * pitch :, :] = jnp.zeros((now.shape[0] - (blocks - 1) * pitch, lanes), F32)
     conduct_pass(then, kappa, cond, along_z, minus, plus, 0, blocks, pitch)
@@ -604,9 +605,8 @@
         run(True)
 
 
-def pick(tables, index, row=None):
-    if row is None:
-        row = lax.shift_right_logical(index, 7)
+def pick(tables, index):
+    row = lax.shift_right_logical(index, 7)
     lane = index & (LANES - 1)
     results = [jnp.zeros(index.shape, F32) for _ in tables]
     for r in range(len(tables[0])):
@@ -622,24 +622,15 @@
 
 
 def stretch_kernel(
-    side, half, after, pos, acted, other, gap, snapped, even_x, odd_x, base, slope, delta, hot, ghost,
+    side, after, pos, acted, other, gap, snapped, even_x, odd_x, base, slope, delta, hot, ghost,
 ):
-    count = pos.shape[1] // LANES
+    exports = ghost.shape[1]
     low_ghost, high_ghost = low_and_high("cut", even_x, odd_x)
 
     def ghosts(n, ref):
-        places = side + 4 * count
-        tables = [
-            [ref[side + ch * count + r : side + ch * count + r + 1, :] for r in range(count)]
-            for ch in range(4)
-        ]
-        index = ref[places:, :].astype(I32)
-        found = pick(tables, index)
-        code = found.pop().astype(I32)
-        group = index // (half * LANES)
-        ghost[n, 0] = group * (2 * half) + lax.shift_right_logical(code, 7)
-        ghost[n, 1] = code & (LANES - 1)
-        return [[f[r : r + 1] for r in range(f.shape[0])] for f in found]
+        ghost[n] = ref[side + 3 * exports : side + 4 * exports, :].astype(I32)
+        places = ref[side : side + 3 * exports, :]
+        return [[places[ch * exports + r : ch * exports + r + 1] for r in range(exports)] for ch in range(3)]
 
     own = [rows_of(pos, ch) for ch in range(3)]
     low = ghosts(0, low_ghost)
@@ -682,7 +673,7 @@
     def ghosts(n, distance):
         rows = slots(distance)
         table = [rows[k][j : j + 1] for j in range(groups) for k in range(double)]
-        found = pick([table], ghost[n, 1], ghost[n, 0])[0]
+        found = pick([table], ghost[n])[0]
         return [found[r : r + 1] for r in range(found.shape[0])]
 
     rows = slots(0)
@@ -763,7 +754,7 @@
     wide = RIM * rows
 
     exports = exported_copies.shape[0] // LANES
-    carried = jax.ShapeDtypeStruct((2 * wide + 4 * (count // LANES) + exports, LANES), F32)
+    carried = jax.ShapeDtypeStruct((2 * wide + 4 * exports, LANES), F32)
     devices = blocks * groups
     strips = jax.ShapeDtypeStruct((2 * RIM, planes, lanes), F32)
     whole = pltpu.VMEM(temp.shape, F32)
@@ -859,13 +850,13 @@
     other = tether_other_grain.reshape(-1, LANES)
     entry = jax.ShapeDtypeStruct(acted.shape, F32)
     base, slope, delta, hot, ghost = call(
-        functools.partial(stretch_kernel, 2 * wide, half),
+        functools.partial(stretch_kernel, 2 * wide),
         [
             entry,
             entry,
             jax.ShapeDtypeStruct((3,) + acted.shape, F32),
             jax.ShapeDtypeStruct((LANES, acted.size), BF16),
-            jax.ShapeDtypeStruct((2, 2, exports, LANES), I32),
+            jax.ShapeDtypeStruct((2, exports, LANES), I32),
         ],
         [
             looked,

time: 51.5 us -> 50.4 us (0.979)
  Pallas kernels: 20.1 us -> 19.4 us
  starting transfers between devices: 22.9 us -> 22.2 us
    ppermute x6, starting transfers between devices: 9.89 us -> 8.64 us  [swaps(): results.append(lax.ppermute(block, axis, pairs))]
    pallas_call x7, Pallas kernels: 20.1 us -> 19.4 us  [call(): pl.pallas_call(kernel, out_shape=outs, in_specs=[pl.BlockSpec(memory_spac...]
    all_to_all x2, starting transfers between devices: 13 us -> 13.6 us  [exchange(): return lax.all_to_all(sent, BOTH, split_axis=0, concat_axis=0, tiled=True)]
where the time goes in v7:
time: 50.4 us; the launch traced here: 50.1 us
  starting transfers between devices  22.2 us (44%)
  Pallas kernels  19.4 us (38%)
  waiting for transfers between devices  7.55 us (15%)
  between operations  0.86 us (2%)
    pallas_call x7, Pallas kernels, call(): pl.pallas_call(kernel, out_shape=outs, in_specs=[pl.BlockSpec(memory_spac...  19.4 us
    all_to_all x2, starting transfers between devices, exchange(): return lax.all_to_all(sent, BOTH, split_axis=0, concat_axis=0, tiled=True)  13.6 us
    ppermute x6, starting transfers between devices, swaps(): results.append(lax.ppermute(block, axis, pairs))  8.64 us
    all_to_all x2, waiting for transfers between devices, exchange(): return lax.all_to_all(sent, BOTH, split_axis=0, concat_axis=0, tiled=True)  7.53 us
  transfers between devices with their start and end apart: 8, of which 2 were waited for; matrix products, arithmetic and copies ran while one was open for 0% of the time, Pallas kernels for 16%

profile of v7, /device:TPU:0, one launch (start us, length us, event | category | flops | bytes accessed | tf_op | source)
XLA Modules:
  0.0 50.1 jit_solution(4847845292813815811)
XLA Ops:
  0.6 0.0 copy-start.1
  0.6 0.0 copy-start
  0.7 3.2 %shard_map.139 = (f32[256,128]{1,0:T(8,128)}, f32[104,128]{1,0:T(8,128)}, f32[104,128]{1,0:T(8,128)}, f32[6,128,128]{2,1,0:T(8,128)}, f32[6,128,128]{2,1,0:T(8,128)}, /*index=5*/s32[2,8,128]{2,1,0:T(8,128)}) custom-call(f32[2048,128]{1,0:T(8,128)} %bitcast.14, f32[2048,128]{1,0:T(8,128)} %bitcast.16, s32[16,128]{1,0:T(8,128)} %bitcast.28, ...), custom_call_target="tpu_custom_call" | custom-call | tf_op jit(solution)/shard_map/pallas_call | solution.py:20
  3.8 7.3 %all-to-all-start = ((f32[32,8,128]{2,1,0:T(8,128)}), f32[32,8,128]{2,1,0:T(8,128)S(1)}, u32[]{:S(2)}, u32[]{:S(2)}) async-start(f32[32,8,128]{2,1,0:T(8,128)} %bitcast.27), calls=%async_computation | async-start | bytes 262144 | tf_op jit(solution)/shard_map/all_to_all | solution.py:796
  11.1 0.3 collective-permute-start.2
  11.5 0.7 %collective-permute-start.3 = (f32[6,128,128]{2,1,0:T(8,128)}, f32[6,128,128]{2,1,0:T(8,128)S(1)}, u32[]{:S(2)}, u32[]{:S(2)}) collective-permute-start(f32[6,128,128]{2,1,0:T(8,128)} %get-tuple-element.33), channel_id=1, source_target_pairs={{1,2},{2,1},{3,4},{4,3},{5,6},{6,5},{9,10},{10,9},{11,12},{12,11},... | collective-permute-start | bytes 1179656 | tf_op jit(solution)/shard_map/ppermute | solution.py:726
  12.1 1.7 %collective-permute-start = (f32[104,128]{1,0:T(8,128)}, f32[104,128]{1,0:T(8,128)S(1)}, u32[]{:S(2)}, u32[]{:S(2)}) collective-permute-start(f32[104,128]{1,0:T(8,128)} %get-tuple-element.29), channel_id=1, source_target_pairs={{0,8},{8,0},{16,24},{24,16},{1,9},{9,1},{17,25},{25,17},{2,10},{10... | collective-permute-start | bytes 159752 | tf_op jit(solution)/shard_map/ppermute | solution.py:726
  13.9 2.4 %collective-permute-start.1 = (f32[104,128]{1,0:T(8,128)}, f32[104,128]{1,0:T(8,128)S(1)}, u32[]{:S(2)}, u32[]{:S(2)}) collective-permute-start(f32[104,128]{1,0:T(8,128)} %get-tuple-element.30), channel_id=1, source_target_pairs={{8,16},{16,8},{24,0},{0,24},{9,17},{17,9},{25,1},{1,25},{10,18},{1... | collective-permute-start | bytes 159752 | tf_op jit(solution)/shard_map/ppermute | solution.py:726
  16.2 3.2 %all-to-all-done = f32[32,8,128]{2,1,0:T(8,128)S(1)} async-done(((f32[32,8,128]{2,1,0:T(8,128)}), f32[32,8,128]{2,1,0:T(8,128)S(1)}, u32[]{:S(2)}, u32[]{:S(2)}) %all-to-all-start) | async-done | bytes 131104 | tf_op jit(solution)/shard_map/all_to_all | solution.py:796
  19.4 2.7 %shard_map.140 = (f32[3264,128]{1,0:T(8,128)S(1)}, f32[272,128]{1,0:T(8,128)S(1)}, f32[272,128]{1,0:T(8,128)S(1)}) custom-call(f32[4,8,8,128]{3,2,1,0:T(8,128)S(1)} %bitcast.18), custom_call_target="tpu_custom_call" | custom-call | tf_op jit(solution)/shard_map/pallas_call | solution.py:20
  22.1 0.0 collective-permute-done.even_x
  22.1 0.0 collective-permute-done.1.odd_x
  22.1 0.1 shard_map.141
  22.2 0.7 %collective-permute-start.5 = (f32[320,128]{1,0:T(8,128)S(1)}, f32[320,128]{1,0:T(8,128)S(1)}, u32[]{:S(2)}, u32[]{:S(2)}) collective-permute-start(f32[320,128]{1,0:T(8,128)S(1)} %get-tuple-element.38), channel_id=1, source_target_pairs={{1,2},{2,1},{3,4},{4,3},{5,6},{6,5},{9,10},{10,9},{11,12},{12,11},... | collective-permute-start | bytes 491528 | tf_op jit(solution)/shard_map/ppermute | solution.py:726
  22.9 2.9 %collective-permute-start.4 = (f32[320,128]{1,0:T(8,128)S(1)}, f32[320,128]{1,0:T(8,128)S(1)}, u32[]{:S(2)}, u32[]{:S(2)}) collective-permute-start(f32[320,128]{1,0:T(8,128)S(1)} %get-tuple-element.31.after), channel_id=1, source_target_pairs={{0,1},{1,0},{2,3},{3,2},{4,5},{5,4},{6,7},{7,6},{8,9},{9,8},{10,11... | collective-permute-start | bytes 491528 | tf_op jit(solution)/shard_map/ppermute | solution.py:726
  25.7 0.0 collective-permute-done.2.even_y
  25.8 0.0 collective-permute-done.3.odd_y
  25.8 0.0 copy-done.1
  25.8 0.0 copy-done
  25.8 2.3 %shard_map.142 = (f32[3264,128]{1,0:T(8,128)S(1)}, f32[3264,128]{1,0:T(8,128)S(1)}, f32[288,128]{1,0:T(8,128)S(1)}) custom-call(f32[320,128]{1,0:T(8,128)S(1)} %get-tuple-element.31.after, f32[2048,128]{1,0:T(8,128)S(1)} %bitcast.15, f32[2048,128]{1,0:T(8,128)S(1)} %bitcast.17, f32[104,128]{1,0:T(8,128)S(1)} %collective-permute-done.even_x, ...), custom_call_target="tpu_custom_call" | custom-call | tf_op jit(solution)/shard_map/pallas_call | solution.py:20
  28.0 0.0 collective-permute-done.5.odd_s
  28.1 0.0 collective-permute-done.4.even_s
  28.1 0.0 copy-start.2
  28.1 0.0 copy-start.3
  28.1 0.0 copy-start.4
  28.1 0.0 copy-start.6
  28.1 0.0 copy-start.7
  28.1 0.0 copy-start.5
  28.1 0.0 copy-start.8
  28.1 6.1 %shard_map.143 = (f32[128,16,128]{2,1,0:T(8,128)}, f32[128,128]{1,0:T(8,128)}) custom-call(f32[4,8,8,128]{3,2,1,0:T(8,128)S(1)} %bitcast.19, f32[3264,128]{1,0:T(8,128)S(1)} %get-tuple-element.34.opened, f32[3264,128]{1,0:T(8,128)S(1)} %get-tuple-element.35.kappa_in, f32[288,128]{1,0:T(8,128)S(1)} %get-tuple-element.36.ends_in, ...), custom_call_target="tpu_custom_call" | custom-call | tf_op jit(solution)/shard_map/pallas_call | solution.py:20
  34.3 6.3 %all-to-all-start.1 = ((f32[32,4,128]{2,1,0:T(4,128)}), f32[32,4,128]{2,1,0:T(4,128)S(1)}, u32[]{:S(2)}, u32[]{:S(2)}) async-start(f32[32,4,128]{2,1,0:T(4,128)} %bitcast.8), calls=%async_computation.1 | async-start | bytes 131072 | tf_op jit(solution)/shard_map/all_to_all | solution.py:796
  40.6 0.0 copy-done.2
  40.6 0.0 copy-done.3
  40.6 0.0 copy-done.4
  40.6 0.0 copy-done.6
  40.6 0.0 copy-done.7
  40.6 3.0 %shard_map.144 = (f32[64,128]{1,0:T(8,128)S(1)}, f32[64,128]{1,0:T(8,128)S(1)}, f32[3,64,128]{2,1,0:T(8,128)S(1)}, bf16[128,8192]{1,0:T(8,128)(2,1)S(1)}, s32[2,2,128]{2,1,0:T(2,128)S(1)}) custom-call(f32[128,128]{1,0:T(8,128)} %get-tuple-element.40.after, f32[3,2048]{1,0:T(4,128)S(1)} %copy-done.2, s32[64,128]{1,0:T(8,128)S(1)} %bitcast.21, ...), custom_call_target="tpu_custom_call" | custom-call | tf_op jit(solution)/shard_map/pallas_call | solution.py:20
  43.6 4.4 %all-to-all-done.1 = f32[32,4,128]{2,1,0:T(4,128)S(1)} async-done(((f32[32,4,128]{2,1,0:T(4,128)}), f32[32,4,128]{2,1,0:T(4,128)S(1)}, u32[]{:S(2)}, u32[]{:S(2)}) %all-to-all-start.1) | async-done | bytes 65568 | tf_op jit(solution)/shard_map/all_to_all | solution.py:796
  48.0 0.0 copy-done.5
  48.0 0.0 copy-done.8
  48.0 2.1 %shard_map.145 = (f32[3,2048]{1,0:T(4,128)}, f32[3,2048]{1,0:T(4,128)}) custom-call(f32[128,128]{1,0:T(8,128)S(1)} %bitcast.20, s32[2,8,128]{2,1,0:T(8,128)S(1)} %copy-done.8, f32[3,2048]{1,0:T(4,128)S(1)} %copy-done.2, f32[3,2048]{1,0:T(4,128)S(1)} %copy-done.5, s32[64,128]{1,0:T(8,128)S(1)} %bitcast.22, s32[64,128]{1,0:T(8,128)S(1)} %bitcast.24, ...), custom_call_target="tpu_custom_call" | custom-call | tf_op jit(solution)/shard_map/pallas_call | solution.py:20
Async XLA Ops:
  0.6 25.1 %copy-start.1 = (f32[128,16,128]{2,1,0:T(8,128)S(1)}, f32[128,16,128]{2,1,0:T(8,128)}, u32[]{:S(2)}) copy-start(f32[128,16,128]{2,1,0:T(8,128)} %param.13) | copy-start | bytes 3145732
  0.6 25.1 %copy-start = (f32[128,16,128]{2,1,0:T(8,128)S(1)}, f32[128,16,128]{2,1,0:T(8,128)}, u32[]{:S(2)}) copy-start(f32[128,16,128]{2,1,0:T(8,128)} %param.12) | copy-start | bytes 3145732
  3.8 15.6 %all-to-all-start = ((f32[32,8,128]{2,1,0:T(8,128)}), f32[32,8,128]{2,1,0:T(8,128)S(1)}, u32[]{:S(2)}, u32[]{:S(2)}) async-start(f32[32,8,128]{2,1,0:T(8,128)} %bitcast.27), calls=%async_computation | async-start | bytes 262144 | tf_op jit(solution)/shard_map/all_to_all | solution.py:796
  11.1 14.6 %collective-permute-start.2 = (f32[6,128,128]{2,1,0:T(8,128)}, f32[6,128,128]{2,1,0:T(8,128)S(1)}, u32[]{:S(2)}, u32[]{:S(2)}) collective-permute-start(f32[6,128,128]{2,1,0:T(8,128)} %get-tuple-element.32), channel_id=1, source_target_pairs={{0,1},{1,0},{2,3},{3,2},{4,5},{5,4},{6,7},{7,6},{8,9},{9,8},{10,11... | collective-permute-start | bytes 1179656 | tf_op jit(solution)/shard_map/ppermute | solution.py:726
  11.5 14.3 %collective-permute-start.3 = (f32[6,128,128]{2,1,0:T(8,128)}, f32[6,128,128]{2,1,0:T(8,128)S(1)}, u32[]{:S(2)}, u32[]{:S(2)}) collective-permute-start(f32[6,128,128]{2,1,0:T(8,128)} %get-tuple-element.33), channel_id=1, source_target_pairs={{1,2},{2,1},{3,4},{4,3},{5,6},{6,5},{9,10},{10,9},{11,12},{12,11},... | collective-permute-start | bytes 1179656 | tf_op jit(solution)/shard_map/ppermute | solution.py:726
  12.1 10.0 %collective-permute-start = (f32[104,128]{1,0:T(8,128)}, f32[104,128]{1,0:T(8,128)S(1)}, u32[]{:S(2)}, u32[]{:S(2)}) collective-permute-start(f32[104,128]{1,0:T(8,128)} %get-tuple-element.29), channel_id=1, source_target_pairs={{0,8},{8,0},{16,24},{24,16},{1,9},{9,1},{17,25},{25,17},{2,10},{10... | collective-permute-start | bytes 159752 | tf_op jit(solution)/shard_map/ppermute | solution.py:726
  13.9 8.2 %collective-permute-start.1 = (f32[104,128]{1,0:T(8,128)}, f32[104,128]{1,0:T(8,128)S(1)}, u32[]{:S(2)}, u32[]{:S(2)}) collective-permute-start(f32[104,128]{1,0:T(8,128)} %get-tuple-element.30), channel_id=1, source_target_pairs={{8,16},{16,8},{24,0},{0,24},{9,17},{17,9},{25,1},{1,25},{10,18},{1... | collective-permute-start | bytes 159752 | tf_op jit(solution)/shard_map/ppermute | solution.py:726
  22.2 5.9 %collective-permute-start.5 = (f32[320,128]{1,0:T(8,128)S(1)}, f32[320,128]{1,0:T(8,128)S(1)}, u32[]{:S(2)}, u32[]{:S(2)}) collective-permute-start(f32[320,128]{1,0:T(8,128)S(1)} %get-tuple-element.38), channel_id=1, source_target_pairs={{1,2},{2,1},{3,4},{4,3},{5,6},{6,5},{9,10},{10,9},{11,12},{12,11},... | collective-permute-start | bytes 491528 | tf_op jit(solution)/shard_map/ppermute | solution.py:726
  22.9 5.2 %collective-permute-start.4 = (f32[320,128]{1,0:T(8,128)S(1)}, f32[320,128]{1,0:T(8,128)S(1)}, u32[]{:S(2)}, u32[]{:S(2)}) collective-permute-start(f32[320,128]{1,0:T(8,128)S(1)} %get-tuple-element.31.after), channel_id=1, source_target_pairs={{0,1},{1,0},{2,3},{3,2},{4,5},{5,4},{6,7},{7,6},{8,9},{9,8},{10,11... | collective-permute-start | bytes 491528 | tf_op jit(solution)/shard_map/ppermute | solution.py:726
  28.1 12.5 %copy-start.2 = (f32[3,2048]{1,0:T(4,128)S(1)}, f32[3,2048]{1,0:T(4,128)}, u32[]{:S(2)}) copy-start(f32[3,2048]{1,0:T(4,128)} %pos.5) | copy-start | bytes 73732
  28.1 12.5 %copy-start.3 = (s32[8192]{0:T(1024)S(1)}, s32[8192]{0:T(1024)}, u32[]{:S(2)}) copy-start(s32[8192]{0:T(1024)} %param.19) | copy-start | bytes 98308
  28.1 12.5 %copy-start.4 = (s32[8192]{0:T(1024)S(1)}, s32[8192]{0:T(1024)}, u32[]{:S(2)}) copy-start(s32[8192]{0:T(1024)} %param.20) | copy-start | bytes 98308
  28.1 12.5 %copy-start.6 = (f32[8192]{0:T(1024)S(1)}, f32[8192]{0:T(1024)}, u32[]{:S(2)}) copy-start(f32[8192]{0:T(1024)} %param.21) | copy-start | bytes 98308
  28.1 12.5 %copy-start.7 = (s32[8192]{0:T(1024)S(1)}, s32[8192]{0:T(1024)}, u32[]{:S(2)}) copy-start(s32[8192]{0:T(1024)} %param.22) | copy-start | bytes 98308
  28.1 19.9 %copy-start.5 = (f32[3,2048]{1,0:T(4,128)S(1)}, f32[3,2048]{1,0:T(4,128)}, u32[]{:S(2)}) copy-start(f32[3,2048]{1,0:T(4,128)} %vel.1) | copy-start | bytes 73732
  28.1 19.9 %copy-start.8 = (s32[2,8,128]{2,1,0:T(8,128)S(1)}, s32[2,8,128]{2,1,0:T(8,128)}, u32[]{:S(2)}) copy-start(s32[2,8,128]{2,1,0:T(8,128)} %get-tuple-element.41.code) | copy-start | bytes 24580
  34.3 13.7 %all-to-all-start.1 = ((f32[32,4,128]{2,1,0:T(4,128)}), f32[32,4,128]{2,1,0:T(4,128)S(1)}, u32[]{:S(2)}, u32[]{:S(2)}) async-start(f32[32,4,128]{2,1,0:T(4,128)} %bitcast.8), calls=%async_computation.1 | async-start | bytes 131072 | tf_op jit(solution)/shard_map/all_to_all | solution.py:796

commit v8 on v7

--- a/solution.py
+++ b/solution.py
@@ -485,8 +485,12 @@
         sides(pair, 0, QUARTERS - 1)
         return unused
 
-    lax.fori_loop(0, pairs, fill_pair, 0)
-    source[...] = jnp.zeros(source.shape, F32)
+    lax.fori_loop(0, pairs, fill_pair, 0, unroll=True)
+    blocks_all = source.shape[0] // pitch
+    for n in range(blocks_all):
+        inner = 1 <= n < planes + 2 * RIM - 1
+        end = PAD if inner else pitch
+        source[n * pitch : n * pitch + end, :] = jnp.zeros((end, lanes), F32)
 
     def product(first, base, count, columns, added=False):
         where_y = across[:, columns]

time: 50.4 us -> 50.4 us (level)
  starting transfers between devices: 22.2 us -> 23.2 us
  Pallas kernels: 19.4 us -> 18.5 us
    ppermute x6, starting transfers between devices: 8.64 us -> 9.57 us  [swaps(): results.append(lax.ppermute(block, axis, pairs))]
    pallas_call x7, Pallas kernels: 19.4 us -> 18.5 us  [call(): pl.pallas_call(kernel, out_shape=outs, in_specs=[pl.BlockSpec(memory_spac...]
  transfers between devices with their start and end apart: 8 -> 8, of which waited for: 2 -> 2; matrix products, arithmetic and copies ran while one was open for 0% -> 0% of each run, Pallas kernels for 16% -> 14%
where the time goes in v8:
time: 50.4 us; the launch traced here: 50.1 us
  starting transfers between devices  23.2 us (46%)
  Pallas kernels  18.5 us (37%)
  waiting for transfers between devices  7.55 us (15%)
  between operations  0.86 us (2%)
    pallas_call x7, Pallas kernels, call(): pl.pallas_call(kernel, out_shape=outs, in_specs=[pl.BlockSpec(memory_spac...  18.5 us
    all_to_all x2, starting transfers between devices, exchange(): return lax.all_to_all(sent, BOTH, split_axis=0, concat_axis=0, tiled=True)  13.6 us
    ppermute x6, starting transfers between devices, swaps(): results.append(lax.ppermute(block, axis, pairs))  9.57 us
    all_to_all x2, waiting for transfers between devices, exchange(): return lax.all_to_all(sent, BOTH, split_axis=0, concat_axis=0, tiled=True)  7.53 us
  transfers between devices with their start and end apart: 8, of which 2 were waited for; matrix products, arithmetic and copies ran while one was open for 0% of the time, Pallas kernels for 14%

profile of v8, /device:TPU:0, one launch (start us, length us, event | category | flops | bytes accessed | tf_op | source)
XLA Modules:
  0.0 50.1 jit_solution(11754999015029063380)
XLA Ops:
  0.6 0.0 copy-start.1
  0.6 0.0 copy-start
  0.7 3.2 %shard_map.139 = (f32[256,128]{1,0:T(8,128)}, f32[104,128]{1,0:T(8,128)}, f32[104,128]{1,0:T(8,128)}, f32[6,128,128]{2,1,0:T(8,128)}, f32[6,128,128]{2,1,0:T(8,128)}, /*index=5*/s32[2,8,128]{2,1,0:T(8,128)}) custom-call(f32[2048,128]{1,0:T(8,128)} %bitcast.14, f32[2048,128]{1,0:T(8,128)} %bitcast.16, s32[16,128]{1,0:T(8,128)} %bitcast.28, ...), custom_call_target="tpu_custom_call" | custom-call | tf_op jit(solution)/shard_map/pallas_call | solution.py:20
  3.8 7.3 %all-to-all-start = ((f32[32,8,128]{2,1,0:T(8,128)}), f32[32,8,128]{2,1,0:T(8,128)S(1)}, u32[]{:S(2)}, u32[]{:S(2)}) async-start(f32[32,8,128]{2,1,0:T(8,128)} %bitcast.27), calls=%async_computation | async-start | bytes 262144 | tf_op jit(solution)/shard_map/all_to_all | solution.py:800
  11.1 0.3 collective-permute-start.2
  11.5 0.7 %collective-permute-start.3 = (f32[6,128,128]{2,1,0:T(8,128)}, f32[6,128,128]{2,1,0:T(8,128)S(1)}, u32[]{:S(2)}, u32[]{:S(2)}) collective-permute-start(f32[6,128,128]{2,1,0:T(8,128)} %get-tuple-element.33), channel_id=1, source_target_pairs={{1,2},{2,1},{3,4},{4,3},{5,6},{6,5},{9,10},{10,9},{11,12},{12,11},... | collective-permute-start | bytes 1179656 | tf_op jit(solution)/shard_map/ppermute | solution.py:730
  12.1 1.7 %collective-permute-start = (f32[104,128]{1,0:T(8,128)}, f32[104,128]{1,0:T(8,128)S(1)}, u32[]{:S(2)}, u32[]{:S(2)}) collective-permute-start(f32[104,128]{1,0:T(8,128)} %get-tuple-element.29), channel_id=1, source_target_pairs={{0,8},{8,0},{16,24},{24,16},{1,9},{9,1},{17,25},{25,17},{2,10},{10... | collective-permute-start | bytes 159752 | tf_op jit(solution)/shard_map/ppermute | solution.py:730
  13.9 2.4 %collective-permute-start.1 = (f32[104,128]{1,0:T(8,128)}, f32[104,128]{1,0:T(8,128)S(1)}, u32[]{:S(2)}, u32[]{:S(2)}) collective-permute-start(f32[104,128]{1,0:T(8,128)} %get-tuple-element.30), channel_id=1, source_target_pairs={{8,16},{16,8},{24,0},{0,24},{9,17},{17,9},{25,1},{1,25},{10,18},{1... | collective-permute-start | bytes 159752 | tf_op jit(solution)/shard_map/ppermute | solution.py:730
  16.2 3.2 %all-to-all-done = f32[32,8,128]{2,1,0:T(8,128)S(1)} async-done(((f32[32,8,128]{2,1,0:T(8,128)}), f32[32,8,128]{2,1,0:T(8,128)S(1)}, u32[]{:S(2)}, u32[]{:S(2)}) %all-to-all-start) | async-done | bytes 131104 | tf_op jit(solution)/shard_map/all_to_all | solution.py:800
  19.4 1.8 %shard_map.140 = (f32[3264,128]{1,0:T(8,128)S(1)}, f32[272,128]{1,0:T(8,128)S(1)}, f32[272,128]{1,0:T(8,128)S(1)}) custom-call(f32[4,8,8,128]{3,2,1,0:T(8,128)S(1)} %bitcast.18), custom_call_target="tpu_custom_call" | custom-call | tf_op jit(solution)/shard_map/pallas_call | solution.py:20
  21.2 0.0 collective-permute-done.even_x
  21.2 0.0 collective-permute-done.1.odd_x
  21.2 0.1 shard_map.141
  21.3 0.7 %collective-permute-start.5 = (f32[320,128]{1,0:T(8,128)S(1)}, f32[320,128]{1,0:T(8,128)S(1)}, u32[]{:S(2)}, u32[]{:S(2)}) collective-permute-start(f32[320,128]{1,0:T(8,128)S(1)} %get-tuple-element.38), channel_id=1, source_target_pairs={{1,2},{2,1},{3,4},{4,3},{5,6},{6,5},{9,10},{10,9},{11,12},{12,11},... | collective-permute-start | bytes 491528 | tf_op jit(solution)/shard_map/ppermute | solution.py:730
  21.9 3.8 %collective-permute-start.4 = (f32[320,128]{1,0:T(8,128)S(1)}, f32[320,128]{1,0:T(8,128)S(1)}, u32[]{:S(2)}, u32[]{:S(2)}) collective-permute-start(f32[320,128]{1,0:T(8,128)S(1)} %get-tuple-element.31.after), channel_id=1, source_target_pairs={{0,1},{1,0},{2,3},{3,2},{4,5},{5,4},{6,7},{7,6},{8,9},{9,8},{10,11... | collective-permute-start | bytes 491528 | tf_op jit(solution)/shard_map/ppermute | solution.py:730
  25.7 0.0 collective-permute-done.2.even_y
  25.8 0.0 collective-permute-done.3.odd_y
  25.8 0.0 copy-done.1
  25.8 0.0 copy-done
  25.8 2.3 %shard_map.142 = (f32[3264,128]{1,0:T(8,128)S(1)}, f32[3264,128]{1,0:T(8,128)S(1)}, f32[288,128]{1,0:T(8,128)S(1)}) custom-call(f32[320,128]{1,0:T(8,128)S(1)} %get-tuple-element.31.after, f32[2048,128]{1,0:T(8,128)S(1)} %bitcast.15, f32[2048,128]{1,0:T(8,128)S(1)} %bitcast.17, f32[104,128]{1,0:T(8,128)S(1)} %collective-permute-done.even_x, ...), custom_call_target="tpu_custom_call" | custom-call | tf_op jit(solution)/shard_map/pallas_call | solution.py:20
  28.0 0.0 collective-permute-done.5.odd_s
  28.1 0.0 collective-permute-done.4.even_s
  28.1 0.0 copy-start.2
  28.1 0.0 copy-start.3
  28.1 0.0 copy-start.4
  28.1 0.0 copy-start.6
  28.1 0.0 copy-start.7
  28.1 0.0 copy-start.5
  28.1 0.0 copy-start.8
  28.1 6.1 %shard_map.143 = (f32[128,16,128]{2,1,0:T(8,128)}, f32[128,128]{1,0:T(8,128)}) custom-call(f32[4,8,8,128]{3,2,1,0:T(8,128)S(1)} %bitcast.19, f32[3264,128]{1,0:T(8,128)S(1)} %get-tuple-element.34.opened, f32[3264,128]{1,0:T(8,128)S(1)} %get-tuple-element.35.kappa_in, f32[288,128]{1,0:T(8,128)S(1)} %get-tuple-element.36.ends_in, ...), custom_call_target="tpu_custom_call" | custom-call | tf_op jit(solution)/shard_map/pallas_call | solution.py:20
  34.3 6.3 %all-to-all-start.1 = ((f32[32,4,128]{2,1,0:T(4,128)}), f32[32,4,128]{2,1,0:T(4,128)S(1)}, u32[]{:S(2)}, u32[]{:S(2)}) async-start(f32[32,4,128]{2,1,0:T(4,128)} %bitcast.8), calls=%async_computation.1 | async-start | bytes 131072 | tf_op jit(solution)/shard_map/all_to_all | solution.py:800
  40.6 0.0 copy-done.2
  40.6 0.0 copy-done.3
  40.6 0.0 copy-done.4
  40.6 0.0 copy-done.6
  40.6 0.0 copy-done.7
  40.6 3.0 %shard_map.144 = (f32[64,128]{1,0:T(8,128)S(1)}, f32[64,128]{1,0:T(8,128)S(1)}, f32[3,64,128]{2,1,0:T(8,128)S(1)}, bf16[128,8192]{1,0:T(8,128)(2,1)S(1)}, s32[2,2,128]{2,1,0:T(2,128)S(1)}) custom-call(f32[128,128]{1,0:T(8,128)} %get-tuple-element.40.after, f32[3,2048]{1,0:T(4,128)S(1)} %copy-done.2, s32[64,128]{1,0:T(8,128)S(1)} %bitcast.21, ...), custom_call_target="tpu_custom_call" | custom-call | tf_op jit(solution)/shard_map/pallas_call | solution.py:20
  43.6 4.4 %all-to-all-done.1 = f32[32,4,128]{2,1,0:T(4,128)S(1)} async-done(((f32[32,4,128]{2,1,0:T(4,128)}), f32[32,4,128]{2,1,0:T(4,128)S(1)}, u32[]{:S(2)}, u32[]{:S(2)}) %all-to-all-start.1) | async-done | bytes 65568 | tf_op jit(solution)/shard_map/all_to_all | solution.py:800
  48.0 0.0 copy-done.5
  48.0 0.0 copy-done.8
  48.0 2.1 %shard_map.145 = (f32[3,2048]{1,0:T(4,128)}, f32[3,2048]{1,0:T(4,128)}) custom-call(f32[128,128]{1,0:T(8,128)S(1)} %bitcast.20, s32[2,8,128]{2,1,0:T(8,128)S(1)} %copy-done.8, f32[3,2048]{1,0:T(4,128)S(1)} %copy-done.2, f32[3,2048]{1,0:T(4,128)S(1)} %copy-done.5, s32[64,128]{1,0:T(8,128)S(1)} %bitcast.22, s32[64,128]{1,0:T(8,128)S(1)} %bitcast.24, ...), custom_call_target="tpu_custom_call" | custom-call | tf_op jit(solution)/shard_map/pallas_call | solution.py:20
Async XLA Ops:
  0.6 25.1 %copy-start.1 = (f32[128,16,128]{2,1,0:T(8,128)S(1)}, f32[128,16,128]{2,1,0:T(8,128)}, u32[]{:S(2)}) copy-start(f32[128,16,128]{2,1,0:T(8,128)} %param.13) | copy-start | bytes 3145732
  0.6 25.1 %copy-start = (f32[128,16,128]{2,1,0:T(8,128)S(1)}, f32[128,16,128]{2,1,0:T(8,128)}, u32[]{:S(2)}) copy-start(f32[128,16,128]{2,1,0:T(8,128)} %param.12) | copy-start | bytes 3145732
  3.8 15.6 %all-to-all-start = ((f32[32,8,128]{2,1,0:T(8,128)}), f32[32,8,128]{2,1,0:T(8,128)S(1)}, u32[]{:S(2)}, u32[]{:S(2)}) async-start(f32[32,8,128]{2,1,0:T(8,128)} %bitcast.27), calls=%async_computation | async-start | bytes 262144 | tf_op jit(solution)/shard_map/all_to_all | solution.py:800
  11.1 14.6 %collective-permute-start.2 = (f32[6,128,128]{2,1,0:T(8,128)}, f32[6,128,128]{2,1,0:T(8,128)S(1)}, u32[]{:S(2)}, u32[]{:S(2)}) collective-permute-start(f32[6,128,128]{2,1,0:T(8,128)} %get-tuple-element.32), channel_id=1, source_target_pairs={{0,1},{1,0},{2,3},{3,2},{4,5},{5,4},{6,7},{7,6},{8,9},{9,8},{10,11... | collective-permute-start | bytes 1179656 | tf_op jit(solution)/shard_map/ppermute | solution.py:730
  11.5 14.3 %collective-permute-start.3 = (f32[6,128,128]{2,1,0:T(8,128)}, f32[6,128,128]{2,1,0:T(8,128)S(1)}, u32[]{:S(2)}, u32[]{:S(2)}) collective-permute-start(f32[6,128,128]{2,1,0:T(8,128)} %get-tuple-element.33), channel_id=1, source_target_pairs={{1,2},{2,1},{3,4},{4,3},{5,6},{6,5},{9,10},{10,9},{11,12},{12,11},... | collective-permute-start | bytes 1179656 | tf_op jit(solution)/shard_map/ppermute | solution.py:730
  12.1 9.0 %collective-permute-start = (f32[104,128]{1,0:T(8,128)}, f32[104,128]{1,0:T(8,128)S(1)}, u32[]{:S(2)}, u32[]{:S(2)}) collective-permute-start(f32[104,128]{1,0:T(8,128)} %get-tuple-element.29), channel_id=1, source_target_pairs={{0,8},{8,0},{16,24},{24,16},{1,9},{9,1},{17,25},{25,17},{2,10},{10... | collective-permute-start | bytes 159752 | tf_op jit(solution)/shard_map/ppermute | solution.py:730
  13.9 7.3 %collective-permute-start.1 = (f32[104,128]{1,0:T(8,128)}, f32[104,128]{1,0:T(8,128)S(1)}, u32[]{:S(2)}, u32[]{:S(2)}) collective-permute-start(f32[104,128]{1,0:T(8,128)} %get-tuple-element.30), channel_id=1, source_target_pairs={{8,16},{16,8},{24,0},{0,24},{9,17},{17,9},{25,1},{1,25},{10,18},{1... | collective-permute-start | bytes 159752 | tf_op jit(solution)/shard_map/ppermute | solution.py:730
  21.3 6.8 %collective-permute-start.5 = (f32[320,128]{1,0:T(8,128)S(1)}, f32[320,128]{1,0:T(8,128)S(1)}, u32[]{:S(2)}, u32[]{:S(2)}) collective-permute-start(f32[320,128]{1,0:T(8,128)S(1)} %get-tuple-element.38), channel_id=1, source_target_pairs={{1,2},{2,1},{3,4},{4,3},{5,6},{6,5},{9,10},{10,9},{11,12},{12,11},... | collective-permute-start | bytes 491528 | tf_op jit(solution)/shard_map/ppermute | solution.py:730
  21.9 6.1 %collective-permute-start.4 = (f32[320,128]{1,0:T(8,128)S(1)}, f32[320,128]{1,0:T(8,128)S(1)}, u32[]{:S(2)}, u32[]{:S(2)}) collective-permute-start(f32[320,128]{1,0:T(8,128)S(1)} %get-tuple-element.31.after), channel_id=1, source_target_pairs={{0,1},{1,0},{2,3},{3,2},{4,5},{5,4},{6,7},{7,6},{8,9},{9,8},{10,11... | collective-permute-start | bytes 491528 | tf_op jit(solution)/shard_map/ppermute | solution.py:730
  28.1 12.5 %copy-start.2 = (f32[3,2048]{1,0:T(4,128)S(1)}, f32[3,2048]{1,0:T(4,128)}, u32[]{:S(2)}) copy-start(f32[3,2048]{1,0:T(4,128)} %pos.5) | copy-start | bytes 73732
  28.1 12.5 %copy-start.3 = (s32[8192]{0:T(1024)S(1)}, s32[8192]{0:T(1024)}, u32[]{:S(2)}) copy-start(s32[8192]{0:T(1024)} %param.19) | copy-start | bytes 98308
  28.1 12.5 %copy-start.4 = (s32[8192]{0:T(1024)S(1)}, s32[8192]{0:T(1024)}, u32[]{:S(2)}) copy-start(s32[8192]{0:T(1024)} %param.20) | copy-start | bytes 98308
  28.1 12.5 %copy-start.6 = (f32[8192]{0:T(1024)S(1)}, f32[8192]{0:T(1024)}, u32[]{:S(2)}) copy-start(f32[8192]{0:T(1024)} %param.21) | copy-start | bytes 98308
  28.1 12.5 %copy-start.7 = (s32[8192]{0:T(1024)S(1)}, s32[8192]{0:T(1024)}, u32[]{:S(2)}) copy-start(s32[8192]{0:T(1024)} %param.22) | copy-start | bytes 98308
  28.1 19.9 %copy-start.5 = (f32[3,2048]{1,0:T(4,128)S(1)}, f32[3,2048]{1,0:T(4,128)}, u32[]{:S(2)}) copy-start(f32[3,2048]{1,0:T(4,128)} %vel.1) | copy-start | bytes 73732
  28.1 19.9 %copy-start.8 = (s32[2,8,128]{2,1,0:T(8,128)S(1)}, s32[2,8,128]{2,1,0:T(8,128)}, u32[]{:S(2)}) copy-start(s32[2,8,128]{2,1,0:T(8,128)} %get-tuple-element.41.code) | copy-start | bytes 24580
  34.3 13.7 %all-to-all-start.1 = ((f32[32,4,128]{2,1,0:T(4,128)}), f32[32,4,128]{2,1,0:T(4,128)S(1)}, u32[]{:S(2)}, u32[]{:S(2)}) async-start(f32[32,4,128]{2,1,0:T(4,128)} %bitcast.8), calls=%async_computation.1 | async-start | bytes 131072 | tf_op jit(solution)/shard_map/all_to_all | solution.py:800

commit v9 on v8

--- a/solution.py
+++ b/solution.py
@@ -799,10 +799,10 @@
         sent = sent.reshape(devices, -1, LANES)
         return lax.all_to_all(sent, BOTH, split_axis=0, concat_axis=0, tiled=True)
 
+    even_y, odd_y = swaps("cross", False, even_y, odd_y)
     got = exchange(sent).reshape(blocks, groups, 4 * half, LANES)
     even_x, odd_x = swaps("cut", True, even_x, odd_x)
 
-    even_y, odd_y = swaps("cross", False, even_y, odd_y)
 
     strips = jax.ShapeDtypeStruct(((RIM - 1) * (-(-total // 8) * 8), lanes), F32)
     entries = 2 * count + 4 * count // QUARTERS

time: 50.4 us -> 50.4 us (level)
  no operation moved by 1% of the time
where the time goes in v9:
time: 50.4 us; the launch traced here: 50.1 us
  starting transfers between devices  23.2 us (46%)
  Pallas kernels  18.5 us (37%)
  waiting for transfers between devices  7.55 us (15%)
  between operations  0.86 us (2%)
    pallas_call x7, Pallas kernels, call(): pl.pallas_call(kernel, out_shape=outs, in_specs=[pl.BlockSpec(memory_spac...  18.5 us
    all_to_all x2, starting transfers between devices, exchange(): return lax.all_to_all(sent, BOTH, split_axis=0, concat_axis=0, tiled=True)  13.6 us
    ppermute x6, starting transfers between devices, swaps(): results.append(lax.ppermute(block, axis, pairs))  9.57 us
    all_to_all x2, waiting for transfers between devices, exchange(): return lax.all_to_all(sent, BOTH, split_axis=0, concat_axis=0, tiled=True)  7.53 us
  transfers between devices with their start and end apart: 8, of which 2 were waited for; matrix products, arithmetic and copies ran while one was open for 0% of the time, Pallas kernels for 14%

profile of v9, /device:TPU:0, one launch (start us, length us, event | category | flops | bytes accessed | tf_op | source)
XLA Modules:
  0.0 50.1 jit_solution(11754999015029063380)
XLA Ops:
  0.6 0.0 copy-start.1
  0.6 0.0 copy-start
  0.7 3.2 %shard_map.139 = (f32[256,128]{1,0:T(8,128)}, f32[104,128]{1,0:T(8,128)}, f32[104,128]{1,0:T(8,128)}, f32[6,128,128]{2,1,0:T(8,128)}, f32[6,128,128]{2,1,0:T(8,128)}, /*index=5*/s32[2,8,128]{2,1,0:T(8,128)}) custom-call(f32[2048,128]{1,0:T(8,128)} %bitcast.14, f32[2048,128]{1,0:T(8,128)} %bitcast.16, s32[16,128]{1,0:T(8,128)} %bitcast.28, ...), custom_call_target="tpu_custom_call" | custom-call | tf_op jit(solution)/shard_map/pallas_call | solution.py:20
  3.8 7.3 %all-to-all-start = ((f32[32,8,128]{2,1,0:T(8,128)}), f32[32,8,128]{2,1,0:T(8,128)S(1)}, u32[]{:S(2)}, u32[]{:S(2)}) async-start(f32[32,8,128]{2,1,0:T(8,128)} %bitcast.27), calls=%async_computation | async-start | bytes 262144 | tf_op jit(solution)/shard_map/all_to_all | solution.py:800
  11.1 0.3 collective-permute-start.2
  11.5 0.7 %collective-permute-start.3 = (f32[6,128,128]{2,1,0:T(8,128)}, f32[6,128,128]{2,1,0:T(8,128)S(1)}, u32[]{:S(2)}, u32[]{:S(2)}) collective-permute-start(f32[6,128,128]{2,1,0:T(8,128)} %get-tuple-element.33), channel_id=1, source_target_pairs={{1,2},{2,1},{3,4},{4,3},{5,6},{6,5},{9,10},{10,9},{11,12},{12,11},... | collective-permute-start | bytes 1179656 | tf_op jit(solution)/shard_map/ppermute | solution.py:730
  12.1 1.7 %collective-permute-start = (f32[104,128]{1,0:T(8,128)}, f32[104,128]{1,0:T(8,128)S(1)}, u32[]{:S(2)}, u32[]{:S(2)}) collective-permute-start(f32[104,128]{1,0:T(8,128)} %get-tuple-element.29), channel_id=1, source_target_pairs={{0,8},{8,0},{16,24},{24,16},{1,9},{9,1},{17,25},{25,17},{2,10},{10... | collective-permute-start | bytes 159752 | tf_op jit(solution)/shard_map/ppermute | solution.py:730
  13.9 2.4 %collective-permute-start.1 = (f32[104,128]{1,0:T(8,128)}, f32[104,128]{1,0:T(8,128)S(1)}, u32[]{:S(2)}, u32[]{:S(2)}) collective-permute-start(f32[104,128]{1,0:T(8,128)} %get-tuple-element.30), channel_id=1, source_target_pairs={{8,16},{16,8},{24,0},{0,24},{9,17},{17,9},{25,1},{1,25},{10,18},{1... | collective-permute-start | bytes 159752 | tf_op jit(solution)/shard_map/ppermute | solution.py:730
  16.2 3.2 %all-to-all-done = f32[32,8,128]{2,1,0:T(8,128)S(1)} async-done(((f32[32,8,128]{2,1,0:T(8,128)}), f32[32,8,128]{2,1,0:T(8,128)S(1)}, u32[]{:S(2)}, u32[]{:S(2)}) %all-to-all-start) | async-done | bytes 131104 | tf_op jit(solution)/shard_map/all_to_all | solution.py:800
  19.4 1.8 %shard_map.140 = (f32[3264,128]{1,0:T(8,128)S(1)}, f32[272,128]{1,0:T(8,128)S(1)}, f32[272,128]{1,0:T(8,128)S(1)}) custom-call(f32[4,8,8,128]{3,2,1,0:T(8,128)S(1)} %bitcast.18), custom_call_target="tpu_custom_call" | custom-call | tf_op jit(solution)/shard_map/pallas_call | solution.py:20
  21.2 0.0 collective-permute-done.even_x
  21.2 0.0 collective-permute-done.1.odd_x
  21.2 0.1 shard_map.141
  21.3 0.7 %collective-permute-start.5 = (f32[320,128]{1,0:T(8,128)S(1)}, f32[320,128]{1,0:T(8,128)S(1)}, u32[]{:S(2)}, u32[]{:S(2)}) collective-permute-start(f32[320,128]{1,0:T(8,128)S(1)} %get-tuple-element.38), channel_id=1, source_target_pairs={{1,2},{2,1},{3,4},{4,3},{5,6},{6,5},{9,10},{10,9},{11,12},{12,11},... | collective-permute-start | bytes 491528 | tf_op jit(solution)/shard_map/ppermute | solution.py:730
  21.9 3.8 %collective-permute-start.4 = (f32[320,128]{1,0:T(8,128)S(1)}, f32[320,128]{1,0:T(8,128)S(1)}, u32[]{:S(2)}, u32[]{:S(2)}) collective-permute-start(f32[320,128]{1,0:T(8,128)S(1)} %get-tuple-element.31.after), channel_id=1, source_target_pairs={{0,1},{1,0},{2,3},{3,2},{4,5},{5,4},{6,7},{7,6},{8,9},{9,8},{10,11... | collective-permute-start | bytes 491528 | tf_op jit(solution)/shard_map/ppermute | solution.py:730
  25.7 0.0 collective-permute-done.2.even_y
  25.8 0.0 collective-permute-done.3.odd_y
  25.8 0.0 copy-done.1
  25.8 0.0 copy-done
  25.8 2.3 %shard_map.142 = (f32[3264,128]{1,0:T(8,128)S(1)}, f32[3264,128]{1,0:T(8,128)S(1)}, f32[288,128]{1,0:T(8,128)S(1)}) custom-call(f32[320,128]{1,0:T(8,128)S(1)} %get-tuple-element.31.after, f32[2048,128]{1,0:T(8,128)S(1)} %bitcast.15, f32[2048,128]{1,0:T(8,128)S(1)} %bitcast.17, f32[104,128]{1,0:T(8,128)S(1)} %collective-permute-done.even_x, ...), custom_call_target="tpu_custom_call" | custom-call | tf_op jit(solution)/shard_map/pallas_call | solution.py:20
  28.0 0.0 collective-permute-done.5.odd_s
  28.1 0.0 collective-permute-done.4.even_s
  28.1 0.0 copy-start.2
  28.1 0.0 copy-start.3
  28.1 0.0 copy-start.4
  28.1 0.0 copy-start.6
  28.1 0.0 copy-start.7
  28.1 0.0 copy-start.5
  28.1 0.0 copy-start.8
  28.1 6.1 %shard_map.143 = (f32[128,16,128]{2,1,0:T(8,128)}, f32[128,128]{1,0:T(8,128)}) custom-call(f32[4,8,8,128]{3,2,1,0:T(8,128)S(1)} %bitcast.19, f32[3264,128]{1,0:T(8,128)S(1)} %get-tuple-element.34.opened, f32[3264,128]{1,0:T(8,128)S(1)} %get-tuple-element.35.kappa_in, f32[288,128]{1,0:T(8,128)S(1)} %get-tuple-element.36.ends_in, ...), custom_call_target="tpu_custom_call" | custom-call | tf_op jit(solution)/shard_map/pallas_call | solution.py:20
  34.3 6.3 %all-to-all-start.1 = ((f32[32,4,128]{2,1,0:T(4,128)}), f32[32,4,128]{2,1,0:T(4,128)S(1)}, u32[]{:S(2)}, u32[]{:S(2)}) async-start(f32[32,4,128]{2,1,0:T(4,128)} %bitcast.8), calls=%async_computation.1 | async-start | bytes 131072 | tf_op jit(solution)/shard_map/all_to_all | solution.py:800
  40.6 0.0 copy-done.2
  40.6 0.0 copy-done.3
  40.6 0.0 copy-done.4
  40.6 0.0 copy-done.6
  40.6 0.0 copy-done.7
  40.6 3.0 %shard_map.144 = (f32[64,128]{1,0:T(8,128)S(1)}, f32[64,128]{1,0:T(8,128)S(1)}, f32[3,64,128]{2,1,0:T(8,128)S(1)}, bf16[128,8192]{1,0:T(8,128)(2,1)S(1)}, s32[2,2,128]{2,1,0:T(2,128)S(1)}) custom-call(f32[128,128]{1,0:T(8,128)} %get-tuple-element.40.after, f32[3,2048]{1,0:T(4,128)S(1)} %copy-done.2, s32[64,128]{1,0:T(8,128)S(1)} %bitcast.21, ...), custom_call_target="tpu_custom_call" | custom-call | tf_op jit(solution)/shard_map/pallas_call | solution.py:20
  43.6 4.4 %all-to-all-done.1 = f32[32,4,128]{2,1,0:T(4,128)S(1)} async-done(((f32[32,4,128]{2,1,0:T(4,128)}), f32[32,4,128]{2,1,0:T(4,128)S(1)}, u32[]{:S(2)}, u32[]{:S(2)}) %all-to-all-start.1) | async-done | bytes 65568 | tf_op jit(solution)/shard_map/all_to_all | solution.py:800
  48.0 0.0 copy-done.5
  48.0 0.0 copy-done.8
  48.0 2.1 %shard_map.145 = (f32[3,2048]{1,0:T(4,128)}, f32[3,2048]{1,0:T(4,128)}) custom-call(f32[128,128]{1,0:T(8,128)S(1)} %bitcast.20, s32[2,8,128]{2,1,0:T(8,128)S(1)} %copy-done.8, f32[3,2048]{1,0:T(4,128)S(1)} %copy-done.2, f32[3,2048]{1,0:T(4,128)S(1)} %copy-done.5, s32[64,128]{1,0:T(8,128)S(1)} %bitcast.22, s32[64,128]{1,0:T(8,128)S(1)} %bitcast.24, ...), custom_call_target="tpu_custom_call" | custom-call | tf_op jit(solution)/shard_map/pallas_call | solution.py:20
Async XLA Ops:
  0.6 25.1 %copy-start.1 = (f32[128,16,128]{2,1,0:T(8,128)S(1)}, f32[128,16,128]{2,1,0:T(8,128)}, u32[]{:S(2)}) copy-start(f32[128,16,128]{2,1,0:T(8,128)} %param.13) | copy-start | bytes 3145732
  0.6 25.1 %copy-start = (f32[128,16,128]{2,1,0:T(8,128)S(1)}, f32[128,16,128]{2,1,0:T(8,128)}, u32[]{:S(2)}) copy-start(f32[128,16,128]{2,1,0:T(8,128)} %param.12) | copy-start | bytes 3145732
  3.8 15.6 %all-to-all-start = ((f32[32,8,128]{2,1,0:T(8,128)}), f32[32,8,128]{2,1,0:T(8,128)S(1)}, u32[]{:S(2)}, u32[]{:S(2)}) async-start(f32[32,8,128]{2,1,0:T(8,128)} %bitcast.27), calls=%async_computation | async-start | bytes 262144 | tf_op jit(solution)/shard_map/all_to_all | solution.py:800
  11.1 14.6 %collective-permute-start.2 = (f32[6,128,128]{2,1,0:T(8,128)}, f32[6,128,128]{2,1,0:T(8,128)S(1)}, u32[]{:S(2)}, u32[]{:S(2)}) collective-permute-start(f32[6,128,128]{2,1,0:T(8,128)} %get-tuple-element.32), channel_id=1, source_target_pairs={{0,1},{1,0},{2,3},{3,2},{4,5},{5,4},{6,7},{7,6},{8,9},{9,8},{10,11... | collective-permute-start | bytes 1179656 | tf_op jit(solution)/shard_map/ppermute | solution.py:730
  11.5 14.3 %collective-permute-start.3 = (f32[6,128,128]{2,1,0:T(8,128)}, f32[6,128,128]{2,1,0:T(8,128)S(1)}, u32[]{:S(2)}, u32[]{:S(2)}) collective-permute-start(f32[6,128,128]{2,1,0:T(8,128)} %get-tuple-element.33), channel_id=1, source_target_pairs={{1,2},{2,1},{3,4},{4,3},{5,6},{6,5},{9,10},{10,9},{11,12},{12,11},... | collective-permute-start | bytes 1179656 | tf_op jit(solution)/shard_map/ppermute | solution.py:730
  12.1 9.0 %collective-permute-start = (f32[104,128]{1,0:T(8,128)}, f32[104,128]{1,0:T(8,128)S(1)}, u32[]{:S(2)}, u32[]{:S(2)}) collective-permute-start(f32[104,128]{1,0:T(8,128)} %get-tuple-element.29), channel_id=1, source_target_pairs={{0,8},{8,0},{16,24},{24,16},{1,9},{9,1},{17,25},{25,17},{2,10},{10... | collective-permute-start | bytes 159752 | tf_op jit(solution)/shard_map/ppermute | solution.py:730
  13.9 7.3 %collective-permute-start.1 = (f32[104,128]{1,0:T(8,128)}, f32[104,128]{1,0:T(8,128)S(1)}, u32[]{:S(2)}, u32[]{:S(2)}) collective-permute-start(f32[104,128]{1,0:T(8,128)} %get-tuple-element.30), channel_id=1, source_target_pairs={{8,16},{16,8},{24,0},{0,24},{9,17},{17,9},{25,1},{1,25},{10,18},{1... | collective-permute-start | bytes 159752 | tf_op jit(solution)/shard_map/ppermute | solution.py:730
  21.3 6.8 %collective-permute-start.5 = (f32[320,128]{1,0:T(8,128)S(1)}, f32[320,128]{1,0:T(8,128)S(1)}, u32[]{:S(2)}, u32[]{:S(2)}) collective-permute-start(f32[320,128]{1,0:T(8,128)S(1)} %get-tuple-element.38), channel_id=1, source_target_pairs={{1,2},{2,1},{3,4},{4,3},{5,6},{6,5},{9,10},{10,9},{11,12},{12,11},... | collective-permute-start | bytes 491528 | tf_op jit(solution)/shard_map/ppermute | solution.py:730
  21.9 6.1 %collective-permute-start.4 = (f32[320,128]{1,0:T(8,128)S(1)}, f32[320,128]{1,0:T(8,128)S(1)}, u32[]{:S(2)}, u32[]{:S(2)}) collective-permute-start(f32[320,128]{1,0:T(8,128)S(1)} %get-tuple-element.31.after), channel_id=1, source_target_pairs={{0,1},{1,0},{2,3},{3,2},{4,5},{5,4},{6,7},{7,6},{8,9},{9,8},{10,11... | collective-permute-start | bytes 491528 | tf_op jit(solution)/shard_map/ppermute | solution.py:730
  28.1 12.5 %copy-start.2 = (f32[3,2048]{1,0:T(4,128)S(1)}, f32[3,2048]{1,0:T(4,128)}, u32[]{:S(2)}) copy-start(f32[3,2048]{1,0:T(4,128)} %pos.5) | copy-start | bytes 73732
  28.1 12.5 %copy-start.3 = (s32[8192]{0:T(1024)S(1)}, s32[8192]{0:T(1024)}, u32[]{:S(2)}) copy-start(s32[8192]{0:T(1024)} %param.19) | copy-start | bytes 98308
  28.1 12.5 %copy-start.4 = (s32[8192]{0:T(1024)S(1)}, s32[8192]{0:T(1024)}, u32[]{:S(2)}) copy-start(s32[8192]{0:T(1024)} %param.20) | copy-start | bytes 98308
  28.1 12.5 %copy-start.6 = (f32[8192]{0:T(1024)S(1)}, f32[8192]{0:T(1024)}, u32[]{:S(2)}) copy-start(f32[8192]{0:T(1024)} %param.21) | copy-start | bytes 98308
  28.1 12.5 %copy-start.7 = (s32[8192]{0:T(1024)S(1)}, s32[8192]{0:T(1024)}, u32[]{:S(2)}) copy-start(s32[8192]{0:T(1024)} %param.22) | copy-start | bytes 98308
  28.1 19.9 %copy-start.5 = (f32[3,2048]{1,0:T(4,128)S(1)}, f32[3,2048]{1,0:T(4,128)}, u32[]{:S(2)}) copy-start(f32[3,2048]{1,0:T(4,128)} %vel.1) | copy-start | bytes 73732
  28.1 19.9 %copy-start.8 = (s32[2,8,128]{2,1,0:T(8,128)S(1)}, s32[2,8,128]{2,1,0:T(8,128)}, u32[]{:S(2)}) copy-start(s32[2,8,128]{2,1,0:T(8,128)} %get-tuple-element.41.code) | copy-start | bytes 24580
  34.3 13.7 %all-to-all-start.1 = ((f32[32,4,128]{2,1,0:T(4,128)}), f32[32,4,128]{2,1,0:T(4,128)S(1)}, u32[]{:S(2)}, u32[]{:S(2)}) async-start(f32[32,4,128]{2,1,0:T(4,128)} %bitcast.8), calls=%async_computation.1 | async-start | bytes 131072 | tf_op jit(solution)/shard_map/all_to_all | solution.py:800
